TPU v7x, 128 devices: a whole 4x4x4 slice. The times are simulated.
128 devices in a mesh: dom: 16 (over y, x_lo, core), st: 8 (over z, x_hi).
Axes of the slice: x: 4 (x_hi: 2, x_lo: 2; x = x_hi * 2 + x_lo), y: 4, z: 4, core: 2. Of those that a mesh axis runs over, the one named last changes fastest.
Arguments:
- states: bfloat16 [128, 64, 64, 128], P('st', 'dom'), may hold values from -6 to 6
- potential: float32 [64, 64, 128], P('dom'), may hold values from -2 to 0
- proj_values: float32 [64, 16, 16, 512], P('dom'), may hold values from -0.25 to 0.25
- block_list: int32 [64, 16, 16], P('dom'), may hold values from 0 to 12287, as said below
- tile_count: int32 [64, 16], P('dom'), may hold values from 1 to 16, as said below
- strength: float32 [12288], replicated, may hold values from 0.25 to 2
Outputs:
- rotated: bfloat16 [128, 64, 64, 128], P('st', 'dom')
Inputs may be any that keep to these rules, and one draw needn't show every extreme that they name: `block_list`: entry (z, j, k) names projector 8 * a + r of atom a; atom a's home plane a // 24 lies within 4 planes of z, counted periodically over 64 planes. Slots 0 to tile_count - 1 of a tile are used, the others ignored; some tile uses all 16.
All inputs are finite; a program needn't handle non-finite values.
Results may differ from a plain program's by a relative error of at most 0.0056.
Values may be sent and summed in bfloat16 or wider, within the bound.
No kernel may reach another device: no remote copies, remote signals or barrier semaphores. Data moves between devices by JAX's collectives and lax.ppermute only.
A program may use at most 128 MiB of HBM per device.

v0:
```python
import jax
import jax.numpy as jnp
from jax import lax
from jax.sharding import PartitionSpec as P

center = 8.25
half_width = 7.75


def passed_along(array, axis, by):
    devices = lax.axis_size(axis)
    return lax.ppermute(array, axis, [(i, (i + by) % devices) for i in range(devices)])


def extended(cells, sides, width):
    for axis, dim in sides:
        count = lax.axis_size(axis)
        head = lax.slice_in_dim(cells, 0, width, axis=dim)
        tail = lax.slice_in_dim(cells, cells.shape[dim] - width, cells.shape[dim], axis=dim)
        cells = jnp.concatenate(
            [
                lax.ppermute(tail, axis, [(i, (i + 1) % count) for i in range(count)]),
                cells,
                lax.ppermute(head, axis, [((i + 1) % count, i) for i in range(count)]),
            ],
            axis=dim,
        )
    return cells


def second_difference(minus_two, minus_one, middle, plus_one, plus_two):
    return (16.0 * (minus_one + plus_one) - (minus_two + plus_two) - 30.0 * middle) / 12.0


def along_axis(field, axis):
    return second_difference(
        jnp.roll(field, 2, axis),
        jnp.roll(field, 1, axis),
        field,
        jnp.roll(field, -1, axis),
        jnp.roll(field, -2, axis),
    )


def per_device(states, potential, proj_values, block_list, tile_count, strength):
    local_states, planes_dev, rows_y, cells_x = states.shape
    slots = block_list.shape[-1]
    tile_cells = proj_values.shape[-1]
    domains = lax.axis_size("dom")
    total_cells = planes_dev * rows_y * cells_x * domains
    nproj = strength.shape[0]
    slot_ids = block_list.reshape(-1, slots)
    used = (jnp.arange(slots)[None, :] < tile_count.reshape(-1)[:, None]).astype(jnp.float32)
    proj_masked = proj_values.reshape(-1, slots, tile_cells) * used[..., None]
    slot_strength = strength[slot_ids]
    slab_rows = nproj // domains
    base_row = (lax.axis_index("dom") - 1) * slab_rows
    window_ids = jnp.mod(slot_ids - base_row, nproj)

    def coefficients(partial_value):
        flat_terms = partial_value.reshape(-1, local_states)
        window = (
            jnp.zeros((3 * slab_rows, local_states), jnp.float32)
            .at[window_ids.reshape(-1)]
            .add(flat_terms)
        )
        from_next = passed_along(window[:slab_rows].astype(jnp.bfloat16), "dom", -1).astype(
            jnp.float32
        )
        from_prior = passed_along(window[2 * slab_rows :].astype(jnp.bfloat16), "dom", 1).astype(
            jnp.float32
        )
        own_total = window[slab_rows : 2 * slab_rows] + from_next + from_prior
        totals = extended(own_total.astype(jnp.bfloat16), (("dom", 0),), slab_rows).astype(
            own_total.dtype
        )
        return totals[window_ids]

    def hamiltonian(field):
        padded = extended(field, (("dom", 1),), 2)
        along_z = second_difference(
            padded[:, 0:planes_dev],
            padded[:, 1 : planes_dev + 1],
            field,
            padded[:, 3 : planes_dev + 3],
            padded[:, 4 : planes_dev + 4],
        )
        kinetic = along_z + along_axis(field, 2) + along_axis(field, 3)
        tiles = field.reshape(local_states, -1, tile_cells)
        partial_value = jnp.einsum(
            "tkc,stc->tks", proj_masked, tiles, precision=lax.Precision.HIGHEST
        )
        chosen = coefficients(partial_value) * slot_strength[..., None]
        applied = jnp.einsum("tkc,tks->stc", proj_masked, chosen, precision=lax.Precision.HIGHEST)
        return -0.5 * kinetic + potential[None] * field + applied.reshape(field.shape)

    previous = states.astype(jnp.float32)
    current = (hamiltonian(previous) - center * previous) / half_width
    for degree in range(3):
        following = 2.0 * (hamiltonian(current) - center * current) / half_width - previous
        previous, current = (current, following)
    filtered = current.astype(jnp.bfloat16).reshape(local_states, -1)
    everything = lax.all_gather(filtered, "st", axis=0, tiled=True)
    part_rows = jnp.einsum("ic,jc->ij", filtered, everything, preferred_element_type=jnp.float32)
    summed = lax.psum(part_rows, "dom")
    margin = lax.all_gather(summed, "st", axis=0, tiled=True) / total_cells
    factor = jnp.linalg.cholesky(margin)
    inverse = jax.scipy.linalg.solve_triangular(
        factor, jnp.eye(margin.shape[0], dtype=jnp.float32), lower=True
    )
    inverse_b = inverse.astype(jnp.bfloat16)
    mine = lax.dynamic_slice_in_dim(inverse_b, lax.axis_index("st") * local_states, local_states, 0)
    rotated = jnp.dot(mine, everything, preferred_element_type=jnp.float32).astype(jnp.bfloat16)
    return rotated.reshape(states.shape)


def solution(mesh):
    return jax.shard_map(
        per_device,
        mesh=mesh,
        in_specs=(
            P("st", "dom", None, None),
            P("dom", None, None),
            P("dom", None, None, None),
            P("dom", None, None),
            P("dom", None),
            P(),
        ),
        out_specs=P("st", "dom", None, None),
        check_vma=False,
    )
```

profile of v0, /device:TPU:0, one launch (start us, length us, event | category | flops | bytes accessed | tf_op | source)
XLA Modules:
  0.0 608.3 jit_solution(10301754788710822766)
XLA Ops:
  14.4 7.6 %scatter_custom_fusion = f32[2304,16]{1,0:T(8,128)} fusion(s32[1024]{0:T(1024)S(1)} %bitcast.78, f32[1024,16]{1,0:T(8,128)} %bitcast.75, f32[]{:T(128)} %constant.101.clone.1), kind=kCustom, calls=%fused_computation.155 | custom fusion | flops 16384 | bytes 147968 | tf_op jit(solution)/shard_map/scatter-add | solution.py:65
  57.4 6.1 %gather_fusion.1 = f32[1024]{0:T(1024)S(1)} fusion(f32[12288]{0:T(1024)S(1)} %copy-done, s32[1024]{0:T(1024)S(1)} %broadcast_clamp_fusion), kind=kCustom, calls=%fused_computation.1 | custom fusion | bytes 12288 | tf_op jit(solution)/shard_map/gather | solution.py:55
  68.5 5.3 gather_fusion
  81.4 15.3 %broadcast_multiply_fusion = (f32[16,4,64,128]{3,2,1,0:T(8,128)S(1)}, f32[16,4,64,128]{3,2,1,0:T(8,128)}) fusion(f32[16,4,64,128]{3,2,1,0:T(8,128)} %convert_element_type.76, f32[16,4,64,128]{3,2,1,0:T(8,128)} %reshape.200, f32[4,64,128]{2,1,0:T(8,128)S(1)} %copy-done.13, f32[16,4,64,2]{3,2,1,0:T(8,128)} %get-tuple-element.76, ...), kind=kLoop, calls=%fused_computation.148 | loop fusion | flops 19398656 | bytes 27394048 | tf_op jit(solution)/shard_map/div | solution.py:98
  116.4 4.7 fusion.83
  121.1 7.5 %scatter_custom_fusion.1 = f32[2304,16]{1,0:T(8,128)} fusion(s32[1024]{0:T(1024)S(1)} %bitcast.79, f32[1024,16]{1,0:T(8,128)} %bitcast.76, f32[]{:T(128)} %constant.101.clone.1), kind=kCustom, calls=%fused_computation.153 | custom fusion | flops 16384 | bytes 147968 | tf_op jit(solution)/shard_map/scatter-add | solution.py:65
  144.4 19.3 %collective-permute-done.11 = bf16[768,16]{1,0:T(8,128)(2,1)} collective-permute-done((bf16[768,16]{1,0:T(8,128)(2,1)S(1)}, bf16[768,16]{1,0:T(8,128)(2,1)}, u32[]{:S(2)}, u32[]{:S(2)}) %collective-permute-start.11) | collective-permute-done | bytes 24608 | tf_op jit(solution)/shard_map/ppermute | solution.py:24
  168.5 5.8 gather_fusion.2
  181.9 14.4 %fusion.40 = f32[16,4,64,128]{3,2,1,0:T(8,128)S(1)} fusion(f32[16,4,64,128]{3,2,1,0:T(8,128)} %reshape.203, f32[16,4,64,128]{3,2,1,0:T(8,128)} %copy-done.4, f32[16,2,64,128]{3,2,1,0:T(8,128)} %collective-permute-done.7, f32[16,2,64,128]{3,2,1,0:T(8,128)} %collective-permute-done.6, f32[16,4,63,128]{3,2,1,0:T(8,128)} %get-tuple-element.56, ...), kind=kLoop, calls=%fused_computation.66 | loop fusion | flops 20447232 | bytes 28442624 | tf_op jit(solution)/shard_map/sub | solution.py:100
  219.7 7.1 %scatter_custom_fusion.2 = f32[2304,16]{1,0:T(8,128)} fusion(s32[1024]{0:T(1024)S(1)} %bitcast.80, f32[1024,16]{1,0:T(8,128)S(1)} %bitcast.77, f32[]{:T(128)} %constant.101.clone.1), kind=kCustom, calls=%fused_computation.151 | custom fusion | flops 16384 | bytes 147460 | tf_op jit(solution)/shard_map/scatter-add | solution.py:65
  232.7 4.8 collective-permute-done.15
  242.5 19.4 %collective-permute-done.17 = bf16[768,16]{1,0:T(8,128)(2,1)S(1)} collective-permute-done((bf16[768,16]{1,0:T(8,128)(2,1)S(1)}, bf16[768,16]{1,0:T(8,128)(2,1)S(1)}, u32[]{:S(2)}, u32[]{:S(2)}) %collective-permute-start.17) | collective-permute-done | bytes 24608 | tf_op jit(solution)/shard_map/ppermute | solution.py:24
  278.6 14.0 %fusion.26 = f32[16,4,64,128]{3,2,1,0:T(8,128)} fusion(f32[16,4,64,128]{3,2,1,0:T(8,128)} %reshape.206, f32[16,4,64,128]{3,2,1,0:T(8,128)S(1)} %fusion.40, f32[16,2,64,128]{3,2,1,0:T(8,128)} %collective-permute-done.13, f32[16,2,64,128]{3,2,1,0:T(8,128)} %collective-permute-done.12, f32[16,4,63,128]{3,2,1,0:T(8,128)} %get-tuple-element.38, ...), kind=kLoop, calls=%fused_computation.52 | loop fusion | flops 20447232 | bytes 27394048 | tf_op jit(solution)/shard_map/sub | solution.py:100
  295.4 5.1 fusion.129
  320.4 7.1 %scatter_custom_fusion.3 = f32[2304,16]{1,0:T(8,128)} fusion(s32[1024]{0:T(1024)S(1)} %bitcast.81, f32[1024,16]{1,0:T(8,128)S(1)} %bitcast.74, f32[]{:T(128)} %constant.101.clone.1), kind=kCustom, calls=%fused_computation.149 | custom fusion | flops 16384 | bytes 147460 | tf_op jit(solution)/shard_map/scatter-add | solution.py:65
  343.2 19.4 %collective-permute-done.23 = bf16[768,16]{1,0:T(8,128)(2,1)S(1)} collective-permute-done((bf16[768,16]{1,0:T(8,128)(2,1)S(1)}, bf16[768,16]{1,0:T(8,128)(2,1)S(1)}, u32[]{:S(2)}, u32[]{:S(2)}) %collective-permute-start.23) | collective-permute-done | bytes 24608 | tf_op jit(solution)/shard_map/ppermute | solution.py:24
  378.7 14.2 %fusion.85 = bf16[16,4,64,128]{3,2,1,0:T(8,128)(2,1)S(1)} fusion(f32[16,4,64,128]{3,2,1,0:T(8,128)S(1)} %fusion.40, f32[16,4,64,128]{3,2,1,0:T(8,128)} %fusion.26, f32[16,4,64,128]{3,2,1,0:T(8,128)} %reshape.209, f32[16,4,64,2]{3,2,1,0:T(8,128)} %get-tuple-element.22, f32[16,4,64,126]{3,2,1,0:T(8,128)} %get-tuple-element.24, ...), kind=kLoop, calls=%fused_computation.139 | loop fusion | flops 20447232 | bytes 26345472 | tf_op jit(solution)/shard_map/convert_element_type | solution.py:102
  394.6 107.7 %all-gather.2.cloned.1.call-done = bf16[128,32768]{1,0:T(8,128)(2,1)} async-done(((bf16[16,32768]{1,0:T(8,128)(2,1)}), bf16[128,32768]{1,0:T(8,128)(2,1)}) %all-gather.2.cloned.1.call-update) | async-done | bytes 8388624 | tf_op jit(solution)/shard_map/all_gather | solution.py:103
  502.3 5.6 fusion.120
  508.0 29.4 %psum.7 = f32[16,128]{1,0:T(8,128)S(1)} all-reduce(f32[16,128]{1,0:T(8,128)S(1)} %fusion.120), channel_id=1, replica_groups=mesh['dom'=16,'st'=8] {'dom'}, use_global_device_ids=true, to_apply=%region_4.5 | all-reduce | flops 2048 | bytes 16384 | tf_op jit(solution)/shard_map/psum | solution.py:105
  537.4 34.5 %all_gather.7 = f32[128,128]{1,0:T(8,128)S(1)} all-gather(f32[16,128]{1,0:T(8,128)S(1)} %psum.7), channel_id=1, replica_groups=mesh['dom'=16,'st'=8] {'st'}, dimensions={0}, use_global_device_ids=true | all-gather | bytes 73728 | tf_op jit(solution)/shard_map/all_gather | solution.py:106
  572.1 11.7 %cholesky.17 = f32[128,128]{1,0:T(8,128)S(1)} custom-call(f32[128,128]{1,0:T(8,128)S(1)} %fusion.116), custom_call_target="Cholesky" | custom-call | tf_op jit(solution)/shard_map/jit(cholesky)/cholesky | solution.py:107
  585.2 9.8 %custom-call.7 = f32[1,128,128]{1,2,0:T(8,128)S(1)} custom-call(f32[1,128,128]{2,1,0:T(8,128)S(1)} %fusion.113), custom_call_target="InvertDiagBlocksLowerTriangular" | custom-call | tf_op jit(solution)/shard_map/jit(_solve_triangular)/triangular_solve | solution.py:108
  595.3 4.6 fusion.86
  (204 shorter events, 213.4 us)
Async XLA Ops:
  6.5 495.8 %all-gather.2.cloned.1.call-start = ((), (), s32[]{:S(2)}) async-start(), calls=%async_computation | async-start | bytes 9437184 | tf_op jit(solution)/shard_map/all_gather | solution.py:103
  24.0 26.3 %collective-permute-start.3 = (bf16[768,16]{1,0:T(8,128)(2,1)}, bf16[768,16]{1,0:T(8,128)(2,1)}, u32[]{:S(2)}, u32[]{:S(2)}) collective-permute-start(bf16[768,16]{1,0:T(8,128)(2,1)} %get-tuple-element.86), channel_id=1, source_target_pairs={{0,8},{8,16},{16,24},{24,32},{32,40},{40,48},{48,56},{56,64},{64,7... | collective-permute-start | bytes 73736 | tf_op jit(solution)/shard_map/ppermute | solution.py:12
  24.0 26.3 %collective-permute-start.2 = (bf16[768,16]{1,0:T(8,128)(2,1)S(1)}, bf16[768,16]{1,0:T(8,128)(2,1)}, u32[]{:S(2)}, u32[]{:S(2)}) collective-permute-start(bf16[768,16]{1,0:T(8,128)(2,1)S(1)} %get-tuple-element.85), channel_id=1, source_target_pairs={{0,120},{8,0},{16,8},{24,16},{32,24},{40,32},{48,40},{56,48},{64,5... | collective-permute-start | bytes 73736 | tf_op jit(solution)/shard_map/ppermute | solution.py:12
  29.4 51.9 %collective-permute-start.1 = (f32[16,2,64,128]{3,2,1,0:T(8,128)}, f32[16,2,64,128]{3,2,1,0:T(8,128)}, u32[]{:S(2)}, u32[]{:S(2)}) collective-permute-start(f32[16,2,64,128]{3,2,1,0:T(8,128)} %get-tuple-element.62), channel_id=1, source_target_pairs={{8,0},{16,8},{24,16},{32,24},{40,32},{48,40},{56,48},{64,56},{72,6... | collective-permute-start | bytes 3145736 | tf_op jit(solution)/shard_map/ppermute | solution.py:24
  29.7 51.6 %collective-permute-start = (f32[16,2,64,128]{3,2,1,0:T(8,128)}, f32[16,2,64,128]{3,2,1,0:T(8,128)}, u32[]{:S(2)}, u32[]{:S(2)}) collective-permute-start(f32[16,2,64,128]{3,2,1,0:T(8,128)} %get-tuple-element.61), channel_id=1, source_target_pairs={{0,8},{8,16},{16,24},{24,32},{32,40},{40,48},{48,56},{56,64},{64,7... | collective-permute-start | bytes 3145736 | tf_op jit(solution)/shard_map/ppermute | solution.py:22
  51.5 12.2 %collective-permute-start.5 = (bf16[768,16]{1,0:T(8,128)(2,1)S(1)}, bf16[768,16]{1,0:T(8,128)(2,1)}, u32[]{:S(2)}, u32[]{:S(2)}) collective-permute-start(bf16[768,16]{1,0:T(8,128)(2,1)S(1)} %fusion.108), channel_id=1, source_target_pairs={{8,0},{16,8},{24,16},{32,24},{40,32},{48,40},{56,48},{64,56},{72,6... | collective-permute-start | bytes 73736 | tf_op jit(solution)/shard_map/ppermute | solution.py:24
  55.2 10.2 %collective-permute-start.4 = (bf16[768,16]{1,0:T(8,128)(2,1)S(1)}, bf16[768,16]{1,0:T(8,128)(2,1)}, u32[]{:S(2)}, u32[]{:S(2)}) collective-permute-start(bf16[768,16]{1,0:T(8,128)(2,1)S(1)} %fusion.108), channel_id=1, source_target_pairs={{0,8},{8,16},{16,24},{24,32},{32,40},{40,48},{48,56},{56,64},{64,7... | collective-permute-start | bytes 73736 | tf_op jit(solution)/shard_map/ppermute | solution.py:22
  129.9 8.8 %collective-permute-start.9 = (bf16[768,16]{1,0:T(8,128)(2,1)S(1)}, bf16[768,16]{1,0:T(8,128)(2,1)S(1)}, u32[]{:S(2)}, u32[]{:S(2)}) collective-permute-start(bf16[768,16]{1,0:T(8,128)(2,1)S(1)} %get-tuple-element.84), channel_id=1, source_target_pairs={{0,8},{8,16},{16,24},{24,32},{32,40},{40,48},{48,56},{56,64},{64,7... | collective-permute-start | bytes 73736 | tf_op jit(solution)/shard_map/ppermute | solution.py:12
  134.6 47.3 %collective-permute-start.7 = (f32[16,2,64,128]{3,2,1,0:T(8,128)}, f32[16,2,64,128]{3,2,1,0:T(8,128)}, u32[]{:S(2)}, u32[]{:S(2)}) collective-permute-start(f32[16,2,64,128]{3,2,1,0:T(8,128)} %get-tuple-element.60), channel_id=1, source_target_pairs={{8,0},{16,8},{24,16},{32,24},{40,32},{48,40},{56,48},{64,56},{72,6... | collective-permute-start | bytes 3145736 | tf_op jit(solution)/shard_map/ppermute | solution.py:24
  135.0 46.9 %collective-permute-start.6 = (f32[16,2,64,128]{3,2,1,0:T(8,128)}, f32[16,2,64,128]{3,2,1,0:T(8,128)}, u32[]{:S(2)}, u32[]{:S(2)}) collective-permute-start(f32[16,2,64,128]{3,2,1,0:T(8,128)} %get-tuple-element.59), channel_id=1, source_target_pairs={{0,8},{8,16},{16,24},{24,32},{32,40},{40,48},{48,56},{56,64},{64,7... | collective-permute-start | bytes 3145736 | tf_op jit(solution)/shard_map/ppermute | solution.py:22
  139.7 24.0 %collective-permute-start.11 = (bf16[768,16]{1,0:T(8,128)(2,1)S(1)}, bf16[768,16]{1,0:T(8,128)(2,1)}, u32[]{:S(2)}, u32[]{:S(2)}) collective-permute-start(bf16[768,16]{1,0:T(8,128)(2,1)S(1)} %fusion.106), channel_id=1, source_target_pairs={{8,0},{16,8},{24,16},{32,24},{40,32},{48,40},{56,48},{64,56},{72,6... | collective-permute-start | bytes 73736 | tf_op jit(solution)/shard_map/ppermute | solution.py:24
  143.7 22.4 %collective-permute-start.10 = (bf16[768,16]{1,0:T(8,128)(2,1)S(1)}, bf16[768,16]{1,0:T(8,128)(2,1)}, u32[]{:S(2)}, u32[]{:S(2)}) collective-permute-start(bf16[768,16]{1,0:T(8,128)(2,1)S(1)} %fusion.106), channel_id=1, source_target_pairs={{0,8},{8,16},{16,24},{24,32},{32,40},{40,48},{48,56},{56,64},{64,7... | collective-permute-start | bytes 73736 | tf_op jit(solution)/shard_map/ppermute | solution.py:22
  228.1 9.4 %collective-permute-start.15 = (bf16[768,16]{1,0:T(8,128)(2,1)S(1)}, bf16[768,16]{1,0:T(8,128)(2,1)S(1)}, u32[]{:S(2)}, u32[]{:S(2)}) collective-permute-start(bf16[768,16]{1,0:T(8,128)(2,1)S(1)} %get-tuple-element.82), channel_id=1, source_target_pairs={{0,8},{8,16},{16,24},{24,32},{32,40},{40,48},{48,56},{56,64},{64,7... | collective-permute-start | bytes 73736 | tf_op jit(solution)/shard_map/ppermute | solution.py:12
  228.2 9.3 %collective-permute-start.14 = (bf16[768,16]{1,0:T(8,128)(2,1)S(1)}, bf16[768,16]{1,0:T(8,128)(2,1)S(1)}, u32[]{:S(2)}, u32[]{:S(2)}) collective-permute-start(bf16[768,16]{1,0:T(8,128)(2,1)S(1)} %get-tuple-element.81), channel_id=1, source_target_pairs={{0,120},{8,0},{16,8},{24,16},{32,24},{40,32},{48,40},{56,48},{64,5... | collective-permute-start | bytes 73736 | tf_op jit(solution)/shard_map/ppermute | solution.py:12
  232.1 46.5 %collective-permute-start.13 = (f32[16,2,64,128]{3,2,1,0:T(8,128)}, f32[16,2,64,128]{3,2,1,0:T(8,128)}, u32[]{:S(2)}, u32[]{:S(2)}) collective-permute-start(f32[16,2,64,128]{3,2,1,0:T(8,128)} %get-tuple-element.42), channel_id=1, source_target_pairs={{8,0},{16,8},{24,16},{32,24},{40,32},{48,40},{56,48},{64,56},{72,6... | collective-permute-start | bytes 3145736 | tf_op jit(solution)/shard_map/ppermute | solution.py:24
  232.2 46.4 %collective-permute-start.12 = (f32[16,2,64,128]{3,2,1,0:T(8,128)}, f32[16,2,64,128]{3,2,1,0:T(8,128)}, u32[]{:S(2)}, u32[]{:S(2)}) collective-permute-start(f32[16,2,64,128]{3,2,1,0:T(8,128)} %get-tuple-element.41), channel_id=1, source_target_pairs={{0,8},{8,16},{16,24},{24,32},{32,40},{40,48},{48,56},{56,64},{64,7... | collective-permute-start | bytes 3145736 | tf_op jit(solution)/shard_map/ppermute | solution.py:22
  238.6 23.3 %collective-permute-start.17 = (bf16[768,16]{1,0:T(8,128)(2,1)S(1)}, bf16[768,16]{1,0:T(8,128)(2,1)S(1)}, u32[]{:S(2)}, u32[]{:S(2)}) collective-permute-start(bf16[768,16]{1,0:T(8,128)(2,1)S(1)} %fusion.104), channel_id=1, source_target_pairs={{8,0},{16,8},{24,16},{32,24},{40,32},{48,40},{56,48},{64,56},{72,6... | collective-permute-start | bytes 73736 | tf_op jit(solution)/shard_map/ppermute | solution.py:24
  242.4 21.5 %collective-permute-start.16 = (bf16[768,16]{1,0:T(8,128)(2,1)S(1)}, bf16[768,16]{1,0:T(8,128)(2,1)S(1)}, u32[]{:S(2)}, u32[]{:S(2)}) collective-permute-start(bf16[768,16]{1,0:T(8,128)(2,1)S(1)} %fusion.104), channel_id=1, source_target_pairs={{0,8},{8,16},{16,24},{24,32},{32,40},{40,48},{48,56},{56,64},{64,7... | collective-permute-start | bytes 73736 | tf_op jit(solution)/shard_map/ppermute | solution.py:22
  328.9 9.4 %collective-permute-start.21 = (bf16[768,16]{1,0:T(8,128)(2,1)S(1)}, bf16[768,16]{1,0:T(8,128)(2,1)S(1)}, u32[]{:S(2)}, u32[]{:S(2)}) collective-permute-start(bf16[768,16]{1,0:T(8,128)(2,1)S(1)} %get-tuple-element.80), channel_id=1, source_target_pairs={{0,8},{8,16},{16,24},{24,32},{32,40},{40,48},{48,56},{56,64},{64,7... | collective-permute-start | bytes 73736 | tf_op jit(solution)/shard_map/ppermute | solution.py:12
  328.9 9.3 %collective-permute-start.20 = (bf16[768,16]{1,0:T(8,128)(2,1)S(1)}, bf16[768,16]{1,0:T(8,128)(2,1)S(1)}, u32[]{:S(2)}, u32[]{:S(2)}) collective-permute-start(bf16[768,16]{1,0:T(8,128)(2,1)S(1)} %get-tuple-element.79), channel_id=1, source_target_pairs={{0,120},{8,0},{16,8},{24,16},{32,24},{40,32},{48,40},{56,48},{64,5... | collective-permute-start | bytes 73736 | tf_op jit(solution)/shard_map/ppermute | solution.py:12
  333.9 44.8 %collective-permute-start.19 = (f32[16,2,64,128]{3,2,1,0:T(8,128)}, f32[16,2,64,128]{3,2,1,0:T(8,128)}, u32[]{:S(2)}, u32[]{:S(2)}) collective-permute-start(f32[16,2,64,128]{3,2,1,0:T(8,128)} %get-tuple-element.8), channel_id=1, source_target_pairs={{8,0},{16,8},{24,16},{32,24},{40,32},{48,40},{56,48},{64,56},{72,6... | collective-permute-start | bytes 3145736 | tf_op jit(solution)/shard_map/ppermute | solution.py:24
  334.0 44.7 %collective-permute-start.18 = (f32[16,2,64,128]{3,2,1,0:T(8,128)}, f32[16,2,64,128]{3,2,1,0:T(8,128)}, u32[]{:S(2)}, u32[]{:S(2)}) collective-permute-start(f32[16,2,64,128]{3,2,1,0:T(8,128)} %get-tuple-element.7), channel_id=1, source_target_pairs={{0,8},{8,16},{16,24},{24,32},{32,40},{40,48},{48,56},{56,64},{64,7... | collective-permute-start | bytes 3145736 | tf_op jit(solution)/shard_map/ppermute | solution.py:22
  339.3 23.4 %collective-permute-start.23 = (bf16[768,16]{1,0:T(8,128)(2,1)S(1)}, bf16[768,16]{1,0:T(8,128)(2,1)S(1)}, u32[]{:S(2)}, u32[]{:S(2)}) collective-permute-start(bf16[768,16]{1,0:T(8,128)(2,1)S(1)} %fusion.102), channel_id=1, source_target_pairs={{8,0},{16,8},{24,16},{32,24},{40,32},{48,40},{56,48},{64,56},{72,6... | collective-permute-start | bytes 73736 | tf_op jit(solution)/shard_map/ppermute | solution.py:24
  342.0 21.9 %collective-permute-start.22 = (bf16[768,16]{1,0:T(8,128)(2,1)S(1)}, bf16[768,16]{1,0:T(8,128)(2,1)S(1)}, u32[]{:S(2)}, u32[]{:S(2)}) collective-permute-start(bf16[768,16]{1,0:T(8,128)(2,1)S(1)} %fusion.102), channel_id=1, source_target_pairs={{0,8},{8,16},{16,24},{24,32},{32,40},{40,48},{48,56},{56,64},{64,7... | collective-permute-start | bytes 73736 | tf_op jit(solution)/shard_map/ppermute | solution.py:22
  (22 other events, 238.7 us)
Sparse Core Ops, SparseCore 0:
  394.7 107.5 all-gather.1
where the time goes:
time: 617 us; the launch traced here: 608 us
  waiting for transfers between devices  182 us (29%)
  local copies, waits for them, and re-layouts  151 us (24%)
  other arithmetic  126 us (20%)
  blocking collectives  63.9 us (10%)
  matrix products  38.1 us (6%)
  starting transfers between devices  32.5 us (5%)
  between operations  14.4 us (2%)
    all_gather x1, waiting for transfers between devices, per_device(): everything = lax.all_gather(filtered, 'st', axis=0, tiled=True)  108 us
    ppermute x8, waiting for transfers between devices, extended(): lax.ppermute(head, axis, [((i + 1) % count, i) for i in range(count)])  58.2 us
    all_gather x1, blocking collectives, per_device(): margin = lax.all_gather(summed, 'st', axis=0, tiled=True) / total_cells  34.5 us
    psum x1, blocking collectives, per_device(): summed = lax.psum(part_rows, 'dom')  29.4 us
    scatter-add x4, other arithmetic, coefficients(): window = jnp.zeros((3 * slab_rows, local_states), jnp.float32).at[window_...  29.2 us
    sub x2, other arithmetic, per_device(): 2.0 * (hamiltonian(current) - center * current) / half_width - previous  28.4 us
    gather x8, local copies, waits for them, and re-layouts, coefficients(): return totals[window_ids]  24 us
    slice x8, local copies, waits for them, and re-layouts, along_axis(): jnp.roll(field, 2, axis)  19.9 us
  transfers between devices with their start and end apart: 25, of which 10 were waited for; matrix products, arithmetic and copies ran while one was open for 17% of the time, Pallas kernels for 0%

commit v1 on v0

v1 whole, which is shorter than its diff:
```python
import jax
import jax.numpy as jnp
from jax import lax
from jax.experimental import pallas as pl
from jax.experimental.pallas import tpu as pltpu
from jax.sharding import PartitionSpec as P

center = 8.25
half_width = 7.75

F32 = jnp.float32
BF16 = jnp.bfloat16
NT = (((1,), (1,)), ((), ()))
NN = (((1,), (0,)), ((), ()))


def passed_along(array, axis, by):
    devices = lax.axis_size(axis)
    return lax.ppermute(array, axis, [(i, (i + by) % devices) for i in range(devices)])


def call(kernel, out_shape, scratch=(), vmem=48, flops=0, nbytes=0):
    return pl.pallas_call(
        kernel,
        out_shape=out_shape,
        scratch_shapes=list(scratch),
        compiler_params=pltpu.CompilerParams(vmem_limit_bytes=vmem * 2**20),
        cost_estimate=pl.CostEstimate(flops=int(flops), bytes_accessed=int(nbytes), transcendentals=0),
    )


def block_mask(rows, cols, row_block, col_block):
    row = lax.broadcasted_iota(jnp.int32, (rows, cols), 0) // row_block
    col = lax.broadcasted_iota(jnp.int32, (rows, cols), 1) // col_block
    return row == col


def project(field, proj, states, slots):
    both = lax.dot_general(field, proj, NT, preferred_element_type=F32)
    both = jnp.where(block_mask(*both.shape, states, slots), both, 0.0)
    return jnp.sum(both.reshape(-1, states, both.shape[1]), axis=0)


def first_kernel(states, slots, field, proj_values, used, proj, partial):
    planes, cols = field.shape[0], proj.shape[1]
    for z in range(planes):
        proj[z] = proj_values[z].astype(BF16)
        at = slice(z * cols, (z + 1) * cols)
        partial[:, at] = (project(field[z], proj[z], states, slots) * used[:, at]).astype(BF16)


def coupling_kernel(ids, table):
    sources, count = ids.shape
    for e in range(sources):
        for q in range(0, count, 128):
            column = jnp.broadcast_to(ids[e : e + 1, q : q + 128], (128, 128)).T
            same = [
                jnp.where(column == ids[0:1, p : p + 128], 1.0, 0.0).astype(BF16)
                for p in range(0, count, 128)
            ]
            for i, p in enumerate(range(0, count, 128)):
                table[e * count + q : e * count + q + 128, p : p + 128] = same[i]


def step_kernel(sizes, first, last, *refs):
    states, slots, rows = sizes
    cur, below, above, own, *others = refs[:8]
    table, weight, used, proj, shifted = refs[8:13]
    rest = list(refs[13:])
    prev = None if first else rest.pop(0)
    if last:
        (nxt, applied) = rest
    else:
        (nxt, low, high, partial, applied) = rest
    planes, height, width = cur.shape
    tiles = height // states
    cols = proj.shape[1]
    gain = (1.0 if first else 2.0) / half_width
    near, far = -gain * 2.0 / 3.0, gain / 24.0

    terms = jnp.concatenate([own[...]] + [o[...] for o in others], axis=1)
    chosen = lax.dot_general(terms, table[...], NN, preferred_element_type=F32)
    chosen = (chosen * weight[...] * gain).astype(BF16)
    mask = block_mask(height, cols, states, slots)
    for z in range(planes):
        spread = jnp.broadcast_to(chosen[:, z * cols : (z + 1) * cols][None], (tiles, states, cols))
        spread = jnp.where(mask, spread.reshape(height, cols), jnp.zeros((), BF16))
        applied[z] = lax.dot_general(spread, proj[z], NN, preferred_element_type=F32)

    def lane(y):
        return slice(y * 128, (y + 1) * 128)

    def tile_step(j, carry):
        def at(t):
            return pl.ds(pl.multiple_of(t * states, states), states)

        here, left, right = at(j), at((j + tiles - 1) % tiles), at((j + 1) % tiles)

        def load(z, y):
            if z < 0:
                return below[z + 2, here, lane(y)].astype(F32)
            if z >= planes:
                return above[z - planes, here, lane(y)].astype(F32)
            if y < 0:
                return cur[z, left, lane(y + rows)].astype(F32)
            if y >= rows:
                return cur[z, right, lane(y - rows)].astype(F32)
            return cur[z, here, lane(y)].astype(F32)

        for y in range(rows):
            for z in range(planes):
                mid = load(z, y)
                one = load(z - 1, y) + load(z + 1, y) + load(z, y - 1) + load(z, y + 1)
                two = load(z - 2, y) + load(z + 2, y) + load(z, y - 2) + load(z, y + 2)
                one += pltpu.roll(mid, 1, 1) + pltpu.roll(mid, 127, 1)
                two += pltpu.roll(mid, 2, 1) + pltpu.roll(mid, 126, 1)
                local = shifted[z, pl.ds(j * rows + y, 1), :]
                new = near * one + far * two + local * mid * gain + applied[z, here, lane(y)]
                if not first:
                    new = new - prev[z, here, lane(y)].astype(F32)
                nxt[z, here, lane(y)] = new.astype(nxt.dtype)
                if not last:
                    if z < planes // 2:
                        low[z, here, lane(y)] = new.astype(BF16)
                    else:
                        high[z - planes // 2, here, lane(y)] = new.astype(BF16)
        return carry

    lax.fori_loop(0, tiles, tile_step, 0)
    if not last:
        for z in range(planes):
            half = low[z] if z < planes // 2 else high[z - planes // 2]
            at = slice(z * cols, (z + 1) * cols)
            partial[:, at] = (project(half, proj[z], states, slots) * used[:, at]).astype(BF16)


def gram_kernel(states, cells, margin):
    groups, height, width = cells.shape
    total = jnp.zeros(margin.shape, F32)
    for j in range(height // states):
        block = cells[:, j * states : (j + 1) * states, :].reshape(groups * states, width)
        total += lax.dot_general(block, block, NT, preferred_element_type=F32)
    margin[...] = total


def rotate_kernel(states, margin, cells, rotated, inverse):
    n = margin.shape[0]
    lanes = lax.broadcasted_iota(jnp.int32, (8, n), 1)
    subs = lax.broadcasted_iota(jnp.int32, (8, n), 0)
    work = [margin[8 * i : 8 * i + 8, :] for i in range(n // 8)]
    for k in range(n):
        b, r = divmod(k, 8)
        row = work[b][r : r + 1, :]
        pivot = row[:, k : k + 1]
        ahead = jnp.where(lanes[0:1] == k, 1.0, row)
        inverse[k : k + 1, :] = jnp.where(lanes[0:1] <= k, ahead, 0.0) * lax.rsqrt(pivot)
        scaled = ahead * (1.0 / pivot)
        for i in range(b, n // 8):
            column = work[i][:, k : k + 1]
            if i == b:
                column = jnp.where(subs[:, 0:1] > r, column, 0.0)
            work[i] = jnp.where(lanes == k, 0.0, work[i]) - column * scaled
    mine = inverse[...].astype(BF16)
    groups, height, width = cells.shape
    for j in range(height // states):
        block = cells[:, j * states : (j + 1) * states, :].reshape(groups * states, width)
        new = lax.dot_general(mine, block, NN, preferred_element_type=F32).astype(BF16)
        rotated[:, j * states : (j + 1) * states, :] = new.reshape(groups, states, width)


def per_device(states, potential, proj_values, block_list, tile_count, strength):
    local_states, planes, rows_y, cells_x = states.shape
    _, tiles, slots, tile_cells = proj_values.shape
    rows = rows_y // tiles
    domains, groups = lax.axis_size("dom"), lax.axis_size("st")
    total_cells = planes * rows_y * cells_x * domains
    height, cols, count = tiles * local_states, tiles * slots, planes * tiles * slots
    sizes = (local_states, slots, rows)
    shape = (planes, height, tile_cells)
    half = (planes // 2, height, tile_cells)

    field = states.reshape(local_states, planes, tiles, rows, cells_x)
    field = field.transpose(1, 2, 0, 3, 4).reshape(shape)
    ids = block_list.reshape(1, count).astype(F32)
    sources = (0, 1, -1, 2, -2)
    all_ids = jnp.concatenate([ids] + [passed_along(ids, "dom", by) for by in sources[1:]], axis=0)
    used = jnp.arange(slots)[None, :] < tile_count.reshape(-1, 1)
    used = used.astype(F32).reshape(1, count)
    weight = strength[block_list.reshape(-1)].reshape(1, count) * used
    shifted = potential + (3.75 - center)

    f32 = lambda s: jax.ShapeDtypeStruct(s, F32)
    bf16 = lambda s: jax.ShapeDtypeStruct(s, BF16)

    low, high = field[: planes // 2], field[planes // 2 :]
    proj, partial = call(
        lambda *r: first_kernel(local_states, slots, *r),
        (bf16((planes, cols, tile_cells)), bf16((local_states, count))),
        flops=5e8, nbytes=4 * 2**20,
    )(field, proj_values.reshape(planes, cols, tile_cells), used)
    table = call(coupling_kernel, bf16((len(sources) * count, count)), flops=1e7, nbytes=10 * 2**20)(all_ids)

    prev, cur = None, field
    for m in range(4):
        first, last = m == 0, m == 3
        below = passed_along(high, "dom", 1)
        above = passed_along(low, "dom", -1)
        terms = [partial] + [passed_along(partial, "dom", by) for by in sources[1:]]
        args = [cur, below, above] + terms + [table, weight, used, proj, shifted]
        if not first:
            args.append(prev)
        if last:
            outs = bf16(shape)
        else:
            outs = (f32(shape), bf16(half), bf16(half), bf16((local_states, count)))
        got = call(
            lambda *r, first=first, last=last: step_kernel(sizes, first, last, *r),
            outs,
            scratch=[pltpu.VMEM(shape, F32)],
            flops=2e9, nbytes=20 * 2**20,
        )(*args)
        if last:
            filtered = got
        else:
            prev = cur
            cur, low, high, partial = got

    cells = filtered.reshape(groups, planes * height // groups, tile_cells)
    cells = lax.all_to_all(cells, "st", 0, 0, tiled=True)
    nstates = groups * local_states
    part = call(lambda *r: gram_kernel(local_states, *r), f32((nstates, nstates)), flops=1e8, nbytes=2**20)(cells)
    both = ("dom", "st")
    per = nstates // (domains * groups)
    mine = lax.all_to_all(part.reshape(domains * groups, per, nstates), both, 0, 0, tiled=True)
    mine = jnp.sum(mine, axis=0, keepdims=True) / total_cells
    margin = lax.all_to_all(jnp.broadcast_to(mine, (domains * groups, per, nstates)), both, 0, 0, tiled=True)
    rotated = call(
        lambda *r: rotate_kernel(local_states, *r),
        bf16(cells.shape),
        scratch=[pltpu.VMEM((nstates, nstates), F32)],
        flops=2e8, nbytes=2**21,
    )(margin.reshape(nstates, nstates), cells)
    rotated = lax.all_to_all(rotated, "st", 0, 0, tiled=True)
    rotated = rotated.reshape(planes, tiles, local_states, rows, cells_x).transpose(2, 0, 1, 3, 4)
    return rotated.reshape(states.shape)


def solution(mesh):
    return jax.shard_map(
        per_device,
        mesh=mesh,
        in_specs=(
            P("st", "dom", None, None),
            P("dom", None, None),
            P("dom", None, None, None),
            P("dom", None, None),
            P("dom", None),
            P(),
        ),
        out_specs=P("st", "dom", None, None),
        check_vma=False,
    )
```

time: 617 us -> 223 us (0.36); the launches traced: 608 us -> 222 us
  waiting for transfers between devices: 182 us -> 31.5 us
  local copies, waits for them, and re-layouts: 151 us -> 14.8 us
  other arithmetic: 126 us -> 1.04 us
  Pallas kernels: 0 us -> 59.4 us
  matrix products: 38.1 us -> 0 us
  between operations: 14.4 us -> 0.27 us
  blocking collectives: 63.9 us -> 73.9 us
  starting transfers between devices: 32.5 us -> 41.3 us
    all_gather x1 -> x0, waiting for transfers between devices: 108 us -> none  [per_device(): everything = lax.all_gather(filtered, 'st', axis=0, tiled=True)]
    slice x40 -> x3, local copies, waits for them, and re-layouts: 77.4 us -> 2.57 us  [per_device(): low, high = (field[:planes // 2], field[planes // 2:])]
    all_to_all x0 -> x4, blocking collectives: none -> 73.9 us  [the longest x1 23.6 us: per_device(): cells = lax.all_to_all(cells, 'st', 0, 0, tiled=True)]
    ppermute x16 -> x0, waiting for transfers between devices: 62.5 us -> none  [the longest x8 58.2 us: extended(): lax.ppermute(head, axis, [((i + 1) % count, i) for i in range(count)])]
    pallas_call x0 -> x8, Pallas kernels: none -> 59.4 us  [the longest x4 41.2 us: per_device(): call(lambda *r, first=first, last=last: step_kernel(sizes, first, last, *...]
    dot_general x10 -> x0, matrix products: 37.9 us -> none  [the longest x4 15.1 us: hamiltonian(): jnp.einsum('tkc,stc->tks', proj_masked, tiles, precision=lax.Precision.HI...]
    all_gather x1 -> x0, blocking collectives: 34.5 us -> none  [per_device(): margin = lax.all_gather(summed, 'st', axis=0, tiled=True) / total_cells]
    psum x1 -> x0, blocking collectives: 29.4 us -> none  [per_device(): summed = lax.psum(part_rows, 'dom')]
  transfers between devices with their start and end apart: 25 -> 28, of which waited for: 10 -> 7; matrix products, arithmetic and copies ran while one was open for 17% -> 5% of each run, Pallas kernels for 0% -> 3%
where the time goes in v1:
time: 223 us; the launch traced here: 222 us
  blocking collectives  73.9 us (33%)
  Pallas kernels  59.4 us (27%)
  starting transfers between devices  41.3 us (19%)
  waiting for transfers between devices  31.5 us (14%)
  local copies, waits for them, and re-layouts  14.8 us (7%)
    ppermute x28, starting transfers between devices, passed_along(): lax.ppermute(array, axis, [(i, (i + by) % devices) for i in range(devices)])  41.3 us
    pallas_call x4, Pallas kernels, per_device(): call(lambda *r, first=first, last=last: step_kernel(sizes, first, last, *...  41.2 us
    ppermute x28, waiting for transfers between devices, passed_along(): lax.ppermute(array, axis, [(i, (i + by) % devices) for i in range(devices)])  31.5 us
    all_to_all x1, blocking collectives, per_device(): cells = lax.all_to_all(cells, 'st', 0, 0, tiled=True)  23.6 us
    all_to_all x1, blocking collectives, per_device(): rotated = lax.all_to_all(rotated, 'st', 0, 0, tiled=True)  20.6 us
    all_to_all x1, blocking collectives, per_device(): lax.all_to_all(part.reshape(domains * groups, per, nstates), both, 0, 0,...  15.8 us
    all_to_all x1, blocking collectives, per_device(): lax.all_to_all(jnp.broadcast_to(mine, (domains * groups, per, nstates)),...  13.8 us
    pallas_call x1, Pallas kernels, per_device(): call(lambda *r: rotate_kernel(local_states, *r), bf16(cells.shape), scrat...  11.1 us
  transfers between devices with their start and end apart: 28, of which 7 were waited for; matrix products, arithmetic and copies ran while one was open for 5% of the time, Pallas kernels for 3%

profile of v1, /device:TPU:0, one launch (start us, length us, event | category | flops | bytes accessed | tf_op | source)
XLA Modules:
  0.0 222.3 jit_solution(6034853069956045229)
XLA Ops:
  0.9 4.1 %collective-permute-start.9 = (f32[1,1024]{1,0:T(1,128)S(1)}, f32[1,1024]{1,0:T(1,128)S(1)}, u32[]{:S(2)}, u32[]{:S(2)}) collective-permute-start(f32[1,1024]{1,0:T(1,128)S(1)} %convert_element_type.28), channel_id=1, source_target_pairs={{0,112},{8,120},{16,0},{24,8},{32,16},{40,24},{48,32},{56,40},{64,... | collective-permute-start | bytes 12296 | tf_op jit(solution)/shard_map/ppermute | solution.py:19
  4.9 3.0 %collective-permute-start.7 = (f32[1,1024]{1,0:T(1,128)S(1)}, f32[1,1024]{1,0:T(1,128)S(1)}, u32[]{:S(2)}, u32[]{:S(2)}) collective-permute-start(f32[1,1024]{1,0:T(1,128)S(1)} %convert_element_type.28), channel_id=1, source_target_pairs={{0,120},{8,0},{16,8},{24,16},{32,24},{40,32},{48,40},{56,48},{64,5... | collective-permute-start | bytes 12296 | tf_op jit(solution)/shard_map/ppermute | solution.py:19
  12.4 3.9 %collective-permute-start.1 = (bf16[2,256,512]{2,1,0:T(8,128)(2,1)}, bf16[2,256,512]{2,1,0:T(8,128)(2,1)S(1)}, u32[]{:S(2)}, u32[]{:S(2)}) collective-permute-start(bf16[2,256,512]{2,1,0:T(8,128)(2,1)} %slice.15), channel_id=1, source_target_pairs={{0,120},{8,0},{16,8},{24,16},{32,24},{40,32},{48,40},{56,48},{64,5... | collective-permute-start | bytes 1572872 | tf_op jit(solution)/shard_map/ppermute | solution.py:19
  19.6 6.1 %gather_fusion = f32[1024]{0:T(1024)S(1)} fusion(f32[12288]{0:T(1024)S(1)} %copy-done, s32[1024]{0:T(1024)S(1)} %broadcast_clamp_fusion), kind=kCustom, calls=%fused_computation | custom fusion | bytes 12288 | tf_op jit(solution)/shard_map/gather | solution.py:189
  27.7 5.2 %collective-permute-start.3 = (bf16[16,1024]{1,0:T(8,128)(2,1)S(1)}, bf16[16,1024]{1,0:T(8,128)(2,1)S(1)}, u32[]{:S(2)}, u32[]{:S(2)}) collective-permute-start(bf16[16,1024]{1,0:T(8,128)(2,1)S(1)} %get-tuple-element.19.r_3_), channel_id=1, source_target_pairs={{0,120},{8,0},{16,8},{24,16},{32,24},{40,32},{48,40},{56,48},{64,5... | collective-permute-start | bytes 98312 | tf_op jit(solution)/shard_map/ppermute | solution.py:19
  33.0 6.1 %shard_map.65.r_8_ = bf16[5120,1024]{1,0:T(8,128)(2,1)} custom-call(f32[5,1024]{1,0:T(8,128)S(1)} %concatenate.3.ids), custom_call_target="tpu_custom_call" | custom-call | flops 10000000 | bytes 10485760 | tf_op jit(solution)/shard_map/pallas_call | solution.py:201
  39.1 9.4 %shard_map.66 = (f32[4,256,512]{2,1,0:T(8,128)}, bf16[2,256,512]{2,1,0:T(8,128)(2,1)S(1)}, bf16[2,256,512]{2,1,0:T(8,128)(2,1)S(1)}, bf16[16,1024]{1,0:T(8,128)(2,1)S(1)}) custom-call(bf16[4,256,512]{2,1,0:T(8,128)(2,1)S(1)} %reshape.129.r_0_.r_13_, bf16[2,256,512]{2,1,0:T(8,128)(2,1)S(1)} %collective-permute-done.r_1_, ...), custom_call_target="tpu_custom_call" | custom-call | flops 2000000000 | bytes 20971520 | tf_op jit(solution)/shard_map/pallas_call | solution.py:216
  48.6 3.9 %collective-permute-start.11 = (bf16[2,256,512]{2,1,0:T(8,128)(2,1)S(1)}, bf16[2,256,512]{2,1,0:T(8,128)(2,1)S(1)}, u32[]{:S(2)}, u32[]{:S(2)}) collective-permute-start(bf16[2,256,512]{2,1,0:T(8,128)(2,1)S(1)} %get-tuple-element.23), channel_id=1, source_target_pairs={{0,120},{8,0},{16,8},{24,16},{32,24},{40,32},{48,40},{56,48},{64,5... | collective-permute-start | bytes 1572872 | tf_op jit(solution)/shard_map/ppermute | solution.py:19
  56.5 4.0 %collective-permute-done.15.r_7_ = bf16[16,1024]{1,0:T(8,128)(2,1)S(1)} collective-permute-done((bf16[16,1024]{1,0:T(8,128)(2,1)S(1)}, bf16[16,1024]{1,0:T(8,128)(2,1)S(1)}, u32[]{:S(2)}, u32[]{:S(2)}) %collective-permute-start.15) | collective-permute-done | bytes 32800 | tf_op jit(solution)/shard_map/ppermute | solution.py:19
  60.5 6.2 %collective-permute-done.14.r_6_ = bf16[16,1024]{1,0:T(8,128)(2,1)S(1)} collective-permute-done((bf16[16,1024]{1,0:T(8,128)(2,1)S(1)}, bf16[16,1024]{1,0:T(8,128)(2,1)S(1)}, u32[]{:S(2)}, u32[]{:S(2)}) %collective-permute-start.14) | collective-permute-done | bytes 32800 | tf_op jit(solution)/shard_map/ppermute | solution.py:19
  66.7 11.1 %shard_map.67 = (f32[4,256,512]{2,1,0:T(8,128)}, bf16[2,256,512]{2,1,0:T(8,128)(2,1)S(1)}, bf16[2,256,512]{2,1,0:T(8,128)(2,1)S(1)}, bf16[16,1024]{1,0:T(8,128)(2,1)S(1)}) custom-call(f32[4,256,512]{2,1,0:T(8,128)} %get-tuple-element.21.r_0_.r_13_, bf16[2,256,512]{2,1,0:T(8,128)(2,1)S(1)} %collective-permute-done.10.r_1_, ...), custom_call_target="tpu_custom_call" | custom-call | flops 2000000000 | bytes 20971520 | tf_op jit(solution)/shard_map/pallas_call | solution.py:216
  77.8 3.9 %collective-permute-start.17 = (bf16[2,256,512]{2,1,0:T(8,128)(2,1)S(1)}, bf16[2,256,512]{2,1,0:T(8,128)(2,1)S(1)}, u32[]{:S(2)}, u32[]{:S(2)}) collective-permute-start(bf16[2,256,512]{2,1,0:T(8,128)(2,1)S(1)} %get-tuple-element.27), channel_id=1, source_target_pairs={{0,120},{8,0},{16,8},{24,16},{32,24},{40,32},{48,40},{56,48},{64,5... | collective-permute-start | bytes 1572872 | tf_op jit(solution)/shard_map/ppermute | solution.py:19
  85.3 4.0 %collective-permute-done.21.r_7_ = bf16[16,1024]{1,0:T(8,128)(2,1)S(1)} collective-permute-done((bf16[16,1024]{1,0:T(8,128)(2,1)S(1)}, bf16[16,1024]{1,0:T(8,128)(2,1)S(1)}, u32[]{:S(2)}, u32[]{:S(2)}) %collective-permute-start.21) | collective-permute-done | bytes 32800 | tf_op jit(solution)/shard_map/ppermute | solution.py:19
  89.3 6.6 %collective-permute-done.20.r_6_ = bf16[16,1024]{1,0:T(8,128)(2,1)S(1)} collective-permute-done((bf16[16,1024]{1,0:T(8,128)(2,1)S(1)}, bf16[16,1024]{1,0:T(8,128)(2,1)S(1)}, u32[]{:S(2)}, u32[]{:S(2)}) %collective-permute-start.20) | collective-permute-done | bytes 32800 | tf_op jit(solution)/shard_map/ppermute | solution.py:19
  95.9 10.8 %shard_map.68 = (f32[4,256,512]{2,1,0:T(8,128)S(1)}, bf16[2,256,512]{2,1,0:T(8,128)(2,1)S(1)}, bf16[2,256,512]{2,1,0:T(8,128)(2,1)S(1)}, bf16[16,1024]{1,0:T(8,128)(2,1)S(1)}) custom-call(f32[4,256,512]{2,1,0:T(8,128)} %get-tuple-element.25.r_0_.r_13_, bf16[2,256,512]{2,1,0:T(8,128)(2,1)S(1)} %collective-permute-done.16.r_1_, ...), custom_call_target="tpu_custom_call" | custom-call | flops 2000000000 | bytes 20971520 | tf_op jit(solution)/shard_map/pallas_call | solution.py:216
  106.9 3.8 %collective-permute-start.23 = (bf16[2,256,512]{2,1,0:T(8,128)(2,1)S(1)}, bf16[2,256,512]{2,1,0:T(8,128)(2,1)S(1)}, u32[]{:S(2)}, u32[]{:S(2)}) collective-permute-start(bf16[2,256,512]{2,1,0:T(8,128)(2,1)S(1)} %get-tuple-element.31), channel_id=1, source_target_pairs={{0,120},{8,0},{16,8},{24,16},{32,24},{40,32},{48,40},{56,48},{64,5... | collective-permute-start | bytes 1572872 | tf_op jit(solution)/shard_map/ppermute | solution.py:19
  114.3 4.1 %collective-permute-done.27.r_7_ = bf16[16,1024]{1,0:T(8,128)(2,1)S(1)} collective-permute-done((bf16[16,1024]{1,0:T(8,128)(2,1)S(1)}, bf16[16,1024]{1,0:T(8,128)(2,1)S(1)}, u32[]{:S(2)}, u32[]{:S(2)}) %collective-permute-start.27) | collective-permute-done | bytes 32800 | tf_op jit(solution)/shard_map/ppermute | solution.py:19
  118.4 6.5 %collective-permute-done.26.r_6_ = bf16[16,1024]{1,0:T(8,128)(2,1)S(1)} collective-permute-done((bf16[16,1024]{1,0:T(8,128)(2,1)S(1)}, bf16[16,1024]{1,0:T(8,128)(2,1)S(1)}, u32[]{:S(2)}, u32[]{:S(2)}) %collective-permute-start.26) | collective-permute-done | bytes 32800 | tf_op jit(solution)/shard_map/ppermute | solution.py:19
  125.0 9.8 %shard_map.69 = bf16[4,256,512]{2,1,0:T(8,128)(2,1)S(1)} custom-call(f32[4,256,512]{2,1,0:T(8,128)S(1)} %get-tuple-element.29.r_0_, bf16[2,256,512]{2,1,0:T(8,128)(2,1)S(1)} %collective-permute-done.22.r_1_, bf16[2,256,512]{2,1,0:T(8,128)(2,1)S(1)} %collective-permute-done.23.r_2_, bf16[16,1024]{1,0:T(8,128)(2,1)S(1)} %get-tuple-element.32.r_3_, ...), custom_call_target="tpu_custom_call" | custom-call | flops 2000000000 | bytes 20971520 | tf_op jit(solution)/shard_map/pallas_call | solution.py:216
  134.8 23.6 %all_to_all.20.r_0_.r_1_ = bf16[8,128,512]{2,1,0:T(8,128)(2,1)S(1)} all-to-all(bf16[8,128,512]{2,1,0:T(8,128)(2,1)S(1)} %bitcast.14), channel_id=1, replica_groups=mesh['dom'=16,'st'=8] {'st'}, dimensions={0} | all-to-all | bytes 2097152 | tf_op jit(solution)/shard_map/all_to_all | solution.py:229
  158.8 15.8 %all_to_all.21 = f32[128,1,128]{2,1,0:T(1,128)S(1)} all-to-all(f32[128,1,128]{2,1,0:T(1,128)S(1)} %bitcast.17), channel_id=1, replica_groups=mesh['dom'=16,'st'=8] {'dom','st'}, dimensions={0} | all-to-all | bytes 131072 | tf_op jit(solution)/shard_map/all_to_all | solution.py:234
  174.8 13.8 %all_to_all.22 = f32[128,1,128]{2,1,0:T(1,128)S(1)} all-to-all(f32[128,1,128]{2,1,0:T(1,128)S(1)} %broadcast_in_dim.2), channel_id=1, replica_groups=mesh['dom'=16,'st'=8] {'dom','st'}, dimensions={0} | all-to-all | bytes 131072 | tf_op jit(solution)/shard_map/all_to_all | solution.py:236
  188.7 11.1 %shard_map.71 = bf16[8,128,512]{2,1,0:T(8,128)(2,1)S(1)} custom-call(f32[128,128]{1,0:T(8,128)S(1)} %bitcast.16, bf16[8,128,512]{2,1,0:T(8,128)(2,1)S(1)} %all_to_all.20.r_0_.r_1_), custom_call_target="tpu_custom_call" | custom-call | flops 200000000 | bytes 2097152 | tf_op jit(solution)/shard_map/pallas_call | solution.py:237
  199.8 20.6 %all_to_all.23 = bf16[8,128,512]{2,1,0:T(8,128)(2,1)S(1)} all-to-all(bf16[8,128,512]{2,1,0:T(8,128)(2,1)S(1)} %shard_map.71), channel_id=1, replica_groups=mesh['dom'=16,'st'=8] {'st'}, dimensions={0} | all-to-all | bytes 2097152 | tf_op jit(solution)/shard_map/all_to_all | solution.py:243
  (77 shorter events, 24.4 us)
Async XLA Ops:
  0.9 18.3 %collective-permute-start.9 = (f32[1,1024]{1,0:T(1,128)S(1)}, f32[1,1024]{1,0:T(1,128)S(1)}, u32[]{:S(2)}, u32[]{:S(2)}) collective-permute-start(f32[1,1024]{1,0:T(1,128)S(1)} %convert_element_type.28), channel_id=1, source_target_pairs={{0,112},{8,120},{16,0},{24,8},{32,16},{40,24},{48,32},{56,40},{64,... | collective-permute-start | bytes 12296 | tf_op jit(solution)/shard_map/ppermute | solution.py:19
  4.9 14.3 %collective-permute-start.8 = (f32[1,1024]{1,0:T(1,128)S(1)}, f32[1,1024]{1,0:T(1,128)S(1)}, u32[]{:S(2)}, u32[]{:S(2)}) collective-permute-start(f32[1,1024]{1,0:T(1,128)S(1)} %convert_element_type.28), channel_id=1, source_target_pairs={{0,16},{8,24},{16,32},{24,40},{32,48},{40,56},{48,64},{56,72},{64,... | collective-permute-start | bytes 12296 | tf_op jit(solution)/shard_map/ppermute | solution.py:19
  4.9 20.9 %collective-permute-start.7 = (f32[1,1024]{1,0:T(1,128)S(1)}, f32[1,1024]{1,0:T(1,128)S(1)}, u32[]{:S(2)}, u32[]{:S(2)}) collective-permute-start(f32[1,1024]{1,0:T(1,128)S(1)} %convert_element_type.28), channel_id=1, source_target_pairs={{0,120},{8,0},{16,8},{24,16},{32,24},{40,32},{48,40},{56,48},{64,5... | collective-permute-start | bytes 12296 | tf_op jit(solution)/shard_map/ppermute | solution.py:19
  11.4 27.8 %collective-permute-start = (bf16[2,256,512]{2,1,0:T(8,128)(2,1)}, bf16[2,256,512]{2,1,0:T(8,128)(2,1)S(1)}, u32[]{:S(2)}, u32[]{:S(2)}) collective-permute-start(bf16[2,256,512]{2,1,0:T(8,128)(2,1)} %slice.13), channel_id=1, source_target_pairs={{0,8},{8,16},{16,24},{24,32},{32,40},{40,48},{48,56},{56,64},{64,7... | collective-permute-start | bytes 1572872 | tf_op jit(solution)/shard_map/ppermute | solution.py:19
  12.4 26.8 %collective-permute-start.1 = (bf16[2,256,512]{2,1,0:T(8,128)(2,1)}, bf16[2,256,512]{2,1,0:T(8,128)(2,1)S(1)}, u32[]{:S(2)}, u32[]{:S(2)}) collective-permute-start(bf16[2,256,512]{2,1,0:T(8,128)(2,1)} %slice.15), channel_id=1, source_target_pairs={{0,120},{8,0},{16,8},{24,16},{32,24},{40,32},{48,40},{56,48},{64,5... | collective-permute-start | bytes 1572872 | tf_op jit(solution)/shard_map/ppermute | solution.py:19
  19.2 8.5 %collective-permute-start.6 = (f32[1,1024]{1,0:T(1,128)S(1)}, f32[1,1024]{1,0:T(1,128)S(1)}, u32[]{:S(2)}, u32[]{:S(2)}) collective-permute-start(f32[1,1024]{1,0:T(1,128)S(1)} %convert_element_type.28), channel_id=1, source_target_pairs={{0,8},{8,16},{16,24},{24,32},{32,40},{40,48},{48,56},{56,64},{64,7... | collective-permute-start | bytes 12296 | tf_op jit(solution)/shard_map/ppermute | solution.py:19
  19.3 13.7 %collective-permute-start.5 = (bf16[16,1024]{1,0:T(8,128)(2,1)S(1)}, bf16[16,1024]{1,0:T(8,128)(2,1)S(1)}, u32[]{:S(2)}, u32[]{:S(2)}) collective-permute-start(bf16[16,1024]{1,0:T(8,128)(2,1)S(1)} %get-tuple-element.19.r_3_), channel_id=1, source_target_pairs={{0,112},{8,120},{16,0},{24,8},{32,16},{40,24},{48,32},{56,40},{64,... | collective-permute-start | bytes 98312 | tf_op jit(solution)/shard_map/ppermute | solution.py:19
  25.8 13.3 %collective-permute-start.4 = (bf16[16,1024]{1,0:T(8,128)(2,1)S(1)}, bf16[16,1024]{1,0:T(8,128)(2,1)S(1)}, u32[]{:S(2)}, u32[]{:S(2)}) collective-permute-start(bf16[16,1024]{1,0:T(8,128)(2,1)S(1)} %get-tuple-element.19.r_3_), channel_id=1, source_target_pairs={{0,16},{8,24},{16,32},{24,40},{32,48},{40,56},{48,64},{56,72},{64,... | collective-permute-start | bytes 98312 | tf_op jit(solution)/shard_map/ppermute | solution.py:19
  27.7 11.4 %collective-permute-start.3 = (bf16[16,1024]{1,0:T(8,128)(2,1)S(1)}, bf16[16,1024]{1,0:T(8,128)(2,1)S(1)}, u32[]{:S(2)}, u32[]{:S(2)}) collective-permute-start(bf16[16,1024]{1,0:T(8,128)(2,1)S(1)} %get-tuple-element.19.r_3_), channel_id=1, source_target_pairs={{0,120},{8,0},{16,8},{24,16},{32,24},{40,32},{48,40},{56,48},{64,5... | collective-permute-start | bytes 98312 | tf_op jit(solution)/shard_map/ppermute | solution.py:19
  48.6 18.1 %collective-permute-start.10 = (bf16[2,256,512]{2,1,0:T(8,128)(2,1)S(1)}, bf16[2,256,512]{2,1,0:T(8,128)(2,1)S(1)}, u32[]{:S(2)}, u32[]{:S(2)}) collective-permute-start(bf16[2,256,512]{2,1,0:T(8,128)(2,1)S(1)} %get-tuple-element.22), channel_id=1, source_target_pairs={{0,8},{8,16},{16,24},{24,32},{32,40},{40,48},{48,56},{56,64},{64,7... | collective-permute-start | bytes 1572872 | tf_op jit(solution)/shard_map/ppermute | solution.py:19
  48.6 18.1 %collective-permute-start.11 = (bf16[2,256,512]{2,1,0:T(8,128)(2,1)S(1)}, bf16[2,256,512]{2,1,0:T(8,128)(2,1)S(1)}, u32[]{:S(2)}, u32[]{:S(2)}) collective-permute-start(bf16[2,256,512]{2,1,0:T(8,128)(2,1)S(1)} %get-tuple-element.23), channel_id=1, source_target_pairs={{0,120},{8,0},{16,8},{24,16},{32,24},{40,32},{48,40},{56,48},{64,5... | collective-permute-start | bytes 1572872 | tf_op jit(solution)/shard_map/ppermute | solution.py:19
  52.4 8.0 %collective-permute-start.15 = (bf16[16,1024]{1,0:T(8,128)(2,1)S(1)}, bf16[16,1024]{1,0:T(8,128)(2,1)S(1)}, u32[]{:S(2)}, u32[]{:S(2)}) collective-permute-start(bf16[16,1024]{1,0:T(8,128)(2,1)S(1)} %get-tuple-element.24.r_3_), channel_id=1, source_target_pairs={{0,112},{8,120},{16,0},{24,8},{32,16},{40,24},{48,32},{56,40},{64,... | collective-permute-start | bytes 98312 | tf_op jit(solution)/shard_map/ppermute | solution.py:19
  52.8 13.8 %collective-permute-start.14 = (bf16[16,1024]{1,0:T(8,128)(2,1)S(1)}, bf16[16,1024]{1,0:T(8,128)(2,1)S(1)}, u32[]{:S(2)}, u32[]{:S(2)}) collective-permute-start(bf16[16,1024]{1,0:T(8,128)(2,1)S(1)} %get-tuple-element.24.r_3_), channel_id=1, source_target_pairs={{0,16},{8,24},{16,32},{24,40},{32,48},{40,56},{48,64},{56,72},{64,... | collective-permute-start | bytes 98312 | tf_op jit(solution)/shard_map/ppermute | solution.py:19
  54.5 12.2 %collective-permute-start.13 = (bf16[16,1024]{1,0:T(8,128)(2,1)S(1)}, bf16[16,1024]{1,0:T(8,128)(2,1)S(1)}, u32[]{:S(2)}, u32[]{:S(2)}) collective-permute-start(bf16[16,1024]{1,0:T(8,128)(2,1)S(1)} %get-tuple-element.24.r_3_), channel_id=1, source_target_pairs={{0,120},{8,0},{16,8},{24,16},{32,24},{40,32},{48,40},{56,48},{64,5... | collective-permute-start | bytes 98312 | tf_op jit(solution)/shard_map/ppermute | solution.py:19
  77.8 18.1 %collective-permute-start.16 = (bf16[2,256,512]{2,1,0:T(8,128)(2,1)S(1)}, bf16[2,256,512]{2,1,0:T(8,128)(2,1)S(1)}, u32[]{:S(2)}, u32[]{:S(2)}) collective-permute-start(bf16[2,256,512]{2,1,0:T(8,128)(2,1)S(1)} %get-tuple-element.26), channel_id=1, source_target_pairs={{0,8},{8,16},{16,24},{24,32},{32,40},{40,48},{48,56},{56,64},{64,7... | collective-permute-start | bytes 1572872 | tf_op jit(solution)/shard_map/ppermute | solution.py:19
  77.8 18.1 %collective-permute-start.17 = (bf16[2,256,512]{2,1,0:T(8,128)(2,1)S(1)}, bf16[2,256,512]{2,1,0:T(8,128)(2,1)S(1)}, u32[]{:S(2)}, u32[]{:S(2)}) collective-permute-start(bf16[2,256,512]{2,1,0:T(8,128)(2,1)S(1)} %get-tuple-element.27), channel_id=1, source_target_pairs={{0,120},{8,0},{16,8},{24,16},{32,24},{40,32},{48,40},{56,48},{64,5... | collective-permute-start | bytes 1572872 | tf_op jit(solution)/shard_map/ppermute | solution.py:19
  81.7 7.6 %collective-permute-start.21 = (bf16[16,1024]{1,0:T(8,128)(2,1)S(1)}, bf16[16,1024]{1,0:T(8,128)(2,1)S(1)}, u32[]{:S(2)}, u32[]{:S(2)}) collective-permute-start(bf16[16,1024]{1,0:T(8,128)(2,1)S(1)} %get-tuple-element.28.r_3_), channel_id=1, source_target_pairs={{0,112},{8,120},{16,0},{24,8},{32,16},{40,24},{48,32},{56,40},{64,... | collective-permute-start | bytes 98312 | tf_op jit(solution)/shard_map/ppermute | solution.py:19
  82.0 13.9 %collective-permute-start.20 = (bf16[16,1024]{1,0:T(8,128)(2,1)S(1)}, bf16[16,1024]{1,0:T(8,128)(2,1)S(1)}, u32[]{:S(2)}, u32[]{:S(2)}) collective-permute-start(bf16[16,1024]{1,0:T(8,128)(2,1)S(1)} %get-tuple-element.28.r_3_), channel_id=1, source_target_pairs={{0,16},{8,24},{16,32},{24,40},{32,48},{40,56},{48,64},{56,72},{64,... | collective-permute-start | bytes 98312 | tf_op jit(solution)/shard_map/ppermute | solution.py:19
  83.7 12.2 %collective-permute-start.19 = (bf16[16,1024]{1,0:T(8,128)(2,1)S(1)}, bf16[16,1024]{1,0:T(8,128)(2,1)S(1)}, u32[]{:S(2)}, u32[]{:S(2)}) collective-permute-start(bf16[16,1024]{1,0:T(8,128)(2,1)S(1)} %get-tuple-element.28.r_3_), channel_id=1, source_target_pairs={{0,120},{8,0},{16,8},{24,16},{32,24},{40,32},{48,40},{56,48},{64,5... | collective-permute-start | bytes 98312 | tf_op jit(solution)/shard_map/ppermute | solution.py:19
  106.8 18.2 %collective-permute-start.22 = (bf16[2,256,512]{2,1,0:T(8,128)(2,1)S(1)}, bf16[2,256,512]{2,1,0:T(8,128)(2,1)S(1)}, u32[]{:S(2)}, u32[]{:S(2)}) collective-permute-start(bf16[2,256,512]{2,1,0:T(8,128)(2,1)S(1)} %get-tuple-element.30), channel_id=1, source_target_pairs={{0,8},{8,16},{16,24},{24,32},{32,40},{40,48},{48,56},{56,64},{64,7... | collective-permute-start | bytes 1572872 | tf_op jit(solution)/shard_map/ppermute | solution.py:19
  106.9 18.1 %collective-permute-start.23 = (bf16[2,256,512]{2,1,0:T(8,128)(2,1)S(1)}, bf16[2,256,512]{2,1,0:T(8,128)(2,1)S(1)}, u32[]{:S(2)}, u32[]{:S(2)}) collective-permute-start(bf16[2,256,512]{2,1,0:T(8,128)(2,1)S(1)} %get-tuple-element.31), channel_id=1, source_target_pairs={{0,120},{8,0},{16,8},{24,16},{32,24},{40,32},{48,40},{56,48},{64,5... | collective-permute-start | bytes 1572872 | tf_op jit(solution)/shard_map/ppermute | solution.py:19
  110.7 7.7 %collective-permute-start.27 = (bf16[16,1024]{1,0:T(8,128)(2,1)S(1)}, bf16[16,1024]{1,0:T(8,128)(2,1)S(1)}, u32[]{:S(2)}, u32[]{:S(2)}) collective-permute-start(bf16[16,1024]{1,0:T(8,128)(2,1)S(1)} %get-tuple-element.32.r_3_), channel_id=1, source_target_pairs={{0,112},{8,120},{16,0},{24,8},{32,16},{40,24},{48,32},{56,40},{64,... | collective-permute-start | bytes 98312 | tf_op jit(solution)/shard_map/ppermute | solution.py:19
  111.0 14.0 %collective-permute-start.26 = (bf16[16,1024]{1,0:T(8,128)(2,1)S(1)}, bf16[16,1024]{1,0:T(8,128)(2,1)S(1)}, u32[]{:S(2)}, u32[]{:S(2)}) collective-permute-start(bf16[16,1024]{1,0:T(8,128)(2,1)S(1)} %get-tuple-element.32.r_3_), channel_id=1, source_target_pairs={{0,16},{8,24},{16,32},{24,40},{32,48},{40,56},{48,64},{56,72},{64,... | collective-permute-start | bytes 98312 | tf_op jit(solution)/shard_map/ppermute | solution.py:19
  112.7 12.2 %collective-permute-start.25 = (bf16[16,1024]{1,0:T(8,128)(2,1)S(1)}, bf16[16,1024]{1,0:T(8,128)(2,1)S(1)}, u32[]{:S(2)}, u32[]{:S(2)}) collective-permute-start(bf16[16,1024]{1,0:T(8,128)(2,1)S(1)} %get-tuple-element.32.r_3_), channel_id=1, source_target_pairs={{0,120},{8,0},{16,8},{24,16},{32,24},{40,32},{48,40},{56,48},{64,5... | collective-permute-start | bytes 98312 | tf_op jit(solution)/shard_map/ppermute | solution.py:19
  (9 other events, 66.5 us)

commit v2 on v1

v2 whole, which is shorter than its diff:
```python
import jax
import jax.numpy as jnp
from jax import lax
from jax.experimental import pallas as pl
from jax.experimental.pallas import tpu as pltpu
from jax.sharding import PartitionSpec as P

center = 8.25
half_width = 7.75

F32 = jnp.float32
BF16 = jnp.bfloat16
NT = (((1,), (1,)), ((), ()))
NN = (((1,), (0,)), ((), ()))


def passed_along(array, axis, by):
    devices = lax.axis_size(axis)
    return lax.ppermute(array, axis, [(i, (i + by) % devices) for i in range(devices)])


def call(kernel, out_shape, scratch=(), vmem=20, flops=0, nbytes=0, **specs):
    return pl.pallas_call(
        kernel,
        out_shape=out_shape,
        **specs,
        scratch_shapes=list(scratch),
        compiler_params=pltpu.CompilerParams(vmem_limit_bytes=vmem * 2**20),
        cost_estimate=pl.CostEstimate(flops=int(flops), bytes_accessed=int(nbytes), transcendentals=0),
    )


def rows_at(t, states, base=0):
    return pl.ds(pl.multiple_of(base + t * states, states), states)


def lane(y):
    return slice(y * 128, (y + 1) * 128)


def block_mask(rows, cols, row_block, col_block):
    row = lax.broadcasted_iota(jnp.int32, (rows, cols), 0) // row_block
    col = lax.broadcasted_iota(jnp.int32, (rows, cols), 1) // col_block
    return row == col


def project(field, proj, states, slots):
    both = lax.dot_general(field, proj, NT, preferred_element_type=F32)
    both = jnp.where(block_mask(*both.shape, states, slots), both, 0.0)
    return jnp.sum(both.reshape(-1, states, both.shape[1]), axis=0)


def write_message(message, base, partial):
    high, width = partial.shape[0], message.shape[1]
    for i in range(partial.shape[1] // width):
        message[base + i * high : base + (i + 1) * high, :] = partial[:, i * width : (i + 1) * width]


def read_message(message, base, high, count):
    width = message.shape[1]
    return jnp.concatenate(
        [message[base + i * high : base + (i + 1) * high, :] for i in range(count // width)], axis=1
    )


def spread_rows(digits, rows_of):
    tiles, slots = digits.shape
    cols = tiles * slots
    to = lax.broadcasted_iota(jnp.int32, (slots, cols), 1) % slots
    pick = jnp.where(lax.broadcasted_iota(jnp.int32, (slots, cols), 0) == to, 1.0, 0.0)
    wide = lax.dot_general(digits.astype(BF16), pick.astype(BF16), NN, preferred_element_type=F32)
    return jnp.sum(jnp.where(rows_of, wide, 0.0), axis=0, keepdims=True)


def first_kernel(states, slots, cells, proj_values, names, counts, *refs):
    field, proj, ids, used, partial, low, high, raw, sems = refs
    planes, height = field.shape[:2]
    cols = proj.shape[1]
    tiles, rows = height // states, cells.shape[1] * states // height
    half = planes // 2
    copies = [pltpu.make_async_copy(proj_values.at[z], raw.at[z], sems.at[z]) for z in range(planes)]
    for copy in copies:
        copy.start()
    rows_of = block_mask(tiles, cols, 1, slots)
    slot = (lax.broadcasted_iota(jnp.int32, (1, cols), 1) % slots).astype(F32)
    tops, bottoms = [], []
    for z in range(planes):
        name = names[z].astype(F32)
        top = jnp.floor(name * (1.0 / 128.0))
        tops.append(spread_rows(top, rows_of))
        bottoms.append(spread_rows(name - 128.0 * top, rows_of))
        count = jnp.broadcast_to(counts[z : z + 1, :].astype(F32), (tiles, tiles))
        count = jnp.where(block_mask(tiles, tiles, 1, 1), count, 0.0)
        count = jnp.broadcast_to(jnp.sum(count, axis=1, keepdims=True), (tiles, cols))
        count = jnp.sum(jnp.where(rows_of, count, 0.0), axis=0, keepdims=True)
        at = slice(z * cols, (z + 1) * cols)
        used[:, at] = jnp.where(slot < count, 1.0, 0.0)
        ids[:, at] = tops[z] * 128.0 + bottoms[z]
        for y in range(tiles * rows):
            field[z, (y // rows) * states : (y // rows + 1) * states, lane(y % rows)] = cells[z, y]
        message = low if z < half else high
        message[z % half * height : (z % half + 1) * height, :] = field[z]
    extra = partial.shape[0] - states
    row = lax.broadcasted_iota(jnp.int32, (extra, planes * cols), 0)
    top, bottom = jnp.concatenate(tops, axis=1), jnp.concatenate(bottoms, axis=1)
    partial[states:, :] = jnp.where(row == 0, top, jnp.where(row == 1, bottom, 0.0)).astype(BF16)
    for z in range(planes):
        copies[z].wait()
        proj[z] = raw[z].astype(BF16)
        at = slice(z * cols, (z + 1) * cols)
        partial[:states, at] = (project(field[z], proj[z], states, slots) * used[:, at]).astype(BF16)
    write_message(low, half * height, partial[...])
    write_message(high, half * height, partial[...])


def fill_table(parts, states, own_ids, table):
    count = own_ids.shape[1]
    for e, part in enumerate(parts):
        digits = part[states : states + 2, :].astype(F32)
        names = digits[0:1] * 128.0 + digits[1:2]
        for q in range(0, count, 128):
            column = jnp.broadcast_to(names[:, q : q + 128], (128, 128)).T
            for p in range(0, count, 128):
                same = jnp.where(column == own_ids[:, p : p + 128], 1.0, 0.0)
                table[e * count + q : e * count + q + 128, p : p + 128] = same.astype(BF16)


def local_kernel(sizes, first, *refs):
    states, slots, rows = sizes
    refs = list(refs)
    cur, potential, own = refs[:3]
    rest = refs[3:]
    if first:
        ids, base, share, table = rest
        fill_table([own[...]], states, ids, table)
    else:
        table, prev, base, share = rest
    planes, height, width = cur.shape
    tiles = height // states
    gain = (1.0 if first else 2.0) / half_width
    near, far = -gain * 2.0 / 3.0, gain / 24.0
    share[...] = lax.dot_general(own[:states, :], table[...], NN, preferred_element_type=F32)

    def tile_step(j, carry):
        here = rows_at(j, states)
        left, right = rows_at((j + tiles - 1) % tiles, states), rows_at((j + 1) % tiles, states)

        def load(z, y):
            if y < 0:
                return cur[z, left, lane(y + rows)].astype(F32)
            if y >= rows:
                return cur[z, right, lane(y - rows)].astype(F32)
            return cur[z, here, lane(y)].astype(F32)

        for y in range(rows):
            mids = [load(z, y) for z in range(planes)]
            for z in range(planes):
                mid = mids[z]
                one = load(z, y - 1) + load(z, y + 1)
                two = load(z, y - 2) + load(z, y + 2)
                one += pltpu.roll(mid, 1, 1) + pltpu.roll(mid, 127, 1)
                two += pltpu.roll(mid, 2, 1) + pltpu.roll(mid, 126, 1)
                for by in (-1, 1):
                    if 0 <= z + by < planes:
                        one += mids[z + by]
                    if 0 <= z + 2 * by < planes:
                        two += mids[z + 2 * by]
                new = near * one + far * two + (potential[z, pl.ds(j * rows + y, 1), :] + (3.75 - center)) * mid * gain
                if not first:
                    new = new - prev[z, here, lane(y)].astype(F32)
                base[z, here, lane(y)] = new
        return carry

    lax.fori_loop(0, tiles, tile_step, 0)


def step_kernel(sizes, first, last, *refs):
    states, slots, rows = sizes
    refs = list(refs)
    base, share, below, above, below2, above2, weight, used, proj = refs[:9]
    rest = refs[9:]
    planes, height, width = base.shape
    half = planes // 2
    tiles = height // states
    cols = proj.shape[1]
    count = planes * cols
    gain = (1.0 if first else 2.0) / half_width
    near, far = -gain * 2.0 / 3.0, gain / 24.0

    taken = below2.shape[0]
    parts = [read_message(r, half * height, taken, count) for r in (below, above)]
    parts += [below2[...], above2[...]]
    if first:
        ids, table = rest.pop(0), rest.pop(0)
        fill_table(parts, states, ids, table)
    else:
        table = rest.pop(0)
    if last:
        (nxt, applied) = rest
    else:
        (nxt, low, high, partial, applied) = rest

    terms = jnp.concatenate([part[:states] for part in parts], axis=1)
    chosen = lax.dot_general(terms, table[...], NN, preferred_element_type=F32) + share[...]
    chosen = (chosen * (weight[...] * used[...]) * gain).astype(BF16)
    mask = block_mask(height, cols, states, slots)
    for z in range(planes):
        spread = jnp.broadcast_to(chosen[:, z * cols : (z + 1) * cols][None], (tiles, states, cols))
        spread = jnp.where(mask, spread.reshape(height, cols), jnp.zeros((), BF16))
        applied[z] = lax.dot_general(spread, proj[z], NN, preferred_element_type=F32)

    def tile_step(j, carry):
        here = rows_at(j, states)
        for y in range(rows):
            b2, b1 = [below[rows_at(j, states, z * height), lane(y)].astype(F32) for z in range(half)]
            a1, a2 = [above[rows_at(j, states, z * height), lane(y)].astype(F32) for z in range(half)]
            outer = {0: near * b1 + far * b2, 1: far * b1}
            outer.update({planes - 2: far * a1, planes - 1: near * a1 + far * a2})
            for z in range(planes):
                new = base[z, here, lane(y)] + applied[z, here, lane(y)]
                if z in outer:
                    new += outer[z]
                nxt[z, here, lane(y)] = new.astype(nxt.dtype)
                if not last:
                    message = low if z < half else high
                    message[rows_at(j, states, z % half * height), lane(y)] = new.astype(BF16)
        return carry

    lax.fori_loop(0, tiles, tile_step, 0)
    if not last:
        for z in range(planes):
            message = low if z < half else high
            plane = message[z % half * height : (z % half + 1) * height, :]
            at = slice(z * cols, (z + 1) * cols)
            partial[:, at] = (project(plane, proj[z], states, slots) * used[:, at]).astype(BF16)
        write_message(low, half * height, partial[...])
        write_message(high, half * height, partial[...])


def gram_kernel(states, cells, margin):
    groups, height, width = cells.shape
    total = jnp.zeros(margin.shape, F32)
    for j in range(height // states):
        block = cells[:, j * states : (j + 1) * states, :].reshape(groups * states, width)
        total += lax.dot_general(block, block, NT, preferred_element_type=F32)
    margin[...] = total


def recip(x):
    r = pltpu.reciprocal(x, approx=True)
    r = r * (2.0 - x * r)
    return r * (2.0 - x * r)

def inverse_factor(margin, inverse):
    n = margin.shape[0]
    lanes = lax.broadcasted_iota(jnp.int32, (8, n), 1)
    subs = lax.broadcasted_iota(jnp.int32, (8, n), 0)
    eye = lax.broadcasted_iota(jnp.int32, (n, n), 0) == lax.broadcasted_iota(jnp.int32, (n, n), 1)
    full = margin[...]
    diagonal = jnp.where(eye, full, 0.0)
    across = lax.rsqrt(jnp.sum(diagonal, axis=0, keepdims=True))
    down = lax.rsqrt(jnp.sum(diagonal, axis=1, keepdims=True))
    full = full * down * across
    work = [full[8 * i : 8 * i + 8, :] for i in range(n // 8)]
    for k in range(0, n, 4):
        b, r = divmod(k, 8)
        rows = [work[b][r + p : r + p + 1, :] for p in range(4)]
        cols = [[jnp.broadcast_to(work[i][:, k + p : k + p + 1], (8, n)) for p in range(4)] for i in range(b, n // 8)]
        entry = lambda p, q: jnp.broadcast_to(cols[0][q][r + p : r + p + 1, :], (8, n))
        s = {(p, q): entry(p, q) for p in range(4) for q in range(p + 1)}
        rows = [jnp.where(lanes == k + p, 1.0, jnp.where((lanes >= k) & (lanes < k + 4), 0.0, jnp.broadcast_to(rows[p], (8, n)))) for p in range(4)]
        a, bb, c = s[0, 0], s[1, 0], s[1, 1]
        det = recip(a * c - bb * bb)
        i00, i01, i11 = c * det, -bb * det, a * det
        x = {}
        for q in (2, 3):
            x[0, q] = i00 * s[q, 0] + i01 * s[q, 1]
            x[1, q] = i01 * s[q, 0] + i11 * s[q, 1]
        g22 = s[2, 2] - (s[2, 0] * x[0, 2] + s[2, 1] * x[1, 2])
        g32 = s[3, 2] - (s[3, 0] * x[0, 2] + s[3, 1] * x[1, 2])
        g33 = s[3, 3] - (s[3, 0] * x[0, 3] + s[3, 1] * x[1, 3])
        det2 = recip(g22 * g33 - g32 * g32)
        h00, h01, h11 = g33 * det2, -g32 * det2, g22 * det2
        low2 = rows[2] - (x[0, 2] * rows[0] + x[1, 2] * rows[1])
        low3 = rows[3] - (x[0, 3] * rows[0] + x[1, 3] * rows[1])
        y2 = h00 * low2 + h01 * low3
        y3 = h01 * low2 + h11 * low3
        y0 = i00 * rows[0] + i01 * rows[1] - (x[0, 2] * y2 + x[0, 3] * y3)
        y1 = i01 * rows[0] + i11 * rows[1] - (x[1, 2] * y2 + x[1, 3] * y3)
        inside = (lanes >= k) & (lanes < k + 4)
        for i in range(b, n // 8):
            c4 = cols[i - b]
            if i == b and r == 0:
                c4 = [jnp.where(subs >= 4, v, 0.0) for v in c4]
            elif i == b:
                continue
            change = (c4[0] * y0 + c4[1] * y1) + (c4[2] * y2 + c4[3] * y3)
            work[i] = jnp.where(inside, 0.0, work[i]) - change
        ra = recip(a)
        l10 = bb * ra
        d1 = c - bb * l10
        rg = recip(g22)
        l32 = g32 * rg
        d3 = g33 - g32 * l32
        out = [rows[0] * lax.rsqrt(a), (rows[1] - l10 * rows[0]) * lax.rsqrt(d1), low2 * lax.rsqrt(g22), (low3 - l32 * low2) * lax.rsqrt(d3)]
        for p in range(4):
            inverse[k + p : k + p + 1, :] = (jnp.where(lanes <= k + p, out[p], 0.0) * across)[0:1]

def rotate_kernel(states, margin, cells, rotated, inverse):
    inverse_factor(margin, inverse)
    mine = inverse[...].astype(BF16)
    groups, height, width = cells.shape
    rows = width // 128
    for j in range(height // states):
        block = cells[:, j * states : (j + 1) * states, :].reshape(groups * states, width)
        new = lax.dot_general(mine, block, NN, preferred_element_type=F32).astype(BF16)
        new = new.reshape(groups, states, width)
        for y in range(rows):
            rotated[:, j * rows + y, :, :] = new[:, :, lane(y)]


def per_device(states, potential, proj_values, block_list, tile_count, strength):
    local_states, planes, rows_y, cells_x = states.shape
    _, tiles, slots, tile_cells = proj_values.shape
    rows = rows_y // tiles
    domains, groups = lax.axis_size("dom"), lax.axis_size("st")
    total_cells = planes * rows_y * cells_x * domains
    height, cols, count = tiles * local_states, tiles * slots, planes * tiles * slots
    sizes = (local_states, slots, rows)
    shape = (planes, height, tile_cells)
    id_rows = 16

    weight = strength[block_list.reshape(-1)].reshape(1, count)

    f32 = lambda s: jax.ShapeDtypeStruct(s, F32)
    bf16 = lambda s: jax.ShapeDtypeStruct(s, BF16)

    def sent(rows_taken):
        message = (planes // 2 * height + rows_taken * count // tile_cells, tile_cells)
        return bf16((rows_taken, count)), bf16(message), bf16(message)

    row = f32((1, count))
    anywhere, whole = pl.BlockSpec(memory_space=pl.ANY), pl.BlockSpec()
    field, proj, ids, used, partial, low, high = call(
        lambda *r: first_kernel(local_states, slots, *r),
        (bf16(shape), bf16((planes, cols, tile_cells)), row, row) + sent(local_states + id_rows),
        scratch=[pltpu.VMEM((planes, cols, tile_cells), F32), pltpu.SemaphoreType.DMA((planes,))],
        in_specs=[whole, anywhere, whole, whole],
        flops=5e8, nbytes=4 * 2**20,
    )(states.transpose(1, 2, 0, 3), proj_values.reshape(planes, cols, tile_cells), block_list, tile_count)

    prev, cur = None, field
    for m in range(4):
        first, last = m == 0, m == 3
        below2, above2 = passed_along(partial, "dom", 2), passed_along(partial, "dom", -2)
        below = passed_along(high, "dom", 1)
        above = passed_along(low, "dom", -1)
        outs = [f32(shape), f32((local_states, count))]
        args = [cur, potential, partial] + ([ids] if first else [own_table, prev])
        got = call(
            lambda *r, first=first: local_kernel(sizes, first, *r),
            outs + ([bf16((count, count))] if first else []),
            flops=1e9, nbytes=8 * 2**20,
        )(*args)
        if first:
            base, share, own_table = got
        else:
            base, share = got
        args = [base, share, below, above, below2, above2, weight, used, proj]
        args += [ids] if first else [table]
        outs = [bf16((4 * count, count))] if first else []
        if last:
            outs += [bf16(shape)]
        else:
            made = sent(local_states)
            outs += [f32(shape), made[1], made[2], made[0]]
        got = call(
            lambda *r, first=first, last=last: step_kernel(sizes, first, last, *r),
            outs,
            scratch=[pltpu.VMEM(shape, F32)],
            flops=1e9, nbytes=8 * 2**20,
        )(*args)
        if first:
            table, *got = got
        if last:
            (filtered,) = got
        else:
            prev = cur
            cur, low, high, partial = got

    cells = filtered.reshape(groups, planes * height // groups, tile_cells)
    cells = lax.all_to_all(cells, "st", 0, 0, tiled=True)
    nstates = groups * local_states
    part = call(lambda *r: gram_kernel(local_states, *r), f32((nstates, nstates)), flops=1e8, nbytes=2**20)(cells)
    both = ("dom", "st")
    per = nstates // (domains * groups)
    mine = lax.all_to_all(part.reshape(domains * groups, per, nstates), both, 0, 0, tiled=True)
    mine = jnp.sum(mine, axis=0, keepdims=True) / total_cells
    margin = lax.all_to_all(jnp.broadcast_to(mine, (domains * groups, per, nstates)), both, 0, 0, tiled=True)
    rotated = call(
        lambda *r: rotate_kernel(local_states, *r),
        bf16((groups, planes * rows_y // groups, local_states, cells_x)),
        scratch=[pltpu.VMEM((nstates, nstates), F32)],
        flops=2e8, nbytes=2**21,
    )(margin.reshape(nstates, nstates), cells)
    rotated = lax.all_to_all(rotated, "st", 0, 0, tiled=True)
    return rotated.reshape(planes, rows_y, local_states, cells_x).transpose(2, 0, 1, 3)


def solution(mesh):
    return jax.shard_map(
        per_device,
        mesh=mesh,
        in_specs=(
            P("st", "dom", None, None),
            P("dom", None, None),
            P("dom", None, None, None),
            P("dom", None, None),
            P("dom", None),
            P(),
        ),
        out_specs=P("st", "dom", None, None),
        check_vma=False,
    )
```

time: 223 us -> 173 us (0.78)
  Pallas kernels: 59.4 us -> 37.6 us
  starting transfers between devices: 41.3 us -> 23.8 us
  local copies, waits for them, and re-layouts: 14.8 us -> 10.3 us
  waiting for transfers between devices: 31.5 us -> 28.8 us
    pallas_call x4, Pallas kernels: 41.2 us -> 11.8 us  [per_device(): call(lambda *r, first=first, last=last: step_kernel(sizes, first, last, *...]
    ppermute x28 -> x16, starting transfers between devices: 41.3 us -> 23.8 us  [passed_along(): lax.ppermute(array, axis, [(i, (i + by) % devices) for i in range(devices)])]
    pallas_call x3 -> x6, Pallas kernels: 17.7 us -> 25.4 us  [the longest x4 15.2 us: per_device(): call(lambda *r, first=first: local_kernel(sizes, first, *r), outs + ([bf1...]
    ppermute x28 -> x16, waiting for transfers between devices: 31.5 us -> 28.8 us  [passed_along(): lax.ppermute(array, axis, [(i, (i + by) % devices) for i in range(devices)])]
    all_to_all x1, blocking collectives: 15.8 us -> 13.1 us  [per_device(): lax.all_to_all(part.reshape(domains * groups, per, nstates), both, 0, 0,...]
    slice x3 -> x0, local copies, waits for them, and re-layouts: 2.57 us -> none  [per_device(): low, high = (field[:planes // 2], field[planes // 2:])]
  transfers between devices with their start and end apart: 28 -> 16, of which waited for: 7 -> 9; matrix products, arithmetic and copies ran while one was open for 5% -> 4% of each run, Pallas kernels for 3% -> 9%
where the time goes in v2:
time: 173 us
  blocking collectives  72.1 us (42%)
  Pallas kernels  37.6 us (22%)
  waiting for transfers between devices  28.8 us (17%)
  starting transfers between devices  23.8 us (14%)
  local copies, waits for them, and re-layouts  10.3 us (6%)
    ppermute x16, waiting for transfers between devices, passed_along(): lax.ppermute(array, axis, [(i, (i + by) % devices) for i in range(devices)])  28.8 us
    all_to_all x1, blocking collectives, per_device(): cells = lax.all_to_all(cells, 'st', 0, 0, tiled=True)  24.5 us
    ppermute x16, starting transfers between devices, passed_along(): lax.ppermute(array, axis, [(i, (i + by) % devices) for i in range(devices)])  23.8 us
    all_to_all x1, blocking collectives, per_device(): rotated = lax.all_to_all(rotated, 'st', 0, 0, tiled=True)  20.6 us
    pallas_call x4, Pallas kernels, per_device(): call(lambda *r, first=first: local_kernel(sizes, first, *r), outs + ([bf1...  15.2 us
    all_to_all x1, blocking collectives, per_device(): lax.all_to_all(jnp.broadcast_to(mine, (domains * groups, per, nstates)),...  13.8 us
    all_to_all x1, blocking collectives, per_device(): lax.all_to_all(part.reshape(domains * groups, per, nstates), both, 0, 0,...  13.1 us
    pallas_call x4, Pallas kernels, per_device(): call(lambda *r, first=first, last=last: step_kernel(sizes, first, last, *...  11.8 us
  transfers between devices with their start and end apart: 16, of which 9 were waited for; matrix products, arithmetic and copies ran while one was open for 4% of the time, Pallas kernels for 9%

profile of v2, /device:TPU:0, one launch (start us, length us, event | category | flops | bytes accessed | tf_op | source)
XLA Modules:
  0.0 173.1 jit_solution(7460037542177899664)
XLA Ops:
  2.8 2.8 %shard_map.64 = (bf16[4,256,512]{2,1,0:T(8,128)(2,1)S(1)}, bf16[4,256,512]{2,1,0:T(8,128)(2,1)S(1)}, f32[1,1024]{1,0:T(1,128)S(1)}, f32[1,1024]{1,0:T(1,128)S(1)...) custom-call(bf16[4,64,16,128]{3,2,1,0:T(8,128)(2,1)S(1)} %bitcast.16, ...), custom_call_target="tpu_custom_call" | custom-call | flops 500000000 | bytes 4194304 | tf_op jit(solution)/shard_map/pallas_call | solution.py:344
  5.8 3.8 %collective-permute-start.1 = (bf16[576,512]{1,0:T(8,128)(2,1)}, bf16[576,512]{1,0:T(8,128)(2,1)S(1)}, u32[]{:S(2)}, u32[]{:S(2)}) collective-permute-start(bf16[576,512]{1,0:T(8,128)(2,1)} %get-tuple-element.40), channel_id=1, source_target_pairs={{0,120},{8,0},{16,8},{24,16},{32,24},{40,32},{48,40},{56,48},{64,5... | collective-permute-start | bytes 1769480 | tf_op jit(solution)/shard_map/ppermute | solution.py:19
  11.8 6.2 %gather_fusion = f32[1024]{0:T(1024)S(1)} fusion(f32[12288]{0:T(1024)S(1)} %copy-done, s32[1024]{0:T(1024)S(1)} %broadcast_clamp_fusion), kind=kCustom, calls=%fused_computation | custom fusion | bytes 12288 | tf_op jit(solution)/shard_map/gather | solution.py:333
  18.0 3.9 %shard_map.65 = (f32[4,256,512]{2,1,0:T(8,128)S(1)}, f32[16,1024]{1,0:T(8,128)S(1)}, bf16[1024,1024]{1,0:T(8,128)(2,1)S(1)}) custom-call(bf16[4,256,512]{2,1,0:T(8,128)(2,1)S(1)} %get-tuple-element.34.r_0_.r_4_, f32[4,64,128]{2,1,0:T(8,128)S(1)} %copy-done.2, bf16[32,1024]{1,0:T(8,128)(2,1)} %get-tuple-element.35.r_2_, f32[1,1024]{1,0:T(1,128)S(1)} %get-tuple-element.36.r_3_.r_9_), custom_call_target="tpu_custom_call" | custom-call | flops 1000000000 | bytes 8388608 | tf_op jit(solution)/shard_map/pallas_call | solution.py:360
  21.9 2.9 %collective-permute-done.3.r_5_ = bf16[32,1024]{1,0:T(8,128)(2,1)S(1)} collective-permute-done((bf16[32,1024]{1,0:T(8,128)(2,1)}, bf16[32,1024]{1,0:T(8,128)(2,1)S(1)}, u32[]{:S(2)}, u32[]{:S(2)}) %collective-permute-start.3) | collective-permute-done | bytes 65568 | tf_op jit(solution)/shard_map/ppermute | solution.py:19
  26.6 4.7 %shard_map.66 = (bf16[4096,1024]{1,0:T(8,128)(2,1)S(1)}, f32[4,256,512]{2,1,0:T(8,128)S(1)}, bf16[544,512]{1,0:T(8,128)(2,1)S(1)}, bf16[544,512]{1,0:T(8,128)(2,1)S(1)}, bf16[16,1024]{1,0:T(8,128)(2,1)S(1)}) custom-call(f32[4,256,512]{2,1,0:T(8,128)S(1)} %get-tuple-element.37.r_0_, f32[16,1024]{1,0:T(8,128)S(1)} %get-tuple-element.38.r_1_, ...), custom_call_target="tpu_custom_call" | custom-call | flops 1000000000 | bytes 8388608 | tf_op jit(solution)/shard_map/pallas_call | solution.py:377
  31.5 3.8 %collective-permute-start.5 = (bf16[544,512]{1,0:T(8,128)(2,1)S(1)}, bf16[544,512]{1,0:T(8,128)(2,1)S(1)}, u32[]{:S(2)}, u32[]{:S(2)}) collective-permute-start(bf16[544,512]{1,0:T(8,128)(2,1)S(1)} %get-tuple-element.49), channel_id=1, source_target_pairs={{0,120},{8,0},{16,8},{24,16},{32,24},{40,32},{48,40},{56,48},{64,5... | collective-permute-start | bytes 1671176 | tf_op jit(solution)/shard_map/ppermute | solution.py:19
  37.3 3.8 %shard_map.67 = (f32[4,256,512]{2,1,0:T(8,128)S(1)}, f32[16,1024]{1,0:T(8,128)S(1)}) custom-call(f32[4,256,512]{2,1,0:T(8,128)S(1)} %get-tuple-element.43.r_0_.r_4_, f32[4,64,128]{2,1,0:T(8,128)S(1)} %copy-done.2, bf16[16,1024]{1,0:T(8,128)(2,1)S(1)} %get-tuple-element.44.r_2_, bf16[1024,1024]{1,0:T(8,128)(2,1)S(1)} %get-tuple-element.45.r_3_, ...), custom_call_target="tpu_custom_call" | custom-call | flops 1000000000 | bytes 8388608 | tf_op jit(solution)/shard_map/pallas_call | solution.py:360
  41.1 6.0 %collective-permute-done.7.r_5_ = bf16[16,1024]{1,0:T(8,128)(2,1)S(1)} collective-permute-done((bf16[16,1024]{1,0:T(8,128)(2,1)S(1)}, bf16[16,1024]{1,0:T(8,128)(2,1)S(1)}, u32[]{:S(2)}, u32[]{:S(2)}) %collective-permute-start.7) | collective-permute-done | bytes 32800 | tf_op jit(solution)/shard_map/ppermute | solution.py:19
  47.1 2.8 %collective-permute-done.6.r_4_ = bf16[16,1024]{1,0:T(8,128)(2,1)S(1)} collective-permute-done((bf16[16,1024]{1,0:T(8,128)(2,1)S(1)}, bf16[16,1024]{1,0:T(8,128)(2,1)S(1)}, u32[]{:S(2)}, u32[]{:S(2)}) %collective-permute-start.6) | collective-permute-done | bytes 32800 | tf_op jit(solution)/shard_map/ppermute | solution.py:19
  49.9 2.5 %shard_map.68 = (f32[4,256,512]{2,1,0:T(8,128)S(1)}, bf16[544,512]{1,0:T(8,128)(2,1)S(1)}, bf16[544,512]{1,0:T(8,128)(2,1)S(1)}, bf16[16,1024]{1,0:T(8,128)(2,1)S(1)}) custom-call(f32[4,256,512]{2,1,0:T(8,128)S(1)} %get-tuple-element.46.r_0_, f32[16,1024]{1,0:T(8,128)S(1)} %get-tuple-element.47.r_1_, bf16[544,512]{1,0:T(8,128)(2,1)S(1)} %collective-permute-done.4.r_2_, ...), custom_call_target="tpu_custom_call" | custom-call | flops 1000000000 | bytes 8388608 | tf_op jit(solution)/shard_map/pallas_call | solution.py:377
  52.5 3.8 %collective-permute-start.9 = (bf16[544,512]{1,0:T(8,128)(2,1)S(1)}, bf16[544,512]{1,0:T(8,128)(2,1)S(1)}, u32[]{:S(2)}, u32[]{:S(2)}) collective-permute-start(bf16[544,512]{1,0:T(8,128)(2,1)S(1)} %get-tuple-element.56), channel_id=1, source_target_pairs={{0,120},{8,0},{16,8},{24,16},{32,24},{40,32},{48,40},{56,48},{64,5... | collective-permute-start | bytes 1671176 | tf_op jit(solution)/shard_map/ppermute | solution.py:19
  58.4 3.8 %shard_map.69 = (f32[4,256,512]{2,1,0:T(8,128)S(1)}, f32[16,1024]{1,0:T(8,128)S(1)}) custom-call(f32[4,256,512]{2,1,0:T(8,128)S(1)} %get-tuple-element.51.r_0_.r_4_, f32[4,64,128]{2,1,0:T(8,128)S(1)} %copy-done.2, bf16[16,1024]{1,0:T(8,128)(2,1)S(1)} %get-tuple-element.52.r_2_, bf16[1024,1024]{1,0:T(8,128)(2,1)S(1)} %get-tuple-element.45.r_3_, ...), custom_call_target="tpu_custom_call" | custom-call | flops 1000000000 | bytes 8388608 | tf_op jit(solution)/shard_map/pallas_call | solution.py:360
  62.1 5.0 %collective-permute-done.11.r_5_ = bf16[16,1024]{1,0:T(8,128)(2,1)S(1)} collective-permute-done((bf16[16,1024]{1,0:T(8,128)(2,1)S(1)}, bf16[16,1024]{1,0:T(8,128)(2,1)S(1)}, u32[]{:S(2)}, u32[]{:S(2)}) %collective-permute-start.11) | collective-permute-done | bytes 32800 | tf_op jit(solution)/shard_map/ppermute | solution.py:19
  68.6 2.5 %shard_map.70 = (f32[4,256,512]{2,1,0:T(8,128)S(1)}, bf16[544,512]{1,0:T(8,128)(2,1)S(1)}, bf16[544,512]{1,0:T(8,128)(2,1)S(1)}, bf16[16,1024]{1,0:T(8,128)(2,1)S(1)}) custom-call(f32[4,256,512]{2,1,0:T(8,128)S(1)} %get-tuple-element.53.r_0_, f32[16,1024]{1,0:T(8,128)S(1)} %get-tuple-element.54.r_1_, bf16[544,512]{1,0:T(8,128)(2,1)S(1)} %collective-permute-done.8.r_2_, ...), custom_call_target="tpu_custom_call" | custom-call | flops 1000000000 | bytes 8388608 | tf_op jit(solution)/shard_map/pallas_call | solution.py:377
  71.7 3.3 %collective-permute-start.13 = (bf16[544,512]{1,0:T(8,128)(2,1)S(1)}, bf16[544,512]{1,0:T(8,128)(2,1)S(1)}, u32[]{:S(2)}, u32[]{:S(2)}) collective-permute-start(bf16[544,512]{1,0:T(8,128)(2,1)S(1)} %get-tuple-element.62), channel_id=1, source_target_pairs={{0,120},{8,0},{16,8},{24,16},{32,24},{40,32},{48,40},{56,48},{64,5... | collective-permute-start | bytes 1671176 | tf_op jit(solution)/shard_map/ppermute | solution.py:19
  77.1 3.7 %shard_map.71 = (f32[4,256,512]{2,1,0:T(8,128)S(1)}, f32[16,1024]{1,0:T(8,128)S(1)}) custom-call(f32[4,256,512]{2,1,0:T(8,128)S(1)} %get-tuple-element.57.r_0_, f32[4,64,128]{2,1,0:T(8,128)S(1)} %copy-done.2, bf16[16,1024]{1,0:T(8,128)(2,1)S(1)} %get-tuple-element.58.r_2_, bf16[1024,1024]{1,0:T(8,128)(2,1)S(1)} %get-tuple-element.45.r_3_, ...), custom_call_target="tpu_custom_call" | custom-call | flops 1000000000 | bytes 8388608 | tf_op jit(solution)/shard_map/pallas_call | solution.py:360
  80.8 6.1 %collective-permute-done.15.r_5_ = bf16[16,1024]{1,0:T(8,128)(2,1)S(1)} collective-permute-done((bf16[16,1024]{1,0:T(8,128)(2,1)S(1)}, bf16[16,1024]{1,0:T(8,128)(2,1)S(1)}, u32[]{:S(2)}, u32[]{:S(2)}) %collective-permute-start.15) | collective-permute-done | bytes 32800 | tf_op jit(solution)/shard_map/ppermute | solution.py:19
  87.0 2.7 %collective-permute-done.14.r_4_ = bf16[16,1024]{1,0:T(8,128)(2,1)S(1)} collective-permute-done((bf16[16,1024]{1,0:T(8,128)(2,1)S(1)}, bf16[16,1024]{1,0:T(8,128)(2,1)S(1)}, u32[]{:S(2)}, u32[]{:S(2)}) %collective-permute-start.14) | collective-permute-done | bytes 32800 | tf_op jit(solution)/shard_map/ppermute | solution.py:19
  91.7 24.5 %all_to_all.20.r_0_.r_1_ = bf16[8,128,512]{2,1,0:T(8,128)(2,1)S(1)} all-to-all(bf16[8,128,512]{2,1,0:T(8,128)(2,1)S(1)} %bitcast.15), channel_id=1, replica_groups=mesh['dom'=16,'st'=8] {'st'}, dimensions={0} | all-to-all | bytes 2097152 | tf_op jit(solution)/shard_map/all_to_all | solution.py:392
  116.7 13.1 %all_to_all.21 = f32[128,1,128]{2,1,0:T(1,128)S(1)} all-to-all(f32[128,1,128]{2,1,0:T(1,128)S(1)} %bitcast.19), channel_id=1, replica_groups=mesh['dom'=16,'st'=8] {'dom','st'}, dimensions={0} | all-to-all | bytes 131072 | tf_op jit(solution)/shard_map/all_to_all | solution.py:397
  130.0 13.8 %all_to_all.22 = f32[128,1,128]{2,1,0:T(1,128)S(1)} all-to-all(f32[128,1,128]{2,1,0:T(1,128)S(1)} %broadcast_in_dim.2), channel_id=1, replica_groups=mesh['dom'=16,'st'=8] {'dom','st'}, dimensions={0} | all-to-all | bytes 131072 | tf_op jit(solution)/shard_map/all_to_all | solution.py:399
  143.8 7.4 %shard_map.74 = bf16[8,32,16,128]{3,2,1,0:T(8,128)(2,1)S(1)} custom-call(f32[128,128]{1,0:T(8,128)S(1)} %bitcast.18, bf16[8,128,512]{2,1,0:T(8,128)(2,1)S(1)} %all_to_all.20.r_0_.r_1_), custom_call_target="tpu_custom_call" | custom-call | flops 200000000 | bytes 2097152 | tf_op jit(solution)/shard_map/pallas_call | solution.py:400
  151.2 20.6 %all_to_all.23 = bf16[8,32,16,128]{3,2,1,0:T(8,128)(2,1)S(1)} all-to-all(bf16[8,32,16,128]{3,2,1,0:T(8,128)(2,1)S(1)} %shard_map.74), channel_id=1, replica_groups=mesh['dom'=16,'st'=8] {'st'}, dimensions={0} | all-to-all | bytes 2097152 | tf_op jit(solution)/shard_map/all_to_all | solution.py:406
  (44 shorter events, 19.1 us)
Async XLA Ops:
  0.0 11.8 %copy-start = (f32[12288]{0:T(1024)S(1)}, f32[12288]{0:T(1024)}, u32[]{:S(2)}) copy-start(f32[12288]{0:T(1024)} %param.11) | copy-start | bytes 147460
  0.0 2.1 %copy-start.5 = (s32[4,16]{1,0:T(4,128)S(1)}, s32[4,16]{1,0:T(4,128)}, u32[]{:S(2)}) copy-start(s32[4,16]{1,0:T(4,128)} %r_3_.1) | copy-start | bytes 772
  0.0 2.1 %copy-start.1 = (f32[4,16,16,512]{3,2,1,0:T(8,128)S(1)}, f32[4,16,16,512]{3,2,1,0:T(8,128)}, u32[]{:S(2)}) copy-start(f32[4,16,16,512]{3,2,1,0:T(8,128)} %param.8) | copy-start | bytes 6291460
  2.1 0.8 copy-start.3
  2.8 8.8 %copy-start.4 = (s32[4,16,16]{2,1,0:T(8,128)S(1)}, s32[4,16,16]{2,1,0:T(8,128)}, u32[]{:S(2)}) copy-start(s32[4,16,16]{2,1,0:T(8,128)} %r_2_.1) | copy-start | bytes 12292
  5.7 20.9 %collective-permute-start = (bf16[576,512]{1,0:T(8,128)(2,1)}, bf16[576,512]{1,0:T(8,128)(2,1)S(1)}, u32[]{:S(2)}, u32[]{:S(2)}) collective-permute-start(bf16[576,512]{1,0:T(8,128)(2,1)} %get-tuple-element.39), channel_id=1, source_target_pairs={{0,8},{8,16},{16,24},{24,32},{32,40},{40,48},{48,56},{56,64},{64,7... | collective-permute-start | bytes 1769480 | tf_op jit(solution)/shard_map/ppermute | solution.py:19
  5.8 20.9 %collective-permute-start.1 = (bf16[576,512]{1,0:T(8,128)(2,1)}, bf16[576,512]{1,0:T(8,128)(2,1)S(1)}, u32[]{:S(2)}, u32[]{:S(2)}) collective-permute-start(bf16[576,512]{1,0:T(8,128)(2,1)} %get-tuple-element.40), channel_id=1, source_target_pairs={{0,120},{8,0},{16,8},{24,16},{32,24},{40,32},{48,40},{56,48},{64,5... | collective-permute-start | bytes 1769480 | tf_op jit(solution)/shard_map/ppermute | solution.py:19
  9.6 15.2 %collective-permute-start.3 = (bf16[32,1024]{1,0:T(8,128)(2,1)}, bf16[32,1024]{1,0:T(8,128)(2,1)S(1)}, u32[]{:S(2)}, u32[]{:S(2)}) collective-permute-start(bf16[32,1024]{1,0:T(8,128)(2,1)} %get-tuple-element.35.r_2_), channel_id=1, source_target_pairs={{0,112},{8,120},{16,0},{24,8},{32,16},{40,24},{48,32},{56,40},{64,... | collective-permute-start | bytes 196616 | tf_op jit(solution)/shard_map/ppermute | solution.py:19
  11.5 15.1 %collective-permute-start.2 = (bf16[32,1024]{1,0:T(8,128)(2,1)}, bf16[32,1024]{1,0:T(8,128)(2,1)}, u32[]{:S(2)}, u32[]{:S(2)}) collective-permute-start(bf16[32,1024]{1,0:T(8,128)(2,1)} %get-tuple-element.35.r_2_), channel_id=1, source_target_pairs={{0,16},{8,24},{16,32},{24,40},{32,48},{40,56},{48,64},{56,72},{64,... | collective-permute-start | bytes 196616 | tf_op jit(solution)/shard_map/ppermute | solution.py:19
  11.8 6.2 %copy-start.2 = (f32[4,64,128]{2,1,0:T(8,128)S(1)}, f32[4,64,128]{2,1,0:T(8,128)}, u32[]{:S(2)}) copy-start(f32[4,64,128]{2,1,0:T(8,128)} %r_1_.7) | copy-start | bytes 393220
  31.4 18.5 %collective-permute-start.4 = (bf16[544,512]{1,0:T(8,128)(2,1)S(1)}, bf16[544,512]{1,0:T(8,128)(2,1)S(1)}, u32[]{:S(2)}, u32[]{:S(2)}) collective-permute-start(bf16[544,512]{1,0:T(8,128)(2,1)S(1)} %get-tuple-element.48), channel_id=1, source_target_pairs={{0,8},{8,16},{16,24},{24,32},{32,40},{40,48},{48,56},{56,64},{64,7... | collective-permute-start | bytes 1671176 | tf_op jit(solution)/shard_map/ppermute | solution.py:19
  31.5 18.4 %collective-permute-start.5 = (bf16[544,512]{1,0:T(8,128)(2,1)S(1)}, bf16[544,512]{1,0:T(8,128)(2,1)S(1)}, u32[]{:S(2)}, u32[]{:S(2)}) collective-permute-start(bf16[544,512]{1,0:T(8,128)(2,1)S(1)} %get-tuple-element.49), channel_id=1, source_target_pairs={{0,120},{8,0},{16,8},{24,16},{32,24},{40,32},{48,40},{56,48},{64,5... | collective-permute-start | bytes 1671176 | tf_op jit(solution)/shard_map/ppermute | solution.py:19
  35.3 11.7 %collective-permute-start.7 = (bf16[16,1024]{1,0:T(8,128)(2,1)S(1)}, bf16[16,1024]{1,0:T(8,128)(2,1)S(1)}, u32[]{:S(2)}, u32[]{:S(2)}) collective-permute-start(bf16[16,1024]{1,0:T(8,128)(2,1)S(1)} %get-tuple-element.44.r_2_), channel_id=1, source_target_pairs={{0,112},{8,120},{16,0},{24,8},{32,16},{40,24},{48,32},{56,40},{64,... | collective-permute-start | bytes 98312 | tf_op jit(solution)/shard_map/ppermute | solution.py:19
  35.3 14.6 %collective-permute-start.6 = (bf16[16,1024]{1,0:T(8,128)(2,1)S(1)}, bf16[16,1024]{1,0:T(8,128)(2,1)S(1)}, u32[]{:S(2)}, u32[]{:S(2)}) collective-permute-start(bf16[16,1024]{1,0:T(8,128)(2,1)S(1)} %get-tuple-element.44.r_2_), channel_id=1, source_target_pairs={{0,16},{8,24},{16,32},{24,40},{32,48},{40,56},{48,64},{56,72},{64,... | collective-permute-start | bytes 98312 | tf_op jit(solution)/shard_map/ppermute | solution.py:19
  52.4 16.2 %collective-permute-start.8 = (bf16[544,512]{1,0:T(8,128)(2,1)S(1)}, bf16[544,512]{1,0:T(8,128)(2,1)S(1)}, u32[]{:S(2)}, u32[]{:S(2)}) collective-permute-start(bf16[544,512]{1,0:T(8,128)(2,1)S(1)} %get-tuple-element.55), channel_id=1, source_target_pairs={{0,8},{8,16},{16,24},{24,32},{32,40},{40,48},{48,56},{56,64},{64,7... | collective-permute-start | bytes 1671176 | tf_op jit(solution)/shard_map/ppermute | solution.py:19
  52.5 16.1 %collective-permute-start.9 = (bf16[544,512]{1,0:T(8,128)(2,1)S(1)}, bf16[544,512]{1,0:T(8,128)(2,1)S(1)}, u32[]{:S(2)}, u32[]{:S(2)}) collective-permute-start(bf16[544,512]{1,0:T(8,128)(2,1)S(1)} %get-tuple-element.56), channel_id=1, source_target_pairs={{0,120},{8,0},{16,8},{24,16},{32,24},{40,32},{48,40},{56,48},{64,5... | collective-permute-start | bytes 1671176 | tf_op jit(solution)/shard_map/ppermute | solution.py:19
  56.3 10.8 %collective-permute-start.11 = (bf16[16,1024]{1,0:T(8,128)(2,1)S(1)}, bf16[16,1024]{1,0:T(8,128)(2,1)S(1)}, u32[]{:S(2)}, u32[]{:S(2)}) collective-permute-start(bf16[16,1024]{1,0:T(8,128)(2,1)S(1)} %get-tuple-element.52.r_2_), channel_id=1, source_target_pairs={{0,112},{8,120},{16,0},{24,8},{32,16},{40,24},{48,32},{56,40},{64,... | collective-permute-start | bytes 98312 | tf_op jit(solution)/shard_map/ppermute | solution.py:19
  56.3 11.3 %collective-permute-start.10 = (bf16[16,1024]{1,0:T(8,128)(2,1)S(1)}, bf16[16,1024]{1,0:T(8,128)(2,1)S(1)}, u32[]{:S(2)}, u32[]{:S(2)}) collective-permute-start(bf16[16,1024]{1,0:T(8,128)(2,1)S(1)} %get-tuple-element.52.r_2_), channel_id=1, source_target_pairs={{0,16},{8,24},{16,32},{24,40},{32,48},{40,56},{48,64},{56,72},{64,... | collective-permute-start | bytes 98312 | tf_op jit(solution)/shard_map/ppermute | solution.py:19
  71.1 18.5 %collective-permute-start.12 = (bf16[544,512]{1,0:T(8,128)(2,1)S(1)}, bf16[544,512]{1,0:T(8,128)(2,1)S(1)}, u32[]{:S(2)}, u32[]{:S(2)}) collective-permute-start(bf16[544,512]{1,0:T(8,128)(2,1)S(1)} %get-tuple-element.61), channel_id=1, source_target_pairs={{0,8},{8,16},{16,24},{24,32},{32,40},{40,48},{48,56},{56,64},{64,7... | collective-permute-start | bytes 1671176 | tf_op jit(solution)/shard_map/ppermute | solution.py:19
  71.7 17.9 %collective-permute-start.13 = (bf16[544,512]{1,0:T(8,128)(2,1)S(1)}, bf16[544,512]{1,0:T(8,128)(2,1)S(1)}, u32[]{:S(2)}, u32[]{:S(2)}) collective-permute-start(bf16[544,512]{1,0:T(8,128)(2,1)S(1)} %get-tuple-element.62), channel_id=1, source_target_pairs={{0,120},{8,0},{16,8},{24,16},{32,24},{40,32},{48,40},{56,48},{64,5... | collective-permute-start | bytes 1671176 | tf_op jit(solution)/shard_map/ppermute | solution.py:19
  75.1 11.9 %collective-permute-start.15 = (bf16[16,1024]{1,0:T(8,128)(2,1)S(1)}, bf16[16,1024]{1,0:T(8,128)(2,1)S(1)}, u32[]{:S(2)}, u32[]{:S(2)}) collective-permute-start(bf16[16,1024]{1,0:T(8,128)(2,1)S(1)} %get-tuple-element.58.r_2_), channel_id=1, source_target_pairs={{0,112},{8,120},{16,0},{24,8},{32,16},{40,24},{48,32},{56,40},{64,... | collective-permute-start | bytes 98312 | tf_op jit(solution)/shard_map/ppermute | solution.py:19
  75.1 14.6 %collective-permute-start.14 = (bf16[16,1024]{1,0:T(8,128)(2,1)S(1)}, bf16[16,1024]{1,0:T(8,128)(2,1)S(1)}, u32[]{:S(2)}, u32[]{:S(2)}) collective-permute-start(bf16[16,1024]{1,0:T(8,128)(2,1)S(1)} %get-tuple-element.58.r_2_), channel_id=1, source_target_pairs={{0,16},{8,24},{16,32},{24,40},{32,48},{40,56},{48,64},{56,72},{64,... | collective-permute-start | bytes 98312 | tf_op jit(solution)/shard_map/ppermute | solution.py:19

commit v3 on v2

v3 whole, which is shorter than its diff:
```python
import jax
import jax.numpy as jnp
from jax import lax
from jax.experimental import pallas as pl
from jax.experimental.pallas import tpu as pltpu
from jax.sharding import Mesh, PartitionSpec as P

center = 8.25
half_width = 7.75

F32 = jnp.float32
BF16 = jnp.bfloat16
NT = (((1,), (1,)), ((), ()))
NN = (((1,), (0,)), ((), ()))
CORES = 2
NO_NAME = 255.0 * 128.0


def passed_along(array, axis, by):
    devices = lax.axis_size(axis)
    return lax.ppermute(array, axis, [(i, (i + by) % devices) for i in range(devices)])


def call(kernel, out_shape, scratch=(), vmem=20, flops=0, nbytes=0, **specs):
    return pl.pallas_call(
        kernel,
        out_shape=out_shape,
        **specs,
        scratch_shapes=list(scratch),
        compiler_params=pltpu.CompilerParams(vmem_limit_bytes=vmem * 2**20),
        cost_estimate=pl.CostEstimate(flops=int(flops), bytes_accessed=int(nbytes), transcendentals=0),
    )


def rows_at(t, states, base=0):
    return pl.ds(pl.multiple_of(base + t * states, states), states)


def lane(y):
    return slice(y * 128, (y + 1) * 128)


def block_mask(rows, cols, row_block, col_block):
    row = lax.broadcasted_iota(jnp.int32, (rows, cols), 0) // row_block
    col = lax.broadcasted_iota(jnp.int32, (rows, cols), 1) // col_block
    return row == col


def project(field, proj, states, slots):
    both = lax.dot_general(field, proj, NT, preferred_element_type=F32)
    both = jnp.where(block_mask(*both.shape, states, slots), both, 0.0)
    return jnp.sum(both.reshape(-1, states, both.shape[1]), axis=0)


def folded(terms):
    half = terms.shape[1] // 2
    return jnp.concatenate([terms[:, :half], terms[:, half:]], axis=0).astype(BF16)


def unfolded(block):
    block = block.astype(F32)
    states = block.shape[0] // 2
    return jnp.concatenate([block[:states], block[states:]], axis=1)


def write_terms(message, base, block):
    high, width = block.shape[0], message.shape[1]
    for i in range(block.shape[1] // width):
        message[base + i * high : base + (i + 1) * high, :] = block[:, i * width : (i + 1) * width]


def read_terms(message, base, states, count):
    width, high = message.shape[1], 2 * states
    parts = [message[base + i * high : base + (i + 1) * high, :] for i in range(count // high * states // width)]
    return unfolded(jnp.concatenate(parts, axis=1))


def read_names(message, base, count):
    width = message.shape[1]
    digits = message[base : base + 16, :].astype(F32)
    parts = count // width
    names = [digits[i : i + 1] * 128.0 + digits[parts + i : parts + i + 1] for i in range(parts)]
    return jnp.concatenate(names, axis=1)


def halves_kernel(core, cells, mine, theirs):
    planes, height, width = mine.shape
    rows = width // 128
    first = core[0] == 0
    for z in range(planes):
        for pair in range(height // 16):
            for y in range(rows):
                one = cells[z, 2 * rows * pair + y].astype(F32)
                two = cells[z, 2 * rows * pair + rows + y].astype(F32)
                lower = jnp.concatenate([one[:8], two[:8]], axis=0)
                upper = jnp.concatenate([one[8:], two[8:]], axis=0)
                at = slice(pair * 16, pair * 16 + 16)
                mine[z, at, lane(y)] = jnp.where(first, lower, upper).astype(BF16)
                theirs[z, at, lane(y)] = jnp.where(first, upper, lower).astype(BF16)


def spread_rows(digits, rows_of):
    tiles, slots = digits.shape
    cols = tiles * slots
    to = lax.broadcasted_iota(jnp.int32, (slots, cols), 1) % slots
    pick = jnp.where(lax.broadcasted_iota(jnp.int32, (slots, cols), 0) == to, 1.0, 0.0)
    wide = lax.dot_general(digits.astype(BF16), pick.astype(BF16), NN, preferred_element_type=F32)
    return jnp.sum(jnp.where(rows_of, wide, 0.0), axis=0, keepdims=True)


def first_kernel(sizes, core, *refs):
    states, slots, rows = sizes
    ours, others = refs[0:5], refs[5:10]
    field, proj, potential, names, partial, low, high = refs[10:]
    planes, height, width = field.shape
    half, cols, tiles = planes // 2, proj.shape[1], height // states
    rows_of = block_mask(tiles, cols, 1, slots)
    diagonal = block_mask(tiles, tiles, 1, 1)
    slot = (lax.broadcasted_iota(jnp.int32, (1, cols), 1) % slots).astype(F32)
    digits = []
    for (cells, proj_of, names_of, counts, potential_of), own in ((ours, True), (others, False)):
        start = core[0] * half if own else (1 - core[0]) * half
        found = []
        for z in range(half):
            field[start + z] = cells[z].astype(F32)
            proj[start + z] = proj_of[z]
            potential[start + z] = potential_of[z]
            name = names_of[z].astype(F32)
            top = jnp.floor(name * (1.0 / 128.0))
            count = jnp.broadcast_to(counts[z : z + 1, :].astype(F32), (tiles, tiles))
            count = jnp.sum(jnp.where(diagonal, count, 0.0), axis=1, keepdims=True)
            count = jnp.sum(jnp.where(rows_of, count, 0.0), axis=0, keepdims=True)
            is_used = slot < count
            found.append(jnp.where(is_used, spread_rows(top, rows_of), NO_NAME / 128.0))
            found.append(jnp.where(is_used, spread_rows(name - 128.0 * top, rows_of), 0.0))
        digits.append([jnp.concatenate(found[i::2], axis=1) for i in (0, 1)])
    first = core[0] == 0
    top, bottom = (
        jnp.concatenate([jnp.where(first, a, b), jnp.where(first, b, a)], axis=1)
        for a, b in zip(digits[0], digits[1])
    )
    named = top * 128.0 + bottom
    names[...] = named
    used = jnp.where(named < NO_NAME, 1.0, 0.0)
    terms = []
    for z in range(planes):
        plane = field[z].astype(BF16)
        at = slice(z * cols, (z + 1) * cols)
        terms.append(project(plane, proj[z], states, slots) * used[:, at])
        if z < 2:
            low[z * height : (z + 1) * height, :] = plane
        if z >= planes - 2:
            high[(z - planes + 2) * height : (z - planes + 3) * height, :] = plane
    block = folded(jnp.concatenate(terms, axis=1))
    partial[...] = block
    parts = named.shape[1] // width
    lines = [v[:, i * width : (i + 1) * width] for v in (top, bottom) for i in range(parts)]
    lines = jnp.concatenate(lines + [jnp.zeros((16 - 2 * parts, width), F32)], axis=0).astype(BF16)
    for message in (low, high):
        write_terms(message, 2 * height, block)
        message[2 * height + 4 * states : 2 * height + 4 * states + 16, :] = lines


def same_names(names, own, store, wanted):
    for q in range(0, names.shape[1], 128):
        column = jnp.broadcast_to(names[:, q : q + 128], (128, 128)).T
        for p in range(0, own.shape[1], 128):
            if wanted(q, p):
                store(q, p, jnp.where(column == own[:, p : p + 128], 1.0, 0.0).astype(BF16))


def doubled(terms):
    return jnp.concatenate([terms, terms], axis=0).astype(BF16)


def look_up(strength, names):
    top = jnp.floor(names * (1.0 / 128.0))
    bottom = names - 128.0 * top
    lines, count = strength.shape[0], names.shape[1]
    line = lax.broadcasted_iota(jnp.int32, (lines, count), 0).astype(F32)
    pick = jnp.where(line == top, 1.0, 0.0)
    of_line = lax.dot_general(
        strength, pick, (((0,), (0,)), ((), ())), precision=lax.Precision.HIGHEST, preferred_element_type=F32
    )
    place = lax.broadcasted_iota(jnp.int32, (128, count), 0).astype(F32)
    return jnp.sum(jnp.where(place == bottom, of_line, 0.0), axis=0, keepdims=True)


def local_kernel(sizes, first, *refs):
    states, slots, rows = sizes
    refs = list(refs)
    cur, potential, own = refs[:3]
    rest = refs[3:]
    if first:
        names, strength, base, share, table, weight = rest
        named = names[...]
        mine = jnp.where(named < NO_NAME, named, -1.0)

        def store(q, p, same):
            table[q : q + 128, p : p + 128] = same

        same_names(named, mine, store, lambda q, p: True)
        weight[...] = look_up(strength[...], named)
    else:
        table, prev, base, share = rest
    planes, height, width = cur.shape
    tiles = height // states
    gain = (1.0 if first else 2.0) / half_width
    near, far = -gain * 2.0 / 3.0, gain / 24.0
    terms = doubled(unfolded(own[...]))
    share[...] = lax.dot_general(terms, table[...], NN, preferred_element_type=F32)[:states]

    def tile_step(j, carry):
        here = rows_at(j, states)
        left, right = rows_at((j + tiles - 1) % tiles, states), rows_at((j + 1) % tiles, states)

        def load(z, y):
            if y < 0:
                return cur[z, left, lane(y + rows)]
            if y >= rows:
                return cur[z, right, lane(y - rows)]
            return cur[z, here, lane(y)]

        for y in range(rows):
            mids = [load(z, y) for z in range(planes)]
            for z in range(planes):
                mid = mids[z]
                one = load(z, y - 1) + load(z, y + 1)
                two = load(z, y - 2) + load(z, y + 2)
                one += pltpu.roll(mid, 1, 1) + pltpu.roll(mid, 127, 1)
                two += pltpu.roll(mid, 2, 1) + pltpu.roll(mid, 126, 1)
                for by in (-1, 1):
                    if 0 <= z + by < planes:
                        one += mids[z + by]
                    if 0 <= z + 2 * by < planes:
                        two += mids[z + 2 * by]
                shift = potential[z, pl.ds(j * rows + y, 1), :] + (3.75 - center)
                new = near * one + far * two + shift * mid * gain
                if not first:
                    new = new - prev[z, here, lane(y)]
                base[z, here, lane(y)] = new
        return carry

    lax.fori_loop(0, tiles, tile_step, 0)


def step_kernel(sizes, first, last, *refs):
    states, slots, rows = sizes
    refs = list(refs)
    base, share, below, above, weight, names, proj = refs[:7]
    rest = refs[7:]
    planes, height, width = base.shape
    tiles = height // states
    cols = proj.shape[1]
    count = planes * cols
    reach = (planes + 1) * cols
    gain = (1.0 if first else 2.0) / half_width
    near, far = -gain * 2.0 / 3.0, gain / 24.0
    table = rest.pop(0)
    if last:
        (nxt, applied) = rest
    else:
        (nxt, low, high, partial, applied, rounded) = rest

    named = names[...]
    if first:
        around = [read_names(r, 2 * height + 4 * states, count) for r in (below, above)]
        mine = jnp.where(named < NO_NAME, named, -1.0)

        def store(q, p, same):
            z = p // cols
            table[z, q - z * cols : q - z * cols + 128, p - z * cols : p - z * cols + 128] = same

        def wanted(q, p):
            return 0 <= q // cols - p // cols <= planes

        same_names(jnp.concatenate(around, axis=1), mine, store, wanted)

    terms = [read_terms(r, 2 * height, states, count) for r in (below, above)]
    terms = doubled(jnp.concatenate(terms, axis=1))
    mask = block_mask(height, cols, states, slots)
    for z in range(planes):
        at = slice(z * cols, (z + 1) * cols)
        chosen = lax.dot_general(terms[:, z * cols : z * cols + reach], table[z], NN, preferred_element_type=F32)
        chosen = (chosen[:states] + share[:, at]) * (weight[:, at] * gain)
        spread = jnp.broadcast_to(chosen[None], (tiles, states, cols)).reshape(height, cols)
        spread = jnp.where(mask, spread, 0.0).astype(BF16)
        applied[z] = lax.dot_general(spread, proj[z], NN, preferred_element_type=F32)

    def pair_step(pair, carry):
        here = rows_at(pair, 2 * states)
        for y in range(rows):
            b2, b1 = [below[rows_at(pair, 2 * states, z * height), lane(y)].astype(F32) for z in range(2)]
            a1, a2 = [above[rows_at(pair, 2 * states, z * height), lane(y)].astype(F32) for z in range(2)]
            outer = {0: near * b1 + far * b2, 1: far * b1}
            outer.update({planes - 2: far * a1, planes - 1: near * a1 + far * a2})
            for z in range(planes):
                new = base[z, here, lane(y)] + applied[z, here, lane(y)]
                if z in outer:
                    new += outer[z]
                if last:
                    pairs = nxt.shape[1] // (2 * states)
                    parts = tiles // 2 // pairs
                    slab, plane = divmod(z, planes // CORES)
                    block = (plane * parts + pair // pairs) * CORES + slab
                    nxt[block, rows_at(pair % pairs, 2 * states), lane(y)] = new.astype(BF16)
                else:
                    nxt[z, here, lane(y)] = new
                    rounded[z, here, lane(y)] = new.astype(BF16)
        return carry

    lax.fori_loop(0, tiles // 2, pair_step, 0)
    if not last:
        used = jnp.where(named < NO_NAME, 1.0, 0.0)
        out = []
        for z in range(planes):
            at = slice(z * cols, (z + 1) * cols)
            out.append(project(rounded[z], proj[z], states, slots) * used[:, at])
            if z < 2:
                low[z * height : (z + 1) * height, :] = rounded[z]
            if z >= planes - 2:
                high[(z - planes + 2) * height : (z - planes + 3) * height, :] = rounded[z]
        block = folded(jnp.concatenate(out, axis=1))
        partial[...] = block
        write_terms(low, 2 * height, block)
        write_terms(high, 2 * height, block)


def gram_kernel(states, cells, margin, ordered):
    sources, height, width = cells.shape
    total = jnp.zeros(margin.shape, F32)
    for pair in range(height // (2 * states)):
        both = cells[:, pair * 2 * states : (pair + 1) * 2 * states, :].astype(F32)
        for i in range(2):
            block = both[:, i * states : (i + 1) * states, :].reshape(sources * states, width).astype(BF16)
            ordered[2 * pair + i] = block
            total += lax.dot_general(block, block, NT, preferred_element_type=F32)
    margin[...] = total


def recip(x):
    r = pltpu.reciprocal(x, approx=True)
    r = r * (2.0 - x * r)
    return r * (2.0 - x * r)

def inverse_factor(margin, inverse):
    n = margin.shape[0]
    lanes = lax.broadcasted_iota(jnp.int32, (8, n), 1)
    subs = lax.broadcasted_iota(jnp.int32, (8, n), 0)
    eye = lax.broadcasted_iota(jnp.int32, (n, n), 0) == lax.broadcasted_iota(jnp.int32, (n, n), 1)
    full = margin[...]
    diagonal = jnp.where(eye, full, 0.0)
    across = lax.rsqrt(jnp.sum(diagonal, axis=0, keepdims=True))
    down = lax.rsqrt(jnp.sum(diagonal, axis=1, keepdims=True))
    full = full * down * across
    work = [full[8 * i : 8 * i + 8, :] for i in range(n // 8)]
    for k in range(0, n, 4):
        b, r = divmod(k, 8)
        rows = [work[b][r + p : r + p + 1, :] for p in range(4)]
        cols = [[jnp.broadcast_to(work[i][:, k + p : k + p + 1], (8, n)) for p in range(4)] for i in range(b, n // 8)]
        entry = lambda p, q: jnp.broadcast_to(cols[0][q][r + p : r + p + 1, :], (8, n))
        s = {(p, q): entry(p, q) for p in range(4) for q in range(p + 1)}
        rows = [jnp.where(lanes == k + p, 1.0, jnp.where((lanes >= k) & (lanes < k + 4), 0.0, jnp.broadcast_to(rows[p], (8, n)))) for p in range(4)]
        a, bb, c = s[0, 0], s[1, 0], s[1, 1]
        det = recip(a * c - bb * bb)
        i00, i01, i11 = c * det, -bb * det, a * det
        x = {}
        for q in (2, 3):
            x[0, q] = i00 * s[q, 0] + i01 * s[q, 1]
            x[1, q] = i01 * s[q, 0] + i11 * s[q, 1]
        g22 = s[2, 2] - (s[2, 0] * x[0, 2] + s[2, 1] * x[1, 2])
        g32 = s[3, 2] - (s[3, 0] * x[0, 2] + s[3, 1] * x[1, 2])
        g33 = s[3, 3] - (s[3, 0] * x[0, 3] + s[3, 1] * x[1, 3])
        det2 = recip(g22 * g33 - g32 * g32)
        h00, h01, h11 = g33 * det2, -g32 * det2, g22 * det2
        low2 = rows[2] - (x[0, 2] * rows[0] + x[1, 2] * rows[1])
        low3 = rows[3] - (x[0, 3] * rows[0] + x[1, 3] * rows[1])
        y2 = h00 * low2 + h01 * low3
        y3 = h01 * low2 + h11 * low3
        y0 = i00 * rows[0] + i01 * rows[1] - (x[0, 2] * y2 + x[0, 3] * y3)
        y1 = i01 * rows[0] + i11 * rows[1] - (x[1, 2] * y2 + x[1, 3] * y3)
        inside = (lanes >= k) & (lanes < k + 4)
        for i in range(b, n // 8):
            c4 = cols[i - b]
            if i == b and r == 0:
                c4 = [jnp.where(subs >= 4, v, 0.0) for v in c4]
            elif i == b:
                continue
            change = (c4[0] * y0 + c4[1] * y1) + (c4[2] * y2 + c4[3] * y3)
            work[i] = jnp.where(inside, 0.0, work[i]) - change
        ra = recip(a)
        l10 = bb * ra
        d1 = c - bb * l10
        rg = recip(g22)
        l32 = g32 * rg
        d3 = g33 - g32 * l32
        out = [rows[0] * lax.rsqrt(a), (rows[1] - l10 * rows[0]) * lax.rsqrt(d1), low2 * lax.rsqrt(g22), (low3 - l32 * low2) * lax.rsqrt(d3)]
        for p in range(4):
            inverse[k + p : k + p + 1, :] = (jnp.where(lanes <= k + p, out[p], 0.0) * across)[0:1]

def rotate_kernel(margin, ordered, rotated, inverse):
    inverse_factor(margin, inverse)
    mine = inverse[...].astype(BF16)
    groups, _, states, _ = rotated.shape
    tiles, nstates, width = ordered.shape
    rows = width // 128
    for j in range(tiles):
        new = lax.dot_general(mine, ordered[j], NN, preferred_element_type=F32).astype(BF16)
        new = new.reshape(groups, states, width)
        for y in range(rows):
            rotated[:, j * rows + y, :, :] = new[:, :, lane(y)]


def per_device(states, potential, proj_values, block_list, tile_count, strength):
    local_states, slab_planes, rows_y, cells_x = states.shape
    _, tiles, slots, tile_cells = proj_values.shape
    rows = rows_y // tiles
    ring, groups = lax.axis_size("ring"), lax.axis_size("st")
    total_cells = slab_planes * rows_y * cells_x * ring * CORES
    share_states, planes = local_states // CORES, slab_planes * CORES
    height, cols, count = tiles * share_states, tiles * slots, planes * tiles * slots
    sizes = (share_states, slots, rows)
    shape = (planes, height, tile_cells)

    f32 = lambda s: jax.ShapeDtypeStruct(s, F32)
    bf16 = lambda s: jax.ShapeDtypeStruct(s, BF16)
    whole, scalar = pl.BlockSpec(), pl.BlockSpec(memory_space=pltpu.SMEM)

    def swapped(array):
        return lax.ppermute(array, "core", [(0, 1), (1, 0)])

    core = lax.axis_index("core").astype(jnp.int32).reshape(1)
    proj_own = proj_values.reshape(slab_planes, cols, tile_cells).astype(BF16)
    ours = [proj_own, block_list, tile_count, potential]
    others = [swapped(array) for array in ours]
    piece = bf16((slab_planes, height, tile_cells))
    mine, theirs = call(
        halves_kernel, (piece, piece), in_specs=[scalar, whole], flops=10**7, nbytes=2 * 2**20
    )(core, states.transpose(1, 2, 0, 3))
    got = swapped(theirs)

    def sent(names):
        message = (2 * height + 4 * share_states + (16 if names else 0), tile_cells)
        return [bf16((2 * share_states, count // 2)), bf16(message), bf16(message)]

    field, proj, shift, names, partial, low, high = call(
        lambda *r: first_kernel(sizes, *r),
        [f32(shape), bf16((planes, cols, tile_cells)), f32((planes, rows_y, cells_x)), f32((1, count))] + sent(True),
        in_specs=[scalar] + [whole] * 10,
        flops=10**9, nbytes=8 * 2**20,
    )(core, mine, *ours, got, *others)

    prev, cur = None, field
    for m in range(4):
        first, last = m == 0, m == 3
        below = passed_along(high, "ring", 1)
        above = passed_along(low, "ring", -1)
        outs = [f32(shape), f32((share_states, count))]
        args = [cur, shift, partial]
        args += [names, strength.reshape(-1, 128)] if first else [own_table, prev]
        got = call(
            lambda *r, first=first: local_kernel(sizes, first, *r),
            outs + ([bf16((count, count)), f32((1, count))] if first else []),
            flops=1e9, nbytes=8 * 2**20,
        )(*args)
        if first:
            base, share, own_table, weight = got
        else:
            base, share = got
        args = [base, share, below, above, weight, names, proj] + ([] if first else [table])
        outs = [bf16((planes, (planes + 1) * cols, cols))] if first else []
        scratch = [pltpu.VMEM(shape, F32)]
        if last:
            outs += [bf16((CORES * groups, planes * height // (CORES * groups), tile_cells))]
        else:
            made = sent(False)
            outs += [f32(shape), made[1], made[2], made[0]]
            scratch += [pltpu.VMEM(shape, BF16)]
        got = call(
            lambda *r, first=first, last=last: step_kernel(sizes, first, last, *r),
            outs, scratch=scratch, flops=1e9, nbytes=8 * 2**20,
        )(*args)
        if first:
            table, *got = got
        if last:
            (filtered,) = got
        else:
            prev = cur
            cur, low, high, partial = got

    cells = lax.all_to_all(filtered, ("st", "core"), 0, 0, tiled=True)
    nstates = groups * local_states
    own_tiles = cells.shape[1] // share_states
    part, ordered = call(
        lambda *r: gram_kernel(share_states, *r),
        (f32((nstates, nstates)), bf16((own_tiles, nstates, tile_cells))),
        flops=1e8, nbytes=2**20,
    )(cells)
    everywhere = ("ring", "core", "st")
    devices = ring * CORES * groups
    per = nstates // devices
    total = lax.all_to_all(part.reshape(devices, per, nstates), everywhere, 0, 0, tiled=True)
    total = jnp.sum(total, axis=0, keepdims=True) / total_cells
    margin = lax.all_to_all(jnp.broadcast_to(total, (devices, per, nstates)), everywhere, 0, 0, tiled=True)
    rotated = call(
        rotate_kernel,
        bf16((groups, slab_planes * rows_y // groups, local_states, cells_x)),
        scratch=[pltpu.VMEM((nstates, nstates), F32)],
        flops=2e8, nbytes=2**21,
    )(margin.reshape(nstates, nstates), ordered)
    rotated = lax.all_to_all(rotated, "st", 0, 0, tiled=True)
    return rotated.reshape(slab_planes, rows_y, local_states, cells_x).transpose(2, 0, 1, 3)


def solution(mesh):
    fine = Mesh(mesh.devices.reshape(-1, CORES, mesh.shape["st"]), ("ring", "core", "st"))
    dom = ("ring", "core")
    return jax.shard_map(
        per_device,
        mesh=fine,
        in_specs=(
            P("st", dom, None, None),
            P(dom, None, None),
            P(dom, None, None, None),
            P(dom, None, None),
            P(dom, None),
            P(),
        ),
        out_specs=P("st", dom, None, None),
        check_vma=False,
    )
```

time: 173 us -> 166 us (0.960)
  local copies, waits for them, and re-layouts: 10.3 us -> 1.99 us
  Pallas kernels: 37.6 us -> 45.6 us
  starting transfers between devices: 23.8 us -> 18.1 us
  waiting for transfers between devices: 28.8 us -> 24.2 us
  other arithmetic: 0.17 us -> 1.99 us
  blocking collectives: 72.1 us -> 73.9 us
    ppermute x16 -> x8, starting transfers between devices: 23.8 us -> 16.8 us  [passed_along(): lax.ppermute(array, axis, [(i, (i + by) % devices) for i in range(devices)])]
    ppermute x16 -> x8, waiting for transfers between devices: 28.8 us -> 22.7 us  [passed_along(): lax.ppermute(array, axis, [(i, (i + by) % devices) for i in range(devices)])]
    gather x1 -> x0, local copies, waits for them, and re-layouts: 6.15 us -> none  [per_device(): weight = strength[block_list.reshape(-1)].reshape(1, count)]
    pallas_call x4, Pallas kernels: 15.2 us -> 20.9 us  [per_device(): call(lambda *r, first=first: local_kernel(sizes, first, *r), outs + ([bf1...]
    pallas_call x4, Pallas kernels: 11.8 us -> 15.6 us  [per_device(): call(lambda *r, first=first, last=last: step_kernel(sizes, first, last, *...]
    unnamed x13 -> x11, local copies, waits for them, and re-layouts: 2.83 us -> 0.71 us
    convert_element_type x0 -> x1, other arithmetic: none -> 1.84 us  [per_device(): proj_own = proj_values.reshape(slab_planes, cols, tile_cells).astype(BF16)]
    all_to_all x3, blocking collectives: 51.5 us -> 53.3 us  [the longest x1 24.9 us: per_device(): cells = lax.all_to_all(filtered, ('st', 'core'), 0, 0, tiled=True)]
  transfers between devices with their start and end apart: 16 -> 13, of which waited for: 9 -> 9; matrix products, arithmetic and copies ran while one was open for 4% -> 0% of each run, Pallas kernels for 9% -> 13%
where the time goes in v3:
time: 166 us
  blocking collectives  73.9 us (45%)
  Pallas kernels  45.6 us (27%)
  waiting for transfers between devices  24.2 us (15%)
  starting transfers between devices  18.1 us (11%)
  local copies, waits for them, and re-layouts  1.99 us (1%)
  other arithmetic  1.99 us (1%)
    all_to_all x1, blocking collectives, per_device(): cells = lax.all_to_all(filtered, ('st', 'core'), 0, 0, tiled=True)  24.9 us
    ppermute x8, waiting for transfers between devices, passed_along(): lax.ppermute(array, axis, [(i, (i + by) % devices) for i in range(devices)])  22.7 us
    pallas_call x4, Pallas kernels, per_device(): call(lambda *r, first=first: local_kernel(sizes, first, *r), outs + ([bf1...  20.9 us
    all_to_all x1, blocking collectives, per_device(): rotated = lax.all_to_all(rotated, 'st', 0, 0, tiled=True)  20.6 us
    ppermute x8, starting transfers between devices, passed_along(): lax.ppermute(array, axis, [(i, (i + by) % devices) for i in range(devices)])  16.8 us
    pallas_call x4, Pallas kernels, per_device(): call(lambda *r, first=first, last=last: step_kernel(sizes, first, last, *...  15.6 us
    all_to_all x1, blocking collectives, per_device(): lax.all_to_all(part.reshape(devices, per, nstates), everywhere, 0, 0, til...  14.5 us
    all_to_all x1, blocking collectives, per_device(): lax.all_to_all(jnp.broadcast_to(total, (devices, per, nstates)), everywhe...  13.9 us
  transfers between devices with their start and end apart: 13, of which 9 were waited for; matrix products, arithmetic and copies ran while one was open for 0% of the time, Pallas kernels for 13%

profile of v3, /device:TPU:0, one launch (start us, length us, event | category | flops | bytes accessed | tf_op | source)
XLA Modules:
  0.0 165.9 jit_solution(9900041558478759573)
XLA Ops:
  0.0 1.8 %convert_element_type.5 = bf16[4,16,16,512]{3,2,1,0:T(8,128)(2,1)S(1)} convert(f32[4,16,16,512]{3,2,1,0:T(8,128)} %param.8) | non-fusion elementwise | flops 524288 | bytes 3145728 | tf_op jit(solution)/shard_map/convert_element_type | solution.py:433
  8.4 2.6 %collective-permute-start.6 = (bf16[304,512]{1,0:T(8,128)(2,1)S(1)}, bf16[304,512]{1,0:T(8,128)(2,1)S(1)}, u32[]{:S(2)}, u32[]{:S(2)}) collective-permute-start(bf16[304,512]{1,0:T(8,128)(2,1)S(1)} %get-tuple-element.48), channel_id=1, source_target_pairs={{0,112},{16,0},{32,16},{48,32},{64,48},{80,64},{96,80},{112,96},{1... | collective-permute-start | bytes 933896 | tf_op jit(solution)/shard_map/ppermute | solution.py:21
  11.0 7.2 %shard_map.66 = (f32[8,128,512]{2,1,0:T(8,128)S(1)}, f32[8,2048]{1,0:T(8,128)S(1)}, bf16[2048,2048]{1,0:T(8,128)(2,1)S(1)}, f32[1,2048]{1,0:T(1,128)S(1)}) custom-call(f32[8,128,512]{2,1,0:T(8,128)S(1)} %get-tuple-element.41.r_0_.r_4_, f32[8,64,128]{2,1,0:T(8,128)S(1)} %get-tuple-element.42.r_1_, bf16[16,1024]{1,0:T(8,128)(2,1)S(1)} %get-tuple-element.43.r_2_, ...), custom_call_target="tpu_custom_call" | custom-call | flops 1000000000 | bytes 8388608 | tf_op jit(solution)/shard_map/pallas_call | solution.py:461
  19.1 4.9 %collective-permute-done.6.r_3_ = bf16[304,512]{1,0:T(8,128)(2,1)S(1)} collective-permute-done((bf16[304,512]{1,0:T(8,128)(2,1)S(1)}, bf16[304,512]{1,0:T(8,128)(2,1)S(1)}, u32[]{:S(2)}, u32[]{:S(2)}) %collective-permute-start.6) | collective-permute-done | bytes 311328 | tf_op jit(solution)/shard_map/ppermute | solution.py:21
  24.0 4.6 %shard_map.67 = (bf16[8,2304,256]{2,1,0:T(8,128)(2,1)S(1)}, f32[8,128,512]{2,1,0:T(8,128)S(1)}, bf16[288,512]{1,0:T(8,128)(2,1)S(1)}, bf16[288,512]{1,0:T(8,128)(2,1)S(1)}, bf16[16,1024]{1,0:T(8,128)(2,1)S(1)}) custom-call(f32[8,128,512]{2,1,0:T(8,128)S(1)} %get-tuple-element.45.r_0_, f32[8,2048]{1,0:T(8,128)S(1)} %get-tuple-element.46.r_1_, ...), custom_call_target="tpu_custom_call" | custom-call | flops 1000000000 | bytes 8388608 | tf_op jit(solution)/shard_map/pallas_call | solution.py:479
  30.2 2.6 %collective-permute-start.8 = (bf16[288,512]{1,0:T(8,128)(2,1)S(1)}, bf16[288,512]{1,0:T(8,128)(2,1)S(1)}, u32[]{:S(2)}, u32[]{:S(2)}) collective-permute-start(bf16[288,512]{1,0:T(8,128)(2,1)S(1)} %get-tuple-element.57), channel_id=1, source_target_pairs={{0,112},{16,0},{32,16},{48,32},{64,48},{80,64},{96,80},{112,96},{1... | collective-permute-start | bytes 884744 | tf_op jit(solution)/shard_map/ppermute | solution.py:21
  32.8 4.6 %shard_map.68 = (f32[8,128,512]{2,1,0:T(8,128)S(1)}, f32[8,2048]{1,0:T(8,128)S(1)}) custom-call(f32[8,128,512]{2,1,0:T(8,128)S(1)} %get-tuple-element.51.r_0_.r_4_, f32[8,64,128]{2,1,0:T(8,128)S(1)} %get-tuple-element.42.r_1_, bf16[16,1024]{1,0:T(8,128)(2,1)S(1)} %get-tuple-element.52.r_2_, bf16[2048,2048]{1,0:T(8,128)(2,1)S(1)} %get-tuple-element.53.r_3_, ...), custom_call_target="tpu_custom_call" | custom-call | flops 1000000000 | bytes 8388608 | tf_op jit(solution)/shard_map/pallas_call | solution.py:461
  37.4 3.4 %collective-permute-done.7.r_2_ = bf16[288,512]{1,0:T(8,128)(2,1)S(1)} collective-permute-done((bf16[288,512]{1,0:T(8,128)(2,1)S(1)}, bf16[288,512]{1,0:T(8,128)(2,1)S(1)}, u32[]{:S(2)}, u32[]{:S(2)}) %collective-permute-start.7) | collective-permute-done | bytes 294944 | tf_op jit(solution)/shard_map/ppermute | solution.py:21
  40.8 3.5 %collective-permute-done.8.r_3_ = bf16[288,512]{1,0:T(8,128)(2,1)S(1)} collective-permute-done((bf16[288,512]{1,0:T(8,128)(2,1)S(1)}, bf16[288,512]{1,0:T(8,128)(2,1)S(1)}, u32[]{:S(2)}, u32[]{:S(2)}) %collective-permute-start.8) | collective-permute-done | bytes 294944 | tf_op jit(solution)/shard_map/ppermute | solution.py:21
  44.3 3.9 %shard_map.69 = (f32[8,128,512]{2,1,0:T(8,128)S(1)}, bf16[288,512]{1,0:T(8,128)(2,1)S(1)}, bf16[288,512]{1,0:T(8,128)(2,1)S(1)}, bf16[16,1024]{1,0:T(8,128)(2,1)S(1)}) custom-call(f32[8,128,512]{2,1,0:T(8,128)S(1)} %get-tuple-element.54.r_0_, f32[8,2048]{1,0:T(8,128)S(1)} %get-tuple-element.55.r_1_, bf16[288,512]{1,0:T(8,128)(2,1)S(1)} %collective-permute-done.7.r_2_, ...), custom_call_target="tpu_custom_call" | custom-call | flops 1000000000 | bytes 8388608 | tf_op jit(solution)/shard_map/pallas_call | solution.py:479
  49.7 2.6 %collective-permute-start.10 = (bf16[288,512]{1,0:T(8,128)(2,1)S(1)}, bf16[288,512]{1,0:T(8,128)(2,1)S(1)}, u32[]{:S(2)}, u32[]{:S(2)}) collective-permute-start(bf16[288,512]{1,0:T(8,128)(2,1)S(1)} %get-tuple-element.64), channel_id=1, source_target_pairs={{0,112},{16,0},{32,16},{48,32},{64,48},{80,64},{96,80},{112,96},{1... | collective-permute-start | bytes 884744 | tf_op jit(solution)/shard_map/ppermute | solution.py:21
  52.4 4.6 %shard_map.70 = (f32[8,128,512]{2,1,0:T(8,128)S(1)}, f32[8,2048]{1,0:T(8,128)S(1)}) custom-call(f32[8,128,512]{2,1,0:T(8,128)S(1)} %get-tuple-element.59.r_0_.r_4_, f32[8,64,128]{2,1,0:T(8,128)S(1)} %get-tuple-element.42.r_1_, bf16[16,1024]{1,0:T(8,128)(2,1)S(1)} %get-tuple-element.60.r_2_, bf16[2048,2048]{1,0:T(8,128)(2,1)S(1)} %get-tuple-element.53.r_3_, ...), custom_call_target="tpu_custom_call" | custom-call | flops 1000000000 | bytes 8388608 | tf_op jit(solution)/shard_map/pallas_call | solution.py:461
  56.9 3.4 %collective-permute-done.9.r_2_ = bf16[288,512]{1,0:T(8,128)(2,1)S(1)} collective-permute-done((bf16[288,512]{1,0:T(8,128)(2,1)S(1)}, bf16[288,512]{1,0:T(8,128)(2,1)S(1)}, u32[]{:S(2)}, u32[]{:S(2)}) %collective-permute-start.9) | collective-permute-done | bytes 294944 | tf_op jit(solution)/shard_map/ppermute | solution.py:21
  60.3 2.3 %collective-permute-done.10.r_3_ = bf16[288,512]{1,0:T(8,128)(2,1)S(1)} collective-permute-done((bf16[288,512]{1,0:T(8,128)(2,1)S(1)}, bf16[288,512]{1,0:T(8,128)(2,1)S(1)}, u32[]{:S(2)}, u32[]{:S(2)}) %collective-permute-start.10) | collective-permute-done | bytes 294944 | tf_op jit(solution)/shard_map/ppermute | solution.py:21
  62.6 3.9 %shard_map.71 = (f32[8,128,512]{2,1,0:T(8,128)S(1)}, bf16[288,512]{1,0:T(8,128)(2,1)S(1)}, bf16[288,512]{1,0:T(8,128)(2,1)S(1)}, bf16[16,1024]{1,0:T(8,128)(2,1)S(1)}) custom-call(f32[8,128,512]{2,1,0:T(8,128)S(1)} %get-tuple-element.61.r_0_, f32[8,2048]{1,0:T(8,128)S(1)} %get-tuple-element.62.r_1_, bf16[288,512]{1,0:T(8,128)(2,1)S(1)} %collective-permute-done.9.r_2_, ...), custom_call_target="tpu_custom_call" | custom-call | flops 1000000000 | bytes 8388608 | tf_op jit(solution)/shard_map/pallas_call | solution.py:479
  68.1 2.7 %collective-permute-start.12 = (bf16[288,512]{1,0:T(8,128)(2,1)S(1)}, bf16[288,512]{1,0:T(8,128)(2,1)S(1)}, u32[]{:S(2)}, u32[]{:S(2)}) collective-permute-start(bf16[288,512]{1,0:T(8,128)(2,1)S(1)} %get-tuple-element.70), channel_id=1, source_target_pairs={{0,112},{16,0},{32,16},{48,32},{64,48},{80,64},{96,80},{112,96},{1... | collective-permute-start | bytes 884744 | tf_op jit(solution)/shard_map/ppermute | solution.py:21
  70.7 4.6 %shard_map.72 = (f32[8,128,512]{2,1,0:T(8,128)S(1)}, f32[8,2048]{1,0:T(8,128)S(1)}) custom-call(f32[8,128,512]{2,1,0:T(8,128)S(1)} %get-tuple-element.65.r_0_, f32[8,64,128]{2,1,0:T(8,128)S(1)} %get-tuple-element.42.r_1_, bf16[16,1024]{1,0:T(8,128)(2,1)S(1)} %get-tuple-element.66.r_2_, bf16[2048,2048]{1,0:T(8,128)(2,1)S(1)} %get-tuple-element.53.r_3_, ...), custom_call_target="tpu_custom_call" | custom-call | flops 1000000000 | bytes 8388608 | tf_op jit(solution)/shard_map/pallas_call | solution.py:461
  75.3 3.0 %collective-permute-done.11.r_2_ = bf16[288,512]{1,0:T(8,128)(2,1)S(1)} collective-permute-done((bf16[288,512]{1,0:T(8,128)(2,1)S(1)}, bf16[288,512]{1,0:T(8,128)(2,1)S(1)}, u32[]{:S(2)}, u32[]{:S(2)}) %collective-permute-start.11) | collective-permute-done | bytes 294944 | tf_op jit(solution)/shard_map/ppermute | solution.py:21
  79.7 3.1 %shard_map.73 = bf16[16,64,512]{2,1,0:T(8,128)(2,1)S(1)} custom-call(f32[8,128,512]{2,1,0:T(8,128)S(1)} %get-tuple-element.67.r_0_, f32[8,2048]{1,0:T(8,128)S(1)} %get-tuple-element.68.r_1_, bf16[288,512]{1,0:T(8,128)(2,1)S(1)} %collective-permute-done.11.r_2_, bf16[288,512]{1,0:T(8,128)(2,1)S(1)} %collective-permute-done.12.r_3_, ...), custom_call_target="tpu_custom_call" | custom-call | flops 1000000000 | bytes 8388608 | tf_op jit(solution)/shard_map/pallas_call | solution.py:479
  82.7 24.9 %all_to_all.20.r_0_ = bf16[16,64,512]{2,1,0:T(8,128)(2,1)S(1)} all-to-all(bf16[16,64,512]{2,1,0:T(8,128)(2,1)S(1)} %shard_map.73), channel_id=1, replica_groups=mesh['ring'=8,'core'=2,'st'=8] {'st','core'}, dimensions={0} | all-to-all | bytes 2097152 | tf_op jit(solution)/shard_map/all_to_all | solution.py:491
  108.1 14.5 %all_to_all.21 = f32[128,1,128]{2,1,0:T(1,128)S(1)} all-to-all(f32[128,1,128]{2,1,0:T(1,128)S(1)} %bitcast.18), channel_id=1, replica_groups=mesh['ring'=8,'core'=2,'st'=8] {'ring','core','st'}, dimensions={0} | all-to-all | bytes 131072 | tf_op jit(solution)/shard_map/all_to_all | solution.py:502
  122.8 13.9 %all_to_all.22 = f32[128,1,128]{2,1,0:T(1,128)S(1)} all-to-all(f32[128,1,128]{2,1,0:T(1,128)S(1)} %broadcast_in_dim.2), channel_id=1, replica_groups=mesh['ring'=8,'core'=2,'st'=8] {'ring','core','st'}, dimensions={0} | all-to-all | bytes 131072 | tf_op jit(solution)/shard_map/all_to_all | solution.py:504
  136.7 7.4 %shard_map.75 = bf16[8,32,16,128]{3,2,1,0:T(8,128)(2,1)S(1)} custom-call(f32[128,128]{1,0:T(8,128)S(1)} %bitcast.17, bf16[8,128,512]{2,1,0:T(8,128)(2,1)S(1)} %get-tuple-element.72.ordered), custom_call_target="tpu_custom_call" | custom-call | flops 200000000 | bytes 2097152 | tf_op jit(solution)/shard_map/pallas_call | solution.py:505
  144.0 20.6 %all_to_all.23 = bf16[8,32,16,128]{3,2,1,0:T(8,128)(2,1)S(1)} all-to-all(bf16[8,32,16,128]{3,2,1,0:T(8,128)(2,1)S(1)} %shard_map.75), channel_id=1, replica_groups=mesh['ring'=8,'core'=2,'st'=8] {'st'}, dimensions={0} | all-to-all | bytes 2097152 | tf_op jit(solution)/shard_map/all_to_all | solution.py:511
  (34 shorter events, 15.3 us)
Async XLA Ops:
  0.0 2.0 %copy-start.4 = (bf16[16,4,64,128]{3,2,1,0:T(8,128)(2,1)S(1)}, bf16[16,4,64,128]{3,2,1,0:T(8,128)(2,1)}, u32[]{:S(2)}) copy-start(bf16[16,4,64,128]{3,2,1,0:T(8,128)(2,1)} %param.6) | copy-start | bytes 3145732
  1.8 1.6 copy-start
  1.9 1.7 %copy-start.2 = (s32[4,16,16]{2,1,0:T(8,128)S(1)}, s32[4,16,16]{2,1,0:T(8,128)}, u32[]{:S(2)}) copy-start(s32[4,16,16]{2,1,0:T(8,128)} %r_3_.1) | copy-start | bytes 12292
  1.9 2.1 %copy-start.3 = (s32[4,16]{1,0:T(4,128)S(1)}, s32[4,16]{1,0:T(4,128)}, u32[]{:S(2)}) copy-start(s32[4,16]{1,0:T(4,128)} %r_4_.1) | copy-start | bytes 772
  1.9 3.7 %collective-permute-start.1 = (bf16[4,256,512]{2,1,0:T(8,128)(2,1)S(1)}, bf16[4,256,512]{2,1,0:T(8,128)(2,1)S(1)}, u32[]{:S(2)}, u32[]{:S(2)}) collective-permute-start(bf16[4,256,512]{2,1,0:T(8,128)(2,1)S(1)} %bitcast.15), channel_id=1, source_target_pairs={{0,8},{8,0},{1,9},{9,1},{2,10},{10,2},{3,11},{11,3},{4,12},{12,4},... | collective-permute-start | bytes 3145736 | tf_op jit(solution)/shard_map/ppermute | solution.py:430
  2.9 8.1 %copy-start.1 = (f32[12288]{0:T(1024)S(1)}, f32[12288]{0:T(1024)}, u32[]{:S(2)}) copy-start(f32[12288]{0:T(1024)} %param.11) | copy-start | bytes 147460
  2.9 2.7 %collective-permute-start = (bf16[4,128,512]{2,1,0:T(8,128)(2,1)S(1)}, bf16[4,128,512]{2,1,0:T(8,128)(2,1)S(1)}, u32[]{:S(2)}, u32[]{:S(2)}) collective-permute-start(bf16[4,128,512]{2,1,0:T(8,128)(2,1)S(1)} %get-tuple-element.40), channel_id=1, source_target_pairs={{0,8},{8,0},{1,9},{9,1},{2,10},{10,2},{3,11},{11,3},{4,12},{12,4},... | collective-permute-start | bytes 1572872 | tf_op jit(solution)/shard_map/ppermute | solution.py:430
  3.5 2.1 %collective-permute-start.4 = (f32[4,64,128]{2,1,0:T(8,128)S(1)}, f32[4,64,128]{2,1,0:T(8,128)S(1)}, u32[]{:S(2)}, u32[]{:S(2)}) collective-permute-start(f32[4,64,128]{2,1,0:T(8,128)S(1)} %copy-done), channel_id=1, source_target_pairs={{0,8},{8,0},{1,9},{9,1},{2,10},{10,2},{3,11},{11,3},{4,12},{12,4},... | collective-permute-start | bytes 393224 | tf_op jit(solution)/shard_map/ppermute | solution.py:430
  3.6 2.0 %collective-permute-start.2 = (s32[4,16,16]{2,1,0:T(8,128)S(1)}, s32[4,16,16]{2,1,0:T(8,128)S(1)}, u32[]{:S(2)}, u32[]{:S(2)}) collective-permute-start(s32[4,16,16]{2,1,0:T(8,128)S(1)} %copy-done.2), channel_id=1, source_target_pairs={{0,8},{8,0},{1,9},{9,1},{2,10},{10,2},{3,11},{11,3},{4,12},{12,4},... | collective-permute-start | bytes 12296 | tf_op jit(solution)/shard_map/ppermute | solution.py:430
  4.0 1.6 collective-permute-start.3
  6.7 12.4 %collective-permute-start.5 = (bf16[304,512]{1,0:T(8,128)(2,1)S(1)}, bf16[304,512]{1,0:T(8,128)(2,1)S(1)}, u32[]{:S(2)}, u32[]{:S(2)}) collective-permute-start(bf16[304,512]{1,0:T(8,128)(2,1)S(1)} %get-tuple-element.47), channel_id=1, source_target_pairs={{0,16},{16,32},{32,48},{48,64},{64,80},{80,96},{96,112},{112,0},{1... | collective-permute-start | bytes 933896 | tf_op jit(solution)/shard_map/ppermute | solution.py:21
  8.4 15.6 %collective-permute-start.6 = (bf16[304,512]{1,0:T(8,128)(2,1)S(1)}, bf16[304,512]{1,0:T(8,128)(2,1)S(1)}, u32[]{:S(2)}, u32[]{:S(2)}) collective-permute-start(bf16[304,512]{1,0:T(8,128)(2,1)S(1)} %get-tuple-element.48), channel_id=1, source_target_pairs={{0,112},{16,0},{32,16},{48,32},{64,48},{80,64},{96,80},{112,96},{1... | collective-permute-start | bytes 933896 | tf_op jit(solution)/shard_map/ppermute | solution.py:21
  28.6 12.1 %collective-permute-start.7 = (bf16[288,512]{1,0:T(8,128)(2,1)S(1)}, bf16[288,512]{1,0:T(8,128)(2,1)S(1)}, u32[]{:S(2)}, u32[]{:S(2)}) collective-permute-start(bf16[288,512]{1,0:T(8,128)(2,1)S(1)} %get-tuple-element.56), channel_id=1, source_target_pairs={{0,16},{16,32},{32,48},{48,64},{64,80},{80,96},{96,112},{112,0},{1... | collective-permute-start | bytes 884744 | tf_op jit(solution)/shard_map/ppermute | solution.py:21
  30.2 14.1 %collective-permute-start.8 = (bf16[288,512]{1,0:T(8,128)(2,1)S(1)}, bf16[288,512]{1,0:T(8,128)(2,1)S(1)}, u32[]{:S(2)}, u32[]{:S(2)}) collective-permute-start(bf16[288,512]{1,0:T(8,128)(2,1)S(1)} %get-tuple-element.57), channel_id=1, source_target_pairs={{0,112},{16,0},{32,16},{48,32},{64,48},{80,64},{96,80},{112,96},{1... | collective-permute-start | bytes 884744 | tf_op jit(solution)/shard_map/ppermute | solution.py:21
  48.2 12.1 %collective-permute-start.9 = (bf16[288,512]{1,0:T(8,128)(2,1)S(1)}, bf16[288,512]{1,0:T(8,128)(2,1)S(1)}, u32[]{:S(2)}, u32[]{:S(2)}) collective-permute-start(bf16[288,512]{1,0:T(8,128)(2,1)S(1)} %get-tuple-element.63), channel_id=1, source_target_pairs={{0,16},{16,32},{32,48},{48,64},{64,80},{80,96},{96,112},{112,0},{1... | collective-permute-start | bytes 884744 | tf_op jit(solution)/shard_map/ppermute | solution.py:21
  49.7 12.9 %collective-permute-start.10 = (bf16[288,512]{1,0:T(8,128)(2,1)S(1)}, bf16[288,512]{1,0:T(8,128)(2,1)S(1)}, u32[]{:S(2)}, u32[]{:S(2)}) collective-permute-start(bf16[288,512]{1,0:T(8,128)(2,1)S(1)} %get-tuple-element.64), channel_id=1, source_target_pairs={{0,112},{16,0},{32,16},{48,32},{64,48},{80,64},{96,80},{112,96},{1... | collective-permute-start | bytes 884744 | tf_op jit(solution)/shard_map/ppermute | solution.py:21
  66.5 11.7 %collective-permute-start.11 = (bf16[288,512]{1,0:T(8,128)(2,1)S(1)}, bf16[288,512]{1,0:T(8,128)(2,1)S(1)}, u32[]{:S(2)}, u32[]{:S(2)}) collective-permute-start(bf16[288,512]{1,0:T(8,128)(2,1)S(1)} %get-tuple-element.69), channel_id=1, source_target_pairs={{0,16},{16,32},{32,48},{48,64},{64,80},{80,96},{96,112},{112,0},{1... | collective-permute-start | bytes 884744 | tf_op jit(solution)/shard_map/ppermute | solution.py:21
  68.1 11.6 %collective-permute-start.12 = (bf16[288,512]{1,0:T(8,128)(2,1)S(1)}, bf16[288,512]{1,0:T(8,128)(2,1)S(1)}, u32[]{:S(2)}, u32[]{:S(2)}) collective-permute-start(bf16[288,512]{1,0:T(8,128)(2,1)S(1)} %get-tuple-element.70), channel_id=1, source_target_pairs={{0,112},{16,0},{32,16},{48,32},{64,48},{80,64},{96,80},{112,96},{1... | collective-permute-start | bytes 884744 | tf_op jit(solution)/shard_map/ppermute | solution.py:21

commit v4 on v3

--- a/solution.py
+++ b/solution.py
@@ -242,6 +242,22 @@
         return carry
 
     lax.fori_loop(0, tiles, tile_step, 0)
+
+
+def turn_kernel(sizes, early, core, *refs):
+    inputs, refs = refs[:5], refs[5:]
+    made, refs = ([], refs) if early else (refs[:4], refs[4:])
+
+    @pl.when((core[0] != 0) if early else (core[0] == 0))
+    def _():
+        local_kernel(sizes, True, *inputs, *refs)
+
+    if not early:
+
+        @pl.when(core[0] != 0)
+        def _():
+            for ready, out in zip(made, refs):
+                out[...] = ready[...]
 
 
 def step_kernel(sizes, first, last, *refs):
@@ -453,20 +469,27 @@
     prev, cur = None, field
     for m in range(4):
         first, last = m == 0, m == 3
+        outs = [f32(shape), f32((share_states, count))]
+        args = [cur, shift, partial]
+        if first:
+            args = [core] + args + [names, strength.reshape(-1, 128)]
+            outs += [bf16((count, count)), f32((1, count))]
+            made = call(
+                lambda *r: turn_kernel(sizes, True, *r), outs,
+                in_specs=[scalar] + [whole] * 5, flops=1e9, nbytes=8 * 2**20,
+            )(*args)
+            low, high, *made = lax.optimization_barrier((low, high, *made))
         below = passed_along(high, "ring", 1)
         above = passed_along(low, "ring", -1)
-        outs = [f32(shape), f32((share_states, count))]
-        args = [cur, shift, partial]
-        args += [names, strength.reshape(-1, 128)] if first else [own_table, prev]
-        got = call(
-            lambda *r, first=first: local_kernel(sizes, first, *r),
-            outs + ([bf16((count, count)), f32((1, count))] if first else []),
-            flops=1e9, nbytes=8 * 2**20,
-        )(*args)
         if first:
-            base, share, own_table, weight = got
+            base, share, own_table, weight = call(
+                lambda *r: turn_kernel(sizes, False, *r), outs,
+                in_specs=[scalar] + [whole] * 9, flops=1e9, nbytes=8 * 2**20,
+            )(*args, *made)
         else:
-            base, share = got
+            base, share = call(
+                lambda *r: local_kernel(sizes, False, *r), outs, flops=1e9, nbytes=8 * 2**20
+            )(*args, own_table, prev)
         args = [base, share, below, above, weight, names, proj] + ([] if first else [table])
         outs = [bf16((planes, (planes + 1) * cols, cols))] if first else []
         scratch = [pltpu.VMEM(shape, F32)]

time: 166 us -> 158 us (0.952)
  waiting for transfers between devices: 24.2 us -> 13.3 us
  blocking collectives: 73.9 us -> 76.4 us
    ppermute x8, waiting for transfers between devices: 22.7 us -> 11.7 us  [passed_along(): lax.ppermute(array, axis, [(i, (i + by) % devices) for i in range(devices)])]
    all_to_all x1, blocking collectives: 24.9 us -> 28.4 us  [per_device(): cells = lax.all_to_all(filtered, ('st', 'core'), 0, 0, tiled=True)]
    pallas_call x4 -> x5, Pallas kernels: 20.9 us -> 21.1 us  [the longest x3 13.7 us: per_device(): call(lambda *r: local_kernel(sizes, False, *r), outs, flops=1000000000.0,...]
  transfers between devices with their start and end apart: 13 -> 13, of which waited for: 9 -> 7; matrix products, arithmetic and copies ran while one was open for 0% -> 0% of each run, Pallas kernels for 13% -> 14%
where the time goes in v4:
time: 158 us
  blocking collectives  76.4 us (48%)
  Pallas kernels  45.6 us (29%)
  starting transfers between devices  18.1 us (11%)
  waiting for transfers between devices  13.3 us (8%)
  local copies, waits for them, and re-layouts  1.99 us (1%)
  other arithmetic  1.99 us (1%)
    all_to_all x1, blocking collectives, per_device(): cells = lax.all_to_all(filtered, ('st', 'core'), 0, 0, tiled=True)  28.4 us
    all_to_all x1, blocking collectives, per_device(): rotated = lax.all_to_all(rotated, 'st', 0, 0, tiled=True)  20.6 us
    ppermute x8, starting transfers between devices, passed_along(): lax.ppermute(array, axis, [(i, (i + by) % devices) for i in range(devices)])  16.8 us
    pallas_call x4, Pallas kernels, per_device(): call(lambda *r, first=first, last=last: step_kernel(sizes, first, last, *...  15.4 us
    all_to_all x1, blocking collectives, per_device(): lax.all_to_all(jnp.broadcast_to(total, (devices, per, nstates)), everywhe...  13.8 us
    pallas_call x3, Pallas kernels, per_device(): call(lambda *r: local_kernel(sizes, False, *r), outs, flops=1000000000.0,...  13.7 us
    all_to_all x1, blocking collectives, per_device(): lax.all_to_all(part.reshape(devices, per, nstates), everywhere, 0, 0, til...  13.6 us
    ppermute x8, waiting for transfers between devices, passed_along(): lax.ppermute(array, axis, [(i, (i + by) % devices) for i in range(devices)])  11.7 us
  transfers between devices with their start and end apart: 13, of which 7 were waited for; matrix products, arithmetic and copies ran while one was open for 0% of the time, Pallas kernels for 14%

profile of v4, /device:TPU:0, one launch (start us, length us, event | category | flops | bytes accessed | tf_op | source)
XLA Modules:
  0.0 157.6 jit_solution(2900818083352248617)
XLA Ops:
  0.0 1.8 %convert_element_type.5 = bf16[4,16,16,512]{3,2,1,0:T(8,128)(2,1)S(1)} convert(f32[4,16,16,512]{3,2,1,0:T(8,128)} %param.8) | non-fusion elementwise | flops 524288 | bytes 3145728 | tf_op jit(solution)/shard_map/convert_element_type | solution.py:449
  6.8 1.6 %collective-permute-start.5 = (bf16[304,512]{1,0:T(8,128)(2,1)S(1)}, bf16[304,512]{1,0:T(8,128)(2,1)S(1)}, u32[]{:S(2)}, u32[]{:S(2)}) collective-permute-start(bf16[304,512]{1,0:T(8,128)(2,1)S(1)} %get-tuple-element.67), channel_id=1, source_target_pairs={{0,16},{16,32},{32,48},{48,64},{64,80},{80,96},{96,112},{112,0},{1... | collective-permute-start | bytes 933896 | tf_op jit(solution)/shard_map/ppermute | solution.py:21
  8.4 2.6 %collective-permute-start.6 = (bf16[304,512]{1,0:T(8,128)(2,1)S(1)}, bf16[304,512]{1,0:T(8,128)(2,1)S(1)}, u32[]{:S(2)}, u32[]{:S(2)}) collective-permute-start(bf16[304,512]{1,0:T(8,128)(2,1)S(1)} %get-tuple-element.68), channel_id=1, source_target_pairs={{0,112},{16,0},{32,16},{48,32},{64,48},{80,64},{96,80},{112,96},{1... | collective-permute-start | bytes 933896 | tf_op jit(solution)/shard_map/ppermute | solution.py:21
  11.0 7.4 %shard_map.67 = (f32[8,128,512]{2,1,0:T(8,128)S(1)}, f32[8,2048]{1,0:T(8,128)S(1)}, bf16[2048,2048]{1,0:T(8,128)(2,1)S(1)}, f32[1,2048]{1,0:T(1,128)S(1)}) custom-call(s32[1]{0:T(128)} %bitcast.core.r_0_, f32[8,128,512]{2,1,0:T(8,128)S(1)} %get-tuple-element.51.r_1_.r_4_, f32[8,64,128]{2,1,0:T(8,128)S(1)} %get-tuple-element.52.r_2_.r_1_, ...), custom_call_target="tpu_custom_call" | custom-call | flops 1000000000 | bytes 8388608 | tf_op jit(solution)/shard_map/pallas_call | solution.py:485
  18.4 4.6 %shard_map.68 = (bf16[8,2304,256]{2,1,0:T(8,128)(2,1)S(1)}, f32[8,128,512]{2,1,0:T(8,128)S(1)}, bf16[288,512]{1,0:T(8,128)(2,1)S(1)}, bf16[288,512]{1,0:T(8,128)(2,1)S(1)}, bf16[16,1024]{1,0:T(8,128)(2,1)S(1)}) custom-call(f32[8,128,512]{2,1,0:T(8,128)S(1)} %get-tuple-element.65.r_0_, f32[8,2048]{1,0:T(8,128)S(1)} %get-tuple-element.66.r_1_, ...), custom_call_target="tpu_custom_call" | custom-call | flops 1000000000 | bytes 8388608 | tf_op jit(solution)/shard_map/pallas_call | solution.py:502
  24.6 2.7 %collective-permute-start.8 = (bf16[288,512]{1,0:T(8,128)(2,1)S(1)}, bf16[288,512]{1,0:T(8,128)(2,1)S(1)}, u32[]{:S(2)}, u32[]{:S(2)}) collective-permute-start(bf16[288,512]{1,0:T(8,128)(2,1)S(1)} %get-tuple-element.77), channel_id=1, source_target_pairs={{0,112},{16,0},{32,16},{48,32},{64,48},{80,64},{96,80},{112,96},{1... | collective-permute-start | bytes 884744 | tf_op jit(solution)/shard_map/ppermute | solution.py:21
  27.3 4.6 %shard_map.69 = (f32[8,128,512]{2,1,0:T(8,128)S(1)}, f32[8,2048]{1,0:T(8,128)S(1)}) custom-call(f32[8,128,512]{2,1,0:T(8,128)S(1)} %get-tuple-element.71.r_0_.r_4_, f32[8,64,128]{2,1,0:T(8,128)S(1)} %get-tuple-element.52.r_2_.r_1_, bf16[16,1024]{1,0:T(8,128)(2,1)S(1)} %get-tuple-element.72.r_2_, bf16[2048,2048]{1,0:T(8,128)(2,1)S(1)} %get-tuple-element.73.r_3_, ...), custom_call_target="tpu_custom_call" | custom-call | flops 1000000000 | bytes 8388608 | tf_op jit(solution)/shard_map/pallas_call | solution.py:490
  32.0 2.9 %collective-permute-done.8.r_3_ = bf16[288,512]{1,0:T(8,128)(2,1)S(1)} collective-permute-done((bf16[288,512]{1,0:T(8,128)(2,1)S(1)}, bf16[288,512]{1,0:T(8,128)(2,1)S(1)}, u32[]{:S(2)}, u32[]{:S(2)}) %collective-permute-start.8) | collective-permute-done | bytes 294944 | tf_op jit(solution)/shard_map/ppermute | solution.py:21
  34.9 3.9 %shard_map.70 = (f32[8,128,512]{2,1,0:T(8,128)S(1)}, bf16[288,512]{1,0:T(8,128)(2,1)S(1)}, bf16[288,512]{1,0:T(8,128)(2,1)S(1)}, bf16[16,1024]{1,0:T(8,128)(2,1)S(1)}) custom-call(f32[8,128,512]{2,1,0:T(8,128)S(1)} %get-tuple-element.74.r_0_, f32[8,2048]{1,0:T(8,128)S(1)} %get-tuple-element.75.r_1_, bf16[288,512]{1,0:T(8,128)(2,1)S(1)} %collective-permute-done.7.r_2_, ...), custom_call_target="tpu_custom_call" | custom-call | flops 1000000000 | bytes 8388608 | tf_op jit(solution)/shard_map/pallas_call | solution.py:502
  38.8 1.6 collective-permute-start.9
  40.3 2.6 %collective-permute-start.10 = (bf16[288,512]{1,0:T(8,128)(2,1)S(1)}, bf16[288,512]{1,0:T(8,128)(2,1)S(1)}, u32[]{:S(2)}, u32[]{:S(2)}) collective-permute-start(bf16[288,512]{1,0:T(8,128)(2,1)S(1)} %get-tuple-element.84), channel_id=1, source_target_pairs={{0,112},{16,0},{32,16},{48,32},{64,48},{80,64},{96,80},{112,96},{1... | collective-permute-start | bytes 884744 | tf_op jit(solution)/shard_map/ppermute | solution.py:21
  43.0 4.6 %shard_map.71 = (f32[8,128,512]{2,1,0:T(8,128)S(1)}, f32[8,2048]{1,0:T(8,128)S(1)}) custom-call(f32[8,128,512]{2,1,0:T(8,128)S(1)} %get-tuple-element.79.r_0_.r_4_, f32[8,64,128]{2,1,0:T(8,128)S(1)} %get-tuple-element.52.r_2_.r_1_, bf16[16,1024]{1,0:T(8,128)(2,1)S(1)} %get-tuple-element.80.r_2_, bf16[2048,2048]{1,0:T(8,128)(2,1)S(1)} %get-tuple-element.73.r_3_, ...), custom_call_target="tpu_custom_call" | custom-call | flops 1000000000 | bytes 8388608 | tf_op jit(solution)/shard_map/pallas_call | solution.py:490
  47.7 3.8 %collective-permute-done.10.r_3_ = bf16[288,512]{1,0:T(8,128)(2,1)S(1)} collective-permute-done((bf16[288,512]{1,0:T(8,128)(2,1)S(1)}, bf16[288,512]{1,0:T(8,128)(2,1)S(1)}, u32[]{:S(2)}, u32[]{:S(2)}) %collective-permute-start.10) | collective-permute-done | bytes 294944 | tf_op jit(solution)/shard_map/ppermute | solution.py:21
  51.4 3.9 %shard_map.72 = (f32[8,128,512]{2,1,0:T(8,128)S(1)}, bf16[288,512]{1,0:T(8,128)(2,1)S(1)}, bf16[288,512]{1,0:T(8,128)(2,1)S(1)}, bf16[16,1024]{1,0:T(8,128)(2,1)S(1)}) custom-call(f32[8,128,512]{2,1,0:T(8,128)S(1)} %get-tuple-element.81.r_0_, f32[8,2048]{1,0:T(8,128)S(1)} %get-tuple-element.82.r_1_, bf16[288,512]{1,0:T(8,128)(2,1)S(1)} %collective-permute-done.9.r_2_, ...), custom_call_target="tpu_custom_call" | custom-call | flops 1000000000 | bytes 8388608 | tf_op jit(solution)/shard_map/pallas_call | solution.py:502
  55.3 1.6 collective-permute-start.11
  56.9 2.7 %collective-permute-start.12 = (bf16[288,512]{1,0:T(8,128)(2,1)S(1)}, bf16[288,512]{1,0:T(8,128)(2,1)S(1)}, u32[]{:S(2)}, u32[]{:S(2)}) collective-permute-start(bf16[288,512]{1,0:T(8,128)(2,1)S(1)} %get-tuple-element.90), channel_id=1, source_target_pairs={{0,112},{16,0},{32,16},{48,32},{64,48},{80,64},{96,80},{112,96},{1... | collective-permute-start | bytes 884744 | tf_op jit(solution)/shard_map/ppermute | solution.py:21
  59.5 4.6 %shard_map.73 = (f32[8,128,512]{2,1,0:T(8,128)S(1)}, f32[8,2048]{1,0:T(8,128)S(1)}) custom-call(f32[8,128,512]{2,1,0:T(8,128)S(1)} %get-tuple-element.85.r_0_, f32[8,64,128]{2,1,0:T(8,128)S(1)} %get-tuple-element.52.r_2_.r_1_, bf16[16,1024]{1,0:T(8,128)(2,1)S(1)} %get-tuple-element.86.r_2_, bf16[2048,2048]{1,0:T(8,128)(2,1)S(1)} %get-tuple-element.73.r_3_, ...), custom_call_target="tpu_custom_call" | custom-call | flops 1000000000 | bytes 8388608 | tf_op jit(solution)/shard_map/pallas_call | solution.py:490
  64.2 4.6 %collective-permute-done.12.r_3_ = bf16[288,512]{1,0:T(8,128)(2,1)S(1)} collective-permute-done((bf16[288,512]{1,0:T(8,128)(2,1)S(1)}, bf16[288,512]{1,0:T(8,128)(2,1)S(1)}, u32[]{:S(2)}, u32[]{:S(2)}) %collective-permute-start.12) | collective-permute-done | bytes 294944 | tf_op jit(solution)/shard_map/ppermute | solution.py:21
  68.9 3.0 %shard_map.74 = bf16[16,64,512]{2,1,0:T(8,128)(2,1)S(1)} custom-call(f32[8,128,512]{2,1,0:T(8,128)S(1)} %get-tuple-element.87.r_0_, f32[8,2048]{1,0:T(8,128)S(1)} %get-tuple-element.88.r_1_, bf16[288,512]{1,0:T(8,128)(2,1)S(1)} %collective-permute-done.11.r_2_, bf16[288,512]{1,0:T(8,128)(2,1)S(1)} %collective-permute-done.12.r_3_, ...), custom_call_target="tpu_custom_call" | custom-call | flops 1000000000 | bytes 8388608 | tf_op jit(solution)/shard_map/pallas_call | solution.py:502
  71.9 28.4 %all_to_all.20.r_0_ = bf16[16,64,512]{2,1,0:T(8,128)(2,1)S(1)} all-to-all(bf16[16,64,512]{2,1,0:T(8,128)(2,1)S(1)} %shard_map.74), channel_id=1, replica_groups=mesh['ring'=8,'core'=2,'st'=8] {'st','core'}, dimensions={0} | all-to-all | bytes 2097152 | tf_op jit(solution)/shard_map/all_to_all | solution.py:514
  100.7 13.6 %all_to_all.21 = f32[128,1,128]{2,1,0:T(1,128)S(1)} all-to-all(f32[128,1,128]{2,1,0:T(1,128)S(1)} %bitcast.18), channel_id=1, replica_groups=mesh['ring'=8,'core'=2,'st'=8] {'ring','core','st'}, dimensions={0} | all-to-all | bytes 131072 | tf_op jit(solution)/shard_map/all_to_all | solution.py:525
  114.4 13.8 %all_to_all.22 = f32[128,1,128]{2,1,0:T(1,128)S(1)} all-to-all(f32[128,1,128]{2,1,0:T(1,128)S(1)} %broadcast_in_dim.2), channel_id=1, replica_groups=mesh['ring'=8,'core'=2,'st'=8] {'ring','core','st'}, dimensions={0} | all-to-all | bytes 131072 | tf_op jit(solution)/shard_map/all_to_all | solution.py:527
  128.3 7.4 %shard_map.76 = bf16[8,32,16,128]{3,2,1,0:T(8,128)(2,1)S(1)} custom-call(f32[128,128]{1,0:T(8,128)S(1)} %bitcast.17, bf16[8,128,512]{2,1,0:T(8,128)(2,1)S(1)} %get-tuple-element.92.ordered), custom_call_target="tpu_custom_call" | custom-call | flops 200000000 | bytes 2097152 | tf_op jit(solution)/shard_map/pallas_call | solution.py:528
  135.7 20.6 %all_to_all.23 = bf16[8,32,16,128]{3,2,1,0:T(8,128)(2,1)S(1)} all-to-all(bf16[8,32,16,128]{3,2,1,0:T(8,128)(2,1)S(1)} %shard_map.76), channel_id=1, replica_groups=mesh['ring'=8,'core'=2,'st'=8] {'st'}, dimensions={0} | all-to-all | bytes 2097152 | tf_op jit(solution)/shard_map/all_to_all | solution.py:534
  (35 shorter events, 8.6 us)
Async XLA Ops:
  0.0 2.0 %copy-start.4 = (bf16[16,4,64,128]{3,2,1,0:T(8,128)(2,1)S(1)}, bf16[16,4,64,128]{3,2,1,0:T(8,128)(2,1)}, u32[]{:S(2)}) copy-start(bf16[16,4,64,128]{3,2,1,0:T(8,128)(2,1)} %param.6) | copy-start | bytes 3145732
  1.8 1.6 %copy-start.1 = (f32[4,64,128]{2,1,0:T(8,128)S(1)}, f32[4,64,128]{2,1,0:T(8,128)}, u32[]{:S(2)}) copy-start(f32[4,64,128]{2,1,0:T(8,128)} %r_5_.1) | copy-start | bytes 393220
  1.9 1.7 %copy-start.2 = (s32[4,16,16]{2,1,0:T(8,128)S(1)}, s32[4,16,16]{2,1,0:T(8,128)}, u32[]{:S(2)}) copy-start(s32[4,16,16]{2,1,0:T(8,128)} %r_3_.1) | copy-start | bytes 12292
  1.9 2.1 %copy-start.3 = (s32[4,16]{1,0:T(4,128)S(1)}, s32[4,16]{1,0:T(4,128)}, u32[]{:S(2)}) copy-start(s32[4,16]{1,0:T(4,128)} %r_4_.1) | copy-start | bytes 772
  1.9 3.7 %collective-permute-start.1 = (bf16[4,256,512]{2,1,0:T(8,128)(2,1)S(1)}, bf16[4,256,512]{2,1,0:T(8,128)(2,1)S(1)}, u32[]{:S(2)}, u32[]{:S(2)}) collective-permute-start(bf16[4,256,512]{2,1,0:T(8,128)(2,1)S(1)} %bitcast.15), channel_id=1, source_target_pairs={{0,8},{8,0},{1,9},{9,1},{2,10},{10,2},{3,11},{11,3},{4,12},{12,4},... | collective-permute-start | bytes 3145736 | tf_op jit(solution)/shard_map/ppermute | solution.py:446
  2.9 3.9 %copy-start = (f32[12288]{0:T(1024)S(1)}, f32[12288]{0:T(1024)}, u32[]{:S(2)}) copy-start(f32[12288]{0:T(1024)} %param.11) | copy-start | bytes 147460
  2.9 2.7 %collective-permute-start = (bf16[4,128,512]{2,1,0:T(8,128)(2,1)S(1)}, bf16[4,128,512]{2,1,0:T(8,128)(2,1)S(1)}, u32[]{:S(2)}, u32[]{:S(2)}) collective-permute-start(bf16[4,128,512]{2,1,0:T(8,128)(2,1)S(1)} %get-tuple-element.50), channel_id=1, source_target_pairs={{0,8},{8,0},{1,9},{9,1},{2,10},{10,2},{3,11},{11,3},{4,12},{12,4},... | collective-permute-start | bytes 1572872 | tf_op jit(solution)/shard_map/ppermute | solution.py:446
  3.5 2.1 %collective-permute-start.4 = (f32[4,64,128]{2,1,0:T(8,128)S(1)}, f32[4,64,128]{2,1,0:T(8,128)S(1)}, u32[]{:S(2)}, u32[]{:S(2)}) collective-permute-start(f32[4,64,128]{2,1,0:T(8,128)S(1)} %copy-done.1), channel_id=1, source_target_pairs={{0,8},{8,0},{1,9},{9,1},{2,10},{10,2},{3,11},{11,3},{4,12},{12,4},... | collective-permute-start | bytes 393224 | tf_op jit(solution)/shard_map/ppermute | solution.py:446
  3.6 2.0 %collective-permute-start.2 = (s32[4,16,16]{2,1,0:T(8,128)S(1)}, s32[4,16,16]{2,1,0:T(8,128)S(1)}, u32[]{:S(2)}, u32[]{:S(2)}) collective-permute-start(s32[4,16,16]{2,1,0:T(8,128)S(1)} %copy-done.2), channel_id=1, source_target_pairs={{0,8},{8,0},{1,9},{9,1},{2,10},{10,2},{3,11},{11,3},{4,12},{12,4},... | collective-permute-start | bytes 12296 | tf_op jit(solution)/shard_map/ppermute | solution.py:446
  4.0 1.6 %collective-permute-start.3 = (s32[4,16]{1,0:T(4,128)S(1)}, s32[4,16]{1,0:T(4,128)S(1)}, u32[]{:S(2)}, u32[]{:S(2)}) collective-permute-start(s32[4,16]{1,0:T(4,128)S(1)} %copy-done.3), channel_id=1, source_target_pairs={{0,8},{8,0},{1,9},{9,1},{2,10},{10,2},{3,11},{11,3},{4,12},{12,4},... | collective-permute-start | bytes 776 | tf_op jit(solution)/shard_map/ppermute | solution.py:446
  6.8 11.6 %collective-permute-start.5 = (bf16[304,512]{1,0:T(8,128)(2,1)S(1)}, bf16[304,512]{1,0:T(8,128)(2,1)S(1)}, u32[]{:S(2)}, u32[]{:S(2)}) collective-permute-start(bf16[304,512]{1,0:T(8,128)(2,1)S(1)} %get-tuple-element.67), channel_id=1, source_target_pairs={{0,16},{16,32},{32,48},{48,64},{64,80},{80,96},{96,112},{112,0},{1... | collective-permute-start | bytes 933896 | tf_op jit(solution)/shard_map/ppermute | solution.py:21
  8.4 10.0 %collective-permute-start.6 = (bf16[304,512]{1,0:T(8,128)(2,1)S(1)}, bf16[304,512]{1,0:T(8,128)(2,1)S(1)}, u32[]{:S(2)}, u32[]{:S(2)}) collective-permute-start(bf16[304,512]{1,0:T(8,128)(2,1)S(1)} %get-tuple-element.68), channel_id=1, source_target_pairs={{0,112},{16,0},{32,16},{48,32},{64,48},{80,64},{96,80},{112,96},{1... | collective-permute-start | bytes 933896 | tf_op jit(solution)/shard_map/ppermute | solution.py:21
  23.1 8.9 %collective-permute-start.7 = (bf16[288,512]{1,0:T(8,128)(2,1)S(1)}, bf16[288,512]{1,0:T(8,128)(2,1)S(1)}, u32[]{:S(2)}, u32[]{:S(2)}) collective-permute-start(bf16[288,512]{1,0:T(8,128)(2,1)S(1)} %get-tuple-element.76), channel_id=1, source_target_pairs={{0,16},{16,32},{32,48},{48,64},{64,80},{80,96},{96,112},{112,0},{1... | collective-permute-start | bytes 884744 | tf_op jit(solution)/shard_map/ppermute | solution.py:21
  24.6 10.3 %collective-permute-start.8 = (bf16[288,512]{1,0:T(8,128)(2,1)S(1)}, bf16[288,512]{1,0:T(8,128)(2,1)S(1)}, u32[]{:S(2)}, u32[]{:S(2)}) collective-permute-start(bf16[288,512]{1,0:T(8,128)(2,1)S(1)} %get-tuple-element.77), channel_id=1, source_target_pairs={{0,112},{16,0},{32,16},{48,32},{64,48},{80,64},{96,80},{112,96},{1... | collective-permute-start | bytes 884744 | tf_op jit(solution)/shard_map/ppermute | solution.py:21
  38.8 8.9 %collective-permute-start.9 = (bf16[288,512]{1,0:T(8,128)(2,1)S(1)}, bf16[288,512]{1,0:T(8,128)(2,1)S(1)}, u32[]{:S(2)}, u32[]{:S(2)}) collective-permute-start(bf16[288,512]{1,0:T(8,128)(2,1)S(1)} %get-tuple-element.83), channel_id=1, source_target_pairs={{0,16},{16,32},{32,48},{48,64},{64,80},{80,96},{96,112},{112,0},{1... | collective-permute-start | bytes 884744 | tf_op jit(solution)/shard_map/ppermute | solution.py:21
  40.3 11.1 %collective-permute-start.10 = (bf16[288,512]{1,0:T(8,128)(2,1)S(1)}, bf16[288,512]{1,0:T(8,128)(2,1)S(1)}, u32[]{:S(2)}, u32[]{:S(2)}) collective-permute-start(bf16[288,512]{1,0:T(8,128)(2,1)S(1)} %get-tuple-element.84), channel_id=1, source_target_pairs={{0,112},{16,0},{32,16},{48,32},{64,48},{80,64},{96,80},{112,96},{1... | collective-permute-start | bytes 884744 | tf_op jit(solution)/shard_map/ppermute | solution.py:21
  55.3 8.9 %collective-permute-start.11 = (bf16[288,512]{1,0:T(8,128)(2,1)S(1)}, bf16[288,512]{1,0:T(8,128)(2,1)S(1)}, u32[]{:S(2)}, u32[]{:S(2)}) collective-permute-start(bf16[288,512]{1,0:T(8,128)(2,1)S(1)} %get-tuple-element.89), channel_id=1, source_target_pairs={{0,16},{16,32},{32,48},{48,64},{64,80},{80,96},{96,112},{112,0},{1... | collective-permute-start | bytes 884744 | tf_op jit(solution)/shard_map/ppermute | solution.py:21
  56.9 12.0 %collective-permute-start.12 = (bf16[288,512]{1,0:T(8,128)(2,1)S(1)}, bf16[288,512]{1,0:T(8,128)(2,1)S(1)}, u32[]{:S(2)}, u32[]{:S(2)}) collective-permute-start(bf16[288,512]{1,0:T(8,128)(2,1)S(1)} %get-tuple-element.90), channel_id=1, source_target_pairs={{0,112},{16,0},{32,16},{48,32},{64,48},{80,64},{96,80},{112,96},{1... | collective-permute-start | bytes 884744 | tf_op jit(solution)/shard_map/ppermute | solution.py:21

commit v5 on v4

--- a/solution.py
+++ b/solution.py
@@ -10,6 +10,7 @@
 
 F32 = jnp.float32
 BF16 = jnp.bfloat16
+F8 = jnp.float8_e4m3fn
 NT = (((1,), (1,)), ((), ()))
 NN = (((1,), (0,)), ((), ()))
 CORES = 2
@@ -166,7 +167,7 @@
         column = jnp.broadcast_to(names[:, q : q + 128], (128, 128)).T
         for p in range(0, own.shape[1], 128):
             if wanted(q, p):
-                store(q, p, jnp.where(column == own[:, p : p + 128], 1.0, 0.0).astype(BF16))
+                store(q, p, jnp.where(column == own[:, p : p + 128], 1.0, 0.0))
 
 
 def doubled(terms):
@@ -186,29 +187,49 @@
     return jnp.sum(jnp.where(place == bottom, of_line, 0.0), axis=0, keepdims=True)
 
 
+def applied_to(chosen, proj, tiles, mask):
+    spread = jnp.broadcast_to(chosen[None], (tiles,) + chosen.shape).reshape(mask.shape)
+    spread = jnp.where(mask, spread, 0.0).astype(BF16)
+    return lax.dot_general(spread, proj, NN, preferred_element_type=F32)
+
+
+def inner_planes(planes):
+    return range(2, planes - 2)
+
+
 def local_kernel(sizes, first, *refs):
     states, slots, rows = sizes
     refs = list(refs)
-    cur, potential, own = refs[:3]
-    rest = refs[3:]
     if first:
-        names, strength, base, share, table, weight = rest
+        cur, potential, own, proj, names, strength, base, share, inner, table, weight, square = refs
         named = names[...]
         mine = jnp.where(named < NO_NAME, named, -1.0)
 
         def store(q, p, same):
-            table[q : q + 128, p : p + 128] = same
+            table[q : q + 128, p : p + 128] = same.astype(BF16)
 
         same_names(named, mine, store, lambda q, p: True)
         weight[...] = look_up(strength[...], named)
     else:
-        table, prev, base, share = rest
+        outer, chosen, done, table, prev, potential, own, proj, cur, base, share, inner = refs
     planes, height, width = cur.shape
-    tiles = height // states
+    tiles, cols = height // states, proj.shape[1]
     gain = (1.0 if first else 2.0) / half_width
     near, far = -gain * 2.0 / 3.0, gain / 24.0
     terms = doubled(unfolded(own[...]))
     share[...] = lax.dot_general(terms, table[...], NN, preferred_element_type=F32)[:states]
+    if first:
+        same_tile = block_mask(cols, cols, slots, slots)
+        for i, z in enumerate(inner_planes(planes)):
+            products = lax.dot_general(proj[z], proj[z], NT, preferred_element_type=F32)
+            square[i] = jnp.where(same_tile, products, 0.0).astype(BF16)
+    else:
+        mask = block_mask(height, cols, states, slots)
+        for z in range(planes):
+            if z in inner_planes(planes):
+                cur[z] = done[z] + applied_to(chosen[:, z * cols : (z + 1) * cols], proj[z], tiles, mask)
+            else:
+                cur[z] = outer[z if z < 2 else z - planes + 4]
 
     def tile_step(j, carry):
         here = rows_at(j, states)
@@ -242,11 +263,13 @@
         return carry
 
     lax.fori_loop(0, tiles, tile_step, 0)
+    for i, z in enumerate(inner_planes(planes)):
+        inner[:, i * cols : (i + 1) * cols] = project(base[z].astype(BF16), proj[z], states, slots)
 
 
 def turn_kernel(sizes, early, core, *refs):
-    inputs, refs = refs[:5], refs[5:]
-    made, refs = ([], refs) if early else (refs[:4], refs[4:])
+    inputs, refs = refs[:6], refs[6:]
+    made, refs = ([], refs) if early else (refs[:6], refs[6:])
 
     @pl.when((core[0] != 0) if early else (core[0] == 0))
     def _():
@@ -260,11 +283,21 @@
                 out[...] = ready[...]
 
 
+def in_pieces(terms):
+    largest = jnp.maximum(jnp.max(jnp.abs(terms), axis=1, keepdims=True), 1e-30)
+    rest = terms * (240.0 / largest)
+    pieces = []
+    for _ in range(3):
+        pieces.append(rest.astype(F8).astype(F32))
+        rest = rest - pieces[-1]
+    return jnp.concatenate(pieces + [jnp.zeros_like(terms)], axis=0).astype(F8), largest * (1.0 / 240.0)
+
+
 def step_kernel(sizes, first, last, *refs):
     states, slots, rows = sizes
     refs = list(refs)
-    base, share, below, above, weight, names, proj = refs[:7]
-    rest = refs[7:]
+    base, share, below, above, weight, names, proj, inner, square = refs[:9]
+    rest = refs[9:]
     planes, height, width = base.shape
     tiles = height // states
     cols = proj.shape[1]
@@ -276,7 +309,7 @@
     if last:
         (nxt, applied) = rest
     else:
-        (nxt, low, high, partial, applied, rounded) = rest
+        (nxt, low, high, partial, selected, applied) = rest
 
     named = names[...]
     if first:
@@ -285,7 +318,7 @@
 
         def store(q, p, same):
             z = p // cols
-            table[z, q - z * cols : q - z * cols + 128, p - z * cols : p - z * cols + 128] = same
+            table[z, q - z * cols : q - z * cols + 128, p - z * cols : p - z * cols + 128] = same.astype(F8)
 
         def wanted(q, p):
             return 0 <= q // cols - p // cols <= planes
@@ -293,15 +326,23 @@
         same_names(jnp.concatenate(around, axis=1), mine, store, wanted)
 
     terms = [read_terms(r, 2 * height, states, count) for r in (below, above)]
-    terms = doubled(jnp.concatenate(terms, axis=1))
+    terms, scale = in_pieces(jnp.concatenate(terms, axis=1))
     mask = block_mask(height, cols, states, slots)
+    used = jnp.where(named < NO_NAME, 1.0, 0.0)
+    out = [None] * planes
     for z in range(planes):
         at = slice(z * cols, (z + 1) * cols)
         chosen = lax.dot_general(terms[:, z * cols : z * cols + reach], table[z], NN, preferred_element_type=F32)
-        chosen = (chosen[:states] + share[:, at]) * (weight[:, at] * gain)
-        spread = jnp.broadcast_to(chosen[None], (tiles, states, cols)).reshape(height, cols)
-        spread = jnp.where(mask, spread, 0.0).astype(BF16)
-        applied[z] = lax.dot_general(spread, proj[z], NN, preferred_element_type=F32)
+        chosen = (chosen[:states] + chosen[states : 2 * states] + chosen[2 * states : 3 * states]) * scale
+        chosen = (chosen + share[:, at]) * (weight[:, at] * gain)
+        if not last:
+            selected[:, at] = chosen
+        if last or z not in inner_planes(planes):
+            applied[z] = applied_to(chosen, proj[z], tiles, mask)
+        else:
+            i = z - inner_planes(planes)[0]
+            of_chosen = lax.dot_general(doubled(chosen), square[i], NN, preferred_element_type=F32)
+            out[z] = (inner[:, i * cols : (i + 1) * cols] + of_chosen[:states]) * used[:, at]
 
     def pair_step(pair, carry):
         here = rows_at(pair, 2 * states)
@@ -311,6 +352,8 @@
             outer = {0: near * b1 + far * b2, 1: far * b1}
             outer.update({planes - 2: far * a1, planes - 1: near * a1 + far * a2})
             for z in range(planes):
+                if not last and z not in outer:
+                    continue
                 new = base[z, here, lane(y)] + applied[z, here, lane(y)]
                 if z in outer:
                     new += outer[z]
@@ -321,21 +364,20 @@
                     block = (plane * parts + pair // pairs) * CORES + slab
                     nxt[block, rows_at(pair % pairs, 2 * states), lane(y)] = new.astype(BF16)
                 else:
-                    nxt[z, here, lane(y)] = new
-                    rounded[z, here, lane(y)] = new.astype(BF16)
+                    i = z if z < 2 else z - planes + 4
+                    nxt[i, here, lane(y)] = new
+                    message = low if i < 2 else high
+                    message[rows_at(pair, 2 * states, i % 2 * height), lane(y)] = new.astype(BF16)
         return carry
 
     lax.fori_loop(0, tiles // 2, pair_step, 0)
     if not last:
-        used = jnp.where(named < NO_NAME, 1.0, 0.0)
-        out = []
         for z in range(planes):
-            at = slice(z * cols, (z + 1) * cols)
-            out.append(project(rounded[z], proj[z], states, slots) * used[:, at])
-            if z < 2:
-                low[z * height : (z + 1) * height, :] = rounded[z]
-            if z >= planes - 2:
-                high[(z - planes + 2) * height : (z - planes + 3) * height, :] = rounded[z]
+            if z in inner_planes(planes):
+                continue
+            i = z if z < 2 else z - planes + 4
+            plane = (low if i < 2 else high)[i % 2 * height : (i % 2 + 1) * height, :]
+            out[z] = project(plane, proj[z], states, slots) * used[:, z * cols : (z + 1) * cols]
         block = folded(jnp.concatenate(out, axis=1))
         partial[...] = block
         write_terms(low, 2 * height, block)
@@ -466,50 +508,49 @@
         flops=10**9, nbytes=8 * 2**20,
     )(core, mine, *ours, got, *others)
 
-    prev, cur = None, field
+    inside = len(inner_planes(planes))
+    prev, cur, outer = None, field, None
     for m in range(4):
         first, last = m == 0, m == 3
-        outs = [f32(shape), f32((share_states, count))]
-        args = [cur, shift, partial]
+        outs = [f32(shape), f32((share_states, count)), f32((share_states, inside * cols))]
         if first:
-            args = [core] + args + [names, strength.reshape(-1, 128)]
-            outs += [bf16((count, count)), f32((1, count))]
+            args = [core, cur, shift, partial, proj, names, strength.reshape(-1, 128)]
+            outs += [bf16((count, count)), f32((1, count)), bf16((inside, cols, cols))]
             made = call(
                 lambda *r: turn_kernel(sizes, True, *r), outs,
-                in_specs=[scalar] + [whole] * 5, flops=1e9, nbytes=8 * 2**20,
+                in_specs=[scalar] + [whole] * 6, flops=1e9, nbytes=8 * 2**20,
             )(*args)
             low, high, *made = lax.optimization_barrier((low, high, *made))
         below = passed_along(high, "ring", 1)
         above = passed_along(low, "ring", -1)
         if first:
-            base, share, own_table, weight = call(
+            base, share, inner, own_table, weight, square = call(
                 lambda *r: turn_kernel(sizes, False, *r), outs,
-                in_specs=[scalar] + [whole] * 9, flops=1e9, nbytes=8 * 2**20,
+                in_specs=[scalar] + [whole] * 12, flops=1e9, nbytes=8 * 2**20,
             )(*args, *made)
         else:
-            base, share = call(
-                lambda *r: local_kernel(sizes, False, *r), outs, flops=1e9, nbytes=8 * 2**20
-            )(*args, own_table, prev)
-        args = [base, share, below, above, weight, names, proj] + ([] if first else [table])
-        outs = [bf16((planes, (planes + 1) * cols, cols))] if first else []
-        scratch = [pltpu.VMEM(shape, F32)]
+            after, base, share, inner = call(
+                lambda *r: local_kernel(sizes, False, *r), [f32(shape)] + outs, flops=1e9, nbytes=8 * 2**20
+            )(outer, chosen, base, own_table, prev, shift, partial, proj)
+            prev, cur = cur, after
+        args = [base, share, below, above, weight, names, proj, inner, square] + ([] if first else [table])
+        outs = [jax.ShapeDtypeStruct((planes, (planes + 1) * cols, cols), F8)] if first else []
         if last:
             outs += [bf16((CORES * groups, planes * height // (CORES * groups), tile_cells))]
         else:
             made = sent(False)
-            outs += [f32(shape), made[1], made[2], made[0]]
-            scratch += [pltpu.VMEM(shape, BF16)]
+            outs += [f32((4, height, tile_cells)), made[1], made[2], made[0], f32((share_states, count))]
         got = call(
             lambda *r, first=first, last=last: step_kernel(sizes, first, last, *r),
-            outs, scratch=scratch, flops=1e9, nbytes=8 * 2**20,
+            outs, scratch=[pltpu.VMEM(shape, F32)], flops=1e9, nbytes=8 * 2**20,
         )(*args)
         if first:
             table, *got = got
         if last:
             (filtered,) = got
         else:
+            outer, low, high, partial, chosen = got
             prev = cur
-            cur, low, high, partial = got
 
     cells = lax.all_to_all(filtered, ("st", "core"), 0, 0, tiled=True)
     nstates = groups * local_states

time: 158 us -> 154 us (0.975)
  waiting for transfers between devices: 13.3 us -> 10.6 us
    pallas_call x4, Pallas kernels: 15.4 us -> 11 us  [per_device(): call(lambda *r, first=first, last=last: step_kernel(sizes, first, last, *...]
    pallas_call x3, Pallas kernels: 13.7 us -> 16.6 us  [per_device(): call(lambda *r: local_kernel(sizes, False, *r), [f32(shape)] + outs, flop...]
    ppermute x8, waiting for transfers between devices: 11.7 us -> 9.1 us  [passed_along(): lax.ppermute(array, axis, [(i, (i + by) % devices) for i in range(devices)])]
  transfers between devices with their start and end apart: 13 -> 13, of which waited for: 7 -> 4; matrix products, arithmetic and copies ran while one was open for 0% -> 0% of each run, Pallas kernels for 14% -> 16%
where the time goes in v5:
time: 154 us
  blocking collectives  76.2 us (49%)
  Pallas kernels  45 us (29%)
  starting transfers between devices  18.1 us (12%)
  waiting for transfers between devices  10.6 us (7%)
  local copies, waits for them, and re-layouts  1.99 us (1%)
  other arithmetic  1.99 us (1%)
    all_to_all x1, blocking collectives, per_device(): cells = lax.all_to_all(filtered, ('st', 'core'), 0, 0, tiled=True)  28.6 us
    all_to_all x1, blocking collectives, per_device(): rotated = lax.all_to_all(rotated, 'st', 0, 0, tiled=True)  20.7 us
    ppermute x8, starting transfers between devices, passed_along(): lax.ppermute(array, axis, [(i, (i + by) % devices) for i in range(devices)])  16.8 us
    pallas_call x3, Pallas kernels, per_device(): call(lambda *r: local_kernel(sizes, False, *r), [f32(shape)] + outs, flop...  16.6 us
    all_to_all x1, blocking collectives, per_device(): lax.all_to_all(jnp.broadcast_to(total, (devices, per, nstates)), everywhe...  13.8 us
    all_to_all x1, blocking collectives, per_device(): lax.all_to_all(part.reshape(devices, per, nstates), everywhere, 0, 0, til...  13.1 us
    pallas_call x4, Pallas kernels, per_device(): call(lambda *r, first=first, last=last: step_kernel(sizes, first, last, *...  11 us
    ppermute x8, waiting for transfers between devices, passed_along(): lax.ppermute(array, axis, [(i, (i + by) % devices) for i in range(devices)])  9.1 us
  transfers between devices with their start and end apart: 13, of which 4 were waited for; matrix products, arithmetic and copies ran while one was open for 0% of the time, Pallas kernels for 16%

profile of v5, /device:TPU:0, one launch (start us, length us, event | category | flops | bytes accessed | tf_op | source)
XLA Modules:
  0.0 154.2 jit_solution(1927849216067608845)
XLA Ops:
  0.0 1.8 %convert_element_type.5 = bf16[4,16,16,512]{3,2,1,0:T(8,128)(2,1)S(1)} convert(f32[4,16,16,512]{3,2,1,0:T(8,128)} %param.8) | non-fusion elementwise | flops 524288 | bytes 3145728 | tf_op jit(solution)/shard_map/convert_element_type | solution.py:491
  4.1 1.5 collective-permute-done.3.r_9_
  6.8 1.6 %collective-permute-start.5 = (bf16[304,512]{1,0:T(8,128)(2,1)S(1)}, bf16[304,512]{1,0:T(8,128)(2,1)S(1)}, u32[]{:S(2)}, u32[]{:S(2)}) collective-permute-start(bf16[304,512]{1,0:T(8,128)(2,1)S(1)} %get-tuple-element.86), channel_id=1, source_target_pairs={{0,16},{16,32},{32,48},{48,64},{64,80},{80,96},{96,112},{112,0},{1... | collective-permute-start | bytes 933896 | tf_op jit(solution)/shard_map/ppermute | solution.py:22
  8.4 2.6 %collective-permute-start.6 = (bf16[304,512]{1,0:T(8,128)(2,1)S(1)}, bf16[304,512]{1,0:T(8,128)(2,1)S(1)}, u32[]{:S(2)}, u32[]{:S(2)}) collective-permute-start(bf16[304,512]{1,0:T(8,128)(2,1)S(1)} %get-tuple-element.87), channel_id=1, source_target_pairs={{0,112},{16,0},{32,16},{48,32},{64,48},{80,64},{96,80},{112,96},{1... | collective-permute-start | bytes 933896 | tf_op jit(solution)/shard_map/ppermute | solution.py:22
  11.0 8.3 %shard_map.67 = (f32[8,128,512]{2,1,0:T(8,128)S(1)}, f32[8,2048]{1,0:T(8,128)S(1)}, f32[8,1024]{1,0:T(8,128)S(1)}, bf16[2048,2048]{1,0:T(8,128)(2,1)S(1)}, f32[1...) custom-call(s32[1]{0:T(128)} %bitcast.core.r_0_, f32[8,128,512]{2,1,0:T(8,128)S(1)} %get-tuple-element.65.r_1_.r_4_, ...), custom_call_target="tpu_custom_call" | custom-call | flops 1000000000 | bytes 8388608 | tf_op jit(solution)/shard_map/pallas_call | solution.py:527
  19.3 3.2 %shard_map.68 = (f8e4m3fn[8,2304,256]{2,1,0:T(32,128)(4,1)S(1)}, f32[4,128,512]{2,1,0:T(8,128)S(1)}, bf16[288,512]{1,0:T(8,128)(2,1)S(1)}, bf16[288,512]{1,0:T(8...) custom-call(f32[8,128,512]{2,1,0:T(8,128)S(1)} %get-tuple-element.84.r_0_.r_2_, ...), custom_call_target="tpu_custom_call" | custom-call | flops 1000000000 | bytes 8388608 | tf_op jit(solution)/shard_map/pallas_call | solution.py:543
  23.0 3.7 %collective-permute-start.8 = (bf16[288,512]{1,0:T(8,128)(2,1)S(1)}, bf16[288,512]{1,0:T(8,128)(2,1)S(1)}, u32[]{:S(2)}, u32[]{:S(2)}) collective-permute-start(bf16[288,512]{1,0:T(8,128)(2,1)S(1)} %get-tuple-element.98), channel_id=1, source_target_pairs={{0,112},{16,0},{32,16},{48,32},{64,48},{80,64},{96,80},{112,96},{1... | collective-permute-start | bytes 884744 | tf_op jit(solution)/shard_map/ppermute | solution.py:22
  26.7 5.3 %shard_map.69 = (f32[8,128,512]{2,1,0:T(8,128)S(1)}, f32[8,128,512]{2,1,0:T(8,128)S(1)}, f32[8,2048]{1,0:T(8,128)S(1)}, f32[8,1024]{1,0:T(8,128)S(1)}) custom-call(f32[4,128,512]{2,1,0:T(8,128)S(1)} %get-tuple-element.91.r_0_, f32[8,2048]{1,0:T(8,128)S(1)} %get-tuple-element.92.r_1_, f32[8,128,512]{2,1,0:T(8,128)S(1)} %get-tuple-element.84.r_0_.r_2_, ...), custom_call_target="tpu_custom_call" | custom-call | flops 1000000000 | bytes 8388608 | tf_op jit(solution)/shard_map/pallas_call | solution.py:532
  32.6 2.6 %shard_map.70 = (f32[4,128,512]{2,1,0:T(8,128)S(1)}, bf16[288,512]{1,0:T(8,128)(2,1)S(1)}, bf16[288,512]{1,0:T(8,128)(2,1)S(1)}, bf16[16,1024]{1,0:T(8,128)(2,1)S(1)}, f32[8,2048]{1,0:T(8,128)S(1)}) custom-call(f32[8,128,512]{2,1,0:T(8,128)S(1)} %get-tuple-element.95.r_0_.r_2_, f32[8,2048]{1,0:T(8,128)S(1)} %get-tuple-element.96.r_1_, ...), custom_call_target="tpu_custom_call" | custom-call | flops 1000000000 | bytes 8388608 | tf_op jit(solution)/shard_map/pallas_call | solution.py:543
  35.2 1.5 %collective-permute-start.9 = (bf16[288,512]{1,0:T(8,128)(2,1)S(1)}, bf16[288,512]{1,0:T(8,128)(2,1)S(1)}, u32[]{:S(2)}, u32[]{:S(2)}) collective-permute-start(bf16[288,512]{1,0:T(8,128)(2,1)S(1)} %get-tuple-element.107), channel_id=1, source_target_pairs={{0,16},{16,32},{32,48},{48,64},{64,80},{80,96},{96,112},{112,0},{1... | collective-permute-start | bytes 884744 | tf_op jit(solution)/shard_map/ppermute | solution.py:22
  36.7 2.7 %collective-permute-start.10 = (bf16[288,512]{1,0:T(8,128)(2,1)S(1)}, bf16[288,512]{1,0:T(8,128)(2,1)S(1)}, u32[]{:S(2)}, u32[]{:S(2)}) collective-permute-start(bf16[288,512]{1,0:T(8,128)(2,1)S(1)} %get-tuple-element.108), channel_id=1, source_target_pairs={{0,112},{16,0},{32,16},{48,32},{64,48},{80,64},{96,80},{112,96},{1... | collective-permute-start | bytes 884744 | tf_op jit(solution)/shard_map/ppermute | solution.py:22
  39.4 5.2 %shard_map.71 = (f32[8,128,512]{2,1,0:T(8,128)S(1)}, f32[8,128,512]{2,1,0:T(8,128)S(1)}, f32[8,2048]{1,0:T(8,128)S(1)}, f32[8,1024]{1,0:T(8,128)S(1)}) custom-call(f32[4,128,512]{2,1,0:T(8,128)S(1)} %get-tuple-element.101.r_0_, f32[8,2048]{1,0:T(8,128)S(1)} %get-tuple-element.102.r_1_, f32[8,128,512]{2,1,0:T(8,128)S(1)} %get-tuple-element.95.r_0_.r_2_, ...), custom_call_target="tpu_custom_call" | custom-call | flops 1000000000 | bytes 8388608 | tf_op jit(solution)/shard_map/pallas_call | solution.py:532
  44.7 3.3 %collective-permute-done.10.r_3_ = bf16[288,512]{1,0:T(8,128)(2,1)S(1)} collective-permute-done((bf16[288,512]{1,0:T(8,128)(2,1)S(1)}, bf16[288,512]{1,0:T(8,128)(2,1)S(1)}, u32[]{:S(2)}, u32[]{:S(2)}) %collective-permute-start.10) | collective-permute-done | bytes 294944 | tf_op jit(solution)/shard_map/ppermute | solution.py:22
  47.9 2.6 %shard_map.72 = (f32[4,128,512]{2,1,0:T(8,128)S(1)}, bf16[288,512]{1,0:T(8,128)(2,1)S(1)}, bf16[288,512]{1,0:T(8,128)(2,1)S(1)}, bf16[16,1024]{1,0:T(8,128)(2,1)S(1)}, f32[8,2048]{1,0:T(8,128)S(1)}) custom-call(f32[8,128,512]{2,1,0:T(8,128)S(1)} %get-tuple-element.105.r_0_.r_2_, f32[8,2048]{1,0:T(8,128)S(1)} %get-tuple-element.106.r_1_, ...), custom_call_target="tpu_custom_call" | custom-call | flops 1000000000 | bytes 8388608 | tf_op jit(solution)/shard_map/pallas_call | solution.py:543
  51.0 3.8 %collective-permute-start.12 = (bf16[288,512]{1,0:T(8,128)(2,1)S(1)}, bf16[288,512]{1,0:T(8,128)(2,1)S(1)}, u32[]{:S(2)}, u32[]{:S(2)}) collective-permute-start(bf16[288,512]{1,0:T(8,128)(2,1)S(1)} %get-tuple-element.117), channel_id=1, source_target_pairs={{0,112},{16,0},{32,16},{48,32},{64,48},{80,64},{96,80},{112,96},{1... | collective-permute-start | bytes 884744 | tf_op jit(solution)/shard_map/ppermute | solution.py:22
  54.8 6.0 %shard_map.73 = (f32[8,128,512]{2,1,0:T(8,128)}, f32[8,128,512]{2,1,0:T(8,128)S(1)}, f32[8,2048]{1,0:T(8,128)S(1)}, f32[8,1024]{1,0:T(8,128)S(1)}) custom-call(f32[4,128,512]{2,1,0:T(8,128)S(1)} %get-tuple-element.110.r_0_, f32[8,2048]{1,0:T(8,128)S(1)} %get-tuple-element.111.r_1_, f32[8,128,512]{2,1,0:T(8,128)S(1)} %get-tuple-element.105.r_0_.r_2_, ...), custom_call_target="tpu_custom_call" | custom-call | flops 1000000000 | bytes 8388608 | tf_op jit(solution)/shard_map/pallas_call | solution.py:532
  60.8 5.3 %collective-permute-done.12.r_3_ = bf16[288,512]{1,0:T(8,128)(2,1)S(1)} collective-permute-done((bf16[288,512]{1,0:T(8,128)(2,1)S(1)}, bf16[288,512]{1,0:T(8,128)(2,1)S(1)}, u32[]{:S(2)}, u32[]{:S(2)}) %collective-permute-start.12) | collective-permute-done | bytes 294944 | tf_op jit(solution)/shard_map/ppermute | solution.py:22
  66.1 2.5 %shard_map.74 = bf16[16,64,512]{2,1,0:T(8,128)(2,1)S(1)} custom-call(f32[8,128,512]{2,1,0:T(8,128)S(1)} %get-tuple-element.114.r_0_, f32[8,2048]{1,0:T(8,128)S(1)} %get-tuple-element.115.r_1_, bf16[288,512]{1,0:T(8,128)(2,1)S(1)} %collective-permute-done.11.r_2_, bf16[288,512]{1,0:T(8,128)(2,1)S(1)} %collective-permute-done.12.r_3_, ...), custom_call_target="tpu_custom_call" | custom-call | flops 1000000000 | bytes 8388608 | tf_op jit(solution)/shard_map/pallas_call | solution.py:543
  68.6 28.6 %all_to_all.20.r_0_ = bf16[16,64,512]{2,1,0:T(8,128)(2,1)S(1)} all-to-all(bf16[16,64,512]{2,1,0:T(8,128)(2,1)S(1)} %shard_map.74), channel_id=1, replica_groups=mesh['ring'=8,'core'=2,'st'=8] {'st','core'}, dimensions={0} | all-to-all | bytes 2097152 | tf_op jit(solution)/shard_map/all_to_all | solution.py:555
  97.7 13.1 %all_to_all.21 = f32[128,1,128]{2,1,0:T(1,128)S(1)} all-to-all(f32[128,1,128]{2,1,0:T(1,128)S(1)} %bitcast.20), channel_id=1, replica_groups=mesh['ring'=8,'core'=2,'st'=8] {'ring','core','st'}, dimensions={0} | all-to-all | bytes 131072 | tf_op jit(solution)/shard_map/all_to_all | solution.py:566
  111.0 13.8 %all_to_all.22 = f32[128,1,128]{2,1,0:T(1,128)S(1)} all-to-all(f32[128,1,128]{2,1,0:T(1,128)S(1)} %broadcast_in_dim.2), channel_id=1, replica_groups=mesh['ring'=8,'core'=2,'st'=8] {'ring','core','st'}, dimensions={0} | all-to-all | bytes 131072 | tf_op jit(solution)/shard_map/all_to_all | solution.py:568
  124.9 7.4 %shard_map.76 = bf16[8,32,16,128]{3,2,1,0:T(8,128)(2,1)S(1)} custom-call(f32[128,128]{1,0:T(8,128)S(1)} %bitcast.17, bf16[8,128,512]{2,1,0:T(8,128)(2,1)S(1)} %get-tuple-element.120.ordered), custom_call_target="tpu_custom_call" | custom-call | flops 200000000 | bytes 2097152 | tf_op jit(solution)/shard_map/pallas_call | solution.py:569
  132.3 20.7 %all_to_all.23 = bf16[8,32,16,128]{3,2,1,0:T(8,128)(2,1)S(1)} all-to-all(bf16[8,32,16,128]{3,2,1,0:T(8,128)(2,1)S(1)} %shard_map.76), channel_id=1, replica_groups=mesh['ring'=8,'core'=2,'st'=8] {'st'}, dimensions={0} | all-to-all | bytes 2097152 | tf_op jit(solution)/shard_map/all_to_all | solution.py:575
  152.9 1.2 copy.14
  (35 shorter events, 5.3 us)
Async XLA Ops:
  0.0 2.0 %copy-start.4 = (bf16[16,4,64,128]{3,2,1,0:T(8,128)(2,1)S(1)}, bf16[16,4,64,128]{3,2,1,0:T(8,128)(2,1)}, u32[]{:S(2)}) copy-start(bf16[16,4,64,128]{3,2,1,0:T(8,128)(2,1)} %param.6) | copy-start | bytes 3145732
  1.8 1.6 %copy-start.1 = (f32[4,64,128]{2,1,0:T(8,128)S(1)}, f32[4,64,128]{2,1,0:T(8,128)}, u32[]{:S(2)}) copy-start(f32[4,64,128]{2,1,0:T(8,128)} %r_5_.1) | copy-start | bytes 393220
  1.9 1.7 %copy-start.2 = (s32[4,16,16]{2,1,0:T(8,128)S(1)}, s32[4,16,16]{2,1,0:T(8,128)}, u32[]{:S(2)}) copy-start(s32[4,16,16]{2,1,0:T(8,128)} %r_3_.1) | copy-start | bytes 12292
  1.9 2.1 %copy-start.3 = (s32[4,16]{1,0:T(4,128)S(1)}, s32[4,16]{1,0:T(4,128)}, u32[]{:S(2)}) copy-start(s32[4,16]{1,0:T(4,128)} %r_4_.1) | copy-start | bytes 772
  1.9 3.7 %collective-permute-start.1 = (bf16[4,256,512]{2,1,0:T(8,128)(2,1)S(1)}, bf16[4,256,512]{2,1,0:T(8,128)(2,1)S(1)}, u32[]{:S(2)}, u32[]{:S(2)}) collective-permute-start(bf16[4,256,512]{2,1,0:T(8,128)(2,1)S(1)} %bitcast.15), channel_id=1, source_target_pairs={{0,8},{8,0},{1,9},{9,1},{2,10},{10,2},{3,11},{11,3},{4,12},{12,4},... | collective-permute-start | bytes 3145736 | tf_op jit(solution)/shard_map/ppermute | solution.py:488
  2.9 3.9 %copy-start = (f32[12288]{0:T(1024)S(1)}, f32[12288]{0:T(1024)}, u32[]{:S(2)}) copy-start(f32[12288]{0:T(1024)} %param.11) | copy-start | bytes 147460
  2.9 2.7 %collective-permute-start = (bf16[4,128,512]{2,1,0:T(8,128)(2,1)S(1)}, bf16[4,128,512]{2,1,0:T(8,128)(2,1)S(1)}, u32[]{:S(2)}, u32[]{:S(2)}) collective-permute-start(bf16[4,128,512]{2,1,0:T(8,128)(2,1)S(1)} %get-tuple-element.64), channel_id=1, source_target_pairs={{0,8},{8,0},{1,9},{9,1},{2,10},{10,2},{3,11},{11,3},{4,12},{12,4},... | collective-permute-start | bytes 1572872 | tf_op jit(solution)/shard_map/ppermute | solution.py:488
  3.5 2.1 %collective-permute-start.4 = (f32[4,64,128]{2,1,0:T(8,128)S(1)}, f32[4,64,128]{2,1,0:T(8,128)S(1)}, u32[]{:S(2)}, u32[]{:S(2)}) collective-permute-start(f32[4,64,128]{2,1,0:T(8,128)S(1)} %copy-done.1), channel_id=1, source_target_pairs={{0,8},{8,0},{1,9},{9,1},{2,10},{10,2},{3,11},{11,3},{4,12},{12,4},... | collective-permute-start | bytes 393224 | tf_op jit(solution)/shard_map/ppermute | solution.py:488
  3.6 2.0 %collective-permute-start.2 = (s32[4,16,16]{2,1,0:T(8,128)S(1)}, s32[4,16,16]{2,1,0:T(8,128)S(1)}, u32[]{:S(2)}, u32[]{:S(2)}) collective-permute-start(s32[4,16,16]{2,1,0:T(8,128)S(1)} %copy-done.2), channel_id=1, source_target_pairs={{0,8},{8,0},{1,9},{9,1},{2,10},{10,2},{3,11},{11,3},{4,12},{12,4},... | collective-permute-start | bytes 12296 | tf_op jit(solution)/shard_map/ppermute | solution.py:488
  4.0 1.6 %collective-permute-start.3 = (s32[4,16]{1,0:T(4,128)S(1)}, s32[4,16]{1,0:T(4,128)S(1)}, u32[]{:S(2)}, u32[]{:S(2)}) collective-permute-start(s32[4,16]{1,0:T(4,128)S(1)} %copy-done.3), channel_id=1, source_target_pairs={{0,8},{8,0},{1,9},{9,1},{2,10},{10,2},{3,11},{11,3},{4,12},{12,4},... | collective-permute-start | bytes 776 | tf_op jit(solution)/shard_map/ppermute | solution.py:488
  6.8 12.5 %collective-permute-start.5 = (bf16[304,512]{1,0:T(8,128)(2,1)S(1)}, bf16[304,512]{1,0:T(8,128)(2,1)S(1)}, u32[]{:S(2)}, u32[]{:S(2)}) collective-permute-start(bf16[304,512]{1,0:T(8,128)(2,1)S(1)} %get-tuple-element.86), channel_id=1, source_target_pairs={{0,16},{16,32},{32,48},{48,64},{64,80},{80,96},{96,112},{112,0},{1... | collective-permute-start | bytes 933896 | tf_op jit(solution)/shard_map/ppermute | solution.py:22
  8.4 10.8 %collective-permute-start.6 = (bf16[304,512]{1,0:T(8,128)(2,1)S(1)}, bf16[304,512]{1,0:T(8,128)(2,1)S(1)}, u32[]{:S(2)}, u32[]{:S(2)}) collective-permute-start(bf16[304,512]{1,0:T(8,128)(2,1)S(1)} %get-tuple-element.87), channel_id=1, source_target_pairs={{0,112},{16,0},{32,16},{48,32},{64,48},{80,64},{96,80},{112,96},{1... | collective-permute-start | bytes 933896 | tf_op jit(solution)/shard_map/ppermute | solution.py:22
  22.5 9.5 %collective-permute-start.7 = (bf16[288,512]{1,0:T(8,128)(2,1)S(1)}, bf16[288,512]{1,0:T(8,128)(2,1)S(1)}, u32[]{:S(2)}, u32[]{:S(2)}) collective-permute-start(bf16[288,512]{1,0:T(8,128)(2,1)S(1)} %get-tuple-element.97), channel_id=1, source_target_pairs={{0,16},{16,32},{32,48},{48,64},{64,80},{80,96},{96,112},{112,0},{1... | collective-permute-start | bytes 884744 | tf_op jit(solution)/shard_map/ppermute | solution.py:22
  23.0 9.6 %collective-permute-start.8 = (bf16[288,512]{1,0:T(8,128)(2,1)S(1)}, bf16[288,512]{1,0:T(8,128)(2,1)S(1)}, u32[]{:S(2)}, u32[]{:S(2)}) collective-permute-start(bf16[288,512]{1,0:T(8,128)(2,1)S(1)} %get-tuple-element.98), channel_id=1, source_target_pairs={{0,112},{16,0},{32,16},{48,32},{64,48},{80,64},{96,80},{112,96},{1... | collective-permute-start | bytes 884744 | tf_op jit(solution)/shard_map/ppermute | solution.py:22
  35.2 9.5 %collective-permute-start.9 = (bf16[288,512]{1,0:T(8,128)(2,1)S(1)}, bf16[288,512]{1,0:T(8,128)(2,1)S(1)}, u32[]{:S(2)}, u32[]{:S(2)}) collective-permute-start(bf16[288,512]{1,0:T(8,128)(2,1)S(1)} %get-tuple-element.107), channel_id=1, source_target_pairs={{0,16},{16,32},{32,48},{48,64},{64,80},{80,96},{96,112},{112,0},{1... | collective-permute-start | bytes 884744 | tf_op jit(solution)/shard_map/ppermute | solution.py:22
  36.7 11.2 %collective-permute-start.10 = (bf16[288,512]{1,0:T(8,128)(2,1)S(1)}, bf16[288,512]{1,0:T(8,128)(2,1)S(1)}, u32[]{:S(2)}, u32[]{:S(2)}) collective-permute-start(bf16[288,512]{1,0:T(8,128)(2,1)S(1)} %get-tuple-element.108), channel_id=1, source_target_pairs={{0,112},{16,0},{32,16},{48,32},{64,48},{80,64},{96,80},{112,96},{1... | collective-permute-start | bytes 884744 | tf_op jit(solution)/shard_map/ppermute | solution.py:22
  50.6 10.2 %collective-permute-start.11 = (bf16[288,512]{1,0:T(8,128)(2,1)S(1)}, bf16[288,512]{1,0:T(8,128)(2,1)S(1)}, u32[]{:S(2)}, u32[]{:S(2)}) collective-permute-start(bf16[288,512]{1,0:T(8,128)(2,1)S(1)} %get-tuple-element.116), channel_id=1, source_target_pairs={{0,16},{16,32},{32,48},{48,64},{64,80},{80,96},{96,112},{112,0},{1... | collective-permute-start | bytes 884744 | tf_op jit(solution)/shard_map/ppermute | solution.py:22
  51.0 15.1 %collective-permute-start.12 = (bf16[288,512]{1,0:T(8,128)(2,1)S(1)}, bf16[288,512]{1,0:T(8,128)(2,1)S(1)}, u32[]{:S(2)}, u32[]{:S(2)}) collective-permute-start(bf16[288,512]{1,0:T(8,128)(2,1)S(1)} %get-tuple-element.117), channel_id=1, source_target_pairs={{0,112},{16,0},{32,16},{48,32},{64,48},{80,64},{96,80},{112,96},{1... | collective-permute-start | bytes 884744 | tf_op jit(solution)/shard_map/ppermute | solution.py:22

commit v6 on v5

--- a/solution.py
+++ b/solution.py
@@ -48,7 +48,10 @@
 
 
 def project(field, proj, states, slots):
-    both = lax.dot_general(field, proj, NT, preferred_element_type=F32)
+    return of_tiles(lax.dot_general(field, proj, NT, preferred_element_type=F32), states, slots)
+
+
+def of_tiles(both, states, slots):
     both = jnp.where(block_mask(*both.shape, states, slots), both, 0.0)
     return jnp.sum(both.reshape(-1, states, both.shape[1]), axis=0)
 
@@ -111,21 +114,18 @@
 
 def first_kernel(sizes, core, *refs):
     states, slots, rows = sizes
-    ours, others = refs[0:5], refs[5:10]
-    field, proj, potential, names, partial, low, high = refs[10:]
-    planes, height, width = field.shape
-    half, cols, tiles = planes // 2, proj.shape[1], height // states
+    ours, others = refs[0:4], refs[4:8]
+    names, partial, low, high = refs[8:]
+    half, height, width = ours[0].shape
+    planes, cols, tiles = CORES * half, ours[1].shape[1], height // states
     rows_of = block_mask(tiles, cols, 1, slots)
     diagonal = block_mask(tiles, tiles, 1, 1)
     slot = (lax.broadcasted_iota(jnp.int32, (1, cols), 1) % slots).astype(F32)
-    digits = []
-    for (cells, proj_of, names_of, counts, potential_of), own in ((ours, True), (others, False)):
-        start = core[0] * half if own else (1 - core[0]) * half
+    digits, terms = [], []
+    for cells, proj_of, names_of, counts in (ours, others):
         found = []
         for z in range(half):
-            field[start + z] = cells[z].astype(F32)
-            proj[start + z] = proj_of[z]
-            potential[start + z] = potential_of[z]
+            terms.append(project(cells[z], proj_of[z], states, slots))
             name = names_of[z].astype(F32)
             top = jnp.floor(name * (1.0 / 128.0))
             count = jnp.broadcast_to(counts[z : z + 1, :].astype(F32), (tiles, tiles))
@@ -143,15 +143,13 @@
     named = top * 128.0 + bottom
     names[...] = named
     used = jnp.where(named < NO_NAME, 1.0, 0.0)
-    terms = []
-    for z in range(planes):
-        plane = field[z].astype(BF16)
-        at = slice(z * cols, (z + 1) * cols)
-        terms.append(project(plane, proj[z], states, slots) * used[:, at])
-        if z < 2:
-            low[z * height : (z + 1) * height, :] = plane
-        if z >= planes - 2:
-            high[(z - planes + 2) * height : (z - planes + 3) * height, :] = plane
+    mine, theirs = ours[0], others[0]
+    for z in range(2):
+        at = slice(z * height, (z + 1) * height)
+        low[at, :] = jnp.where(first, mine[z], theirs[z])
+        high[at, :] = jnp.where(first, theirs[half - 2 + z], mine[half - 2 + z])
+    terms = [jnp.where(first, terms[z], terms[(z + half) % planes]) for z in range(planes)]
+    terms = [terms[z] * used[:, z * cols : (z + 1) * cols] for z in range(planes)]
     block = folded(jnp.concatenate(terms, axis=1))
     partial[...] = block
     parts = named.shape[1] // width
@@ -172,6 +170,21 @@
 
 def doubled(terms):
     return jnp.concatenate([terms, terms], axis=0).astype(BF16)
+
+
+def in_pieces(terms):
+    largest = jnp.maximum(jnp.max(jnp.abs(terms), axis=1, keepdims=True), 1e-30)
+    rest = terms * (240.0 / largest)
+    pieces = []
+    for _ in range(3):
+        pieces.append(rest.astype(F8).astype(F32))
+        rest = rest - pieces[-1]
+    return jnp.concatenate(pieces + [jnp.zeros_like(terms)], axis=0).astype(F8), largest * (1.0 / 240.0)
+
+
+def from_pieces(sums, scale):
+    states = scale.shape[0]
+    return (sums[:states] + sums[states : 2 * states] + sums[2 * states : 3 * states]) * scale
 
 
 def look_up(strength, names):
@@ -201,12 +214,19 @@
     states, slots, rows = sizes
     refs = list(refs)
     if first:
-        cur, potential, own, proj, names, strength, base, share, inner, table, weight, square = refs
+        core, own, names, strength = refs[0], refs[7], refs[8], refs[9]
+        cur, potential, proj, base, share, inner, table, weight, square, turned = refs[10:]
+        half = refs[1].shape[0]
+        for start, (cells, values, proj_of) in ((core[0] * half, refs[1:4]), ((1 - core[0]) * half, refs[4:7])):
+            for z in range(half):
+                cur[start + z] = cells[z].astype(F32)
+                potential[start + z] = values[z]
+                proj[start + z] = proj_of[z]
         named = names[...]
         mine = jnp.where(named < NO_NAME, named, -1.0)
 
         def store(q, p, same):
-            table[q : q + 128, p : p + 128] = same.astype(BF16)
+            table[q : q + 128, p : p + 128] = same.astype(F8)
 
         same_names(named, mine, store, lambda q, p: True)
         weight[...] = look_up(strength[...], named)
@@ -216,13 +236,15 @@
     tiles, cols = height // states, proj.shape[1]
     gain = (1.0 if first else 2.0) / half_width
     near, far = -gain * 2.0 / 3.0, gain / 24.0
-    terms = doubled(unfolded(own[...]))
-    share[...] = lax.dot_general(terms, table[...], NN, preferred_element_type=F32)[:states]
+    terms, scale = in_pieces(unfolded(own[...]))
+    share[...] = from_pieces(lax.dot_general(terms, table[...], NN, preferred_element_type=F32), scale)
     if first:
         same_tile = block_mask(cols, cols, slots, slots)
         for i, z in enumerate(inner_planes(planes)):
             products = lax.dot_general(proj[z], proj[z], NT, preferred_element_type=F32)
             square[i] = jnp.where(same_tile, products, 0.0).astype(BF16)
+        for i, z in enumerate((0, 1, planes - 2, planes - 1)):
+            turned[i] = proj[z].astype(F32).T.astype(BF16)
     else:
         mask = block_mask(height, cols, states, slots)
         for z in range(planes):
@@ -268,12 +290,12 @@
 
 
 def turn_kernel(sizes, early, core, *refs):
-    inputs, refs = refs[:6], refs[6:]
-    made, refs = ([], refs) if early else (refs[:6], refs[6:])
+    inputs, refs = refs[:9], refs[9:]
+    made, refs = ([], refs) if early else (refs[:10], refs[10:])
 
     @pl.when((core[0] != 0) if early else (core[0] == 0))
     def _():
-        local_kernel(sizes, True, *inputs, *refs)
+        local_kernel(sizes, True, core, *inputs, *refs)
 
     if not early:
 
@@ -283,21 +305,11 @@
                 out[...] = ready[...]
 
 
-def in_pieces(terms):
-    largest = jnp.maximum(jnp.max(jnp.abs(terms), axis=1, keepdims=True), 1e-30)
-    rest = terms * (240.0 / largest)
-    pieces = []
-    for _ in range(3):
-        pieces.append(rest.astype(F8).astype(F32))
-        rest = rest - pieces[-1]
-    return jnp.concatenate(pieces + [jnp.zeros_like(terms)], axis=0).astype(F8), largest * (1.0 / 240.0)
-
-
 def step_kernel(sizes, first, last, *refs):
     states, slots, rows = sizes
     refs = list(refs)
-    base, share, below, above, weight, names, proj, inner, square = refs[:9]
-    rest = refs[9:]
+    base, share, below, above, weight, names, proj, inner, square, turned = refs[:10]
+    rest = refs[10:]
     planes, height, width = base.shape
     tiles = height // states
     cols = proj.shape[1]
@@ -333,7 +345,7 @@
     for z in range(planes):
         at = slice(z * cols, (z + 1) * cols)
         chosen = lax.dot_general(terms[:, z * cols : z * cols + reach], table[z], NN, preferred_element_type=F32)
-        chosen = (chosen[:states] + chosen[states : 2 * states] + chosen[2 * states : 3 * states]) * scale
+        chosen = from_pieces(chosen, scale)
         chosen = (chosen + share[:, at]) * (weight[:, at] * gain)
         if not last:
             selected[:, at] = chosen
@@ -377,7 +389,8 @@
                 continue
             i = z if z < 2 else z - planes + 4
             plane = (low if i < 2 else high)[i % 2 * height : (i % 2 + 1) * height, :]
-            out[z] = project(plane, proj[z], states, slots) * used[:, z * cols : (z + 1) * cols]
+            both = lax.dot_general(plane, turned[i], NN, preferred_element_type=F32)
+            out[z] = of_tiles(both, states, slots) * used[:, z * cols : (z + 1) * cols]
         block = folded(jnp.concatenate(out, axis=1))
         partial[...] = block
         write_terms(low, 2 * height, block)
@@ -399,12 +412,11 @@
 def recip(x):
     r = pltpu.reciprocal(x, approx=True)
     r = r * (2.0 - x * r)
-    return r * (2.0 - x * r)
+    return r
 
 def inverse_factor(margin, inverse):
     n = margin.shape[0]
     lanes = lax.broadcasted_iota(jnp.int32, (8, n), 1)
-    subs = lax.broadcasted_iota(jnp.int32, (8, n), 0)
     eye = lax.broadcasted_iota(jnp.int32, (n, n), 0) == lax.broadcasted_iota(jnp.int32, (n, n), 1)
     full = margin[...]
     diagonal = jnp.where(eye, full, 0.0)
@@ -412,49 +424,42 @@
     down = lax.rsqrt(jnp.sum(diagonal, axis=1, keepdims=True))
     full = full * down * across
     work = [full[8 * i : 8 * i + 8, :] for i in range(n // 8)]
-    for k in range(0, n, 4):
-        b, r = divmod(k, 8)
-        rows = [work[b][r + p : r + p + 1, :] for p in range(4)]
-        cols = [[jnp.broadcast_to(work[i][:, k + p : k + p + 1], (8, n)) for p in range(4)] for i in range(b, n // 8)]
-        entry = lambda p, q: jnp.broadcast_to(cols[0][q][r + p : r + p + 1, :], (8, n))
-        s = {(p, q): entry(p, q) for p in range(4) for q in range(p + 1)}
-        rows = [jnp.where(lanes == k + p, 1.0, jnp.where((lanes >= k) & (lanes < k + 4), 0.0, jnp.broadcast_to(rows[p], (8, n)))) for p in range(4)]
-        a, bb, c = s[0, 0], s[1, 0], s[1, 1]
-        det = recip(a * c - bb * bb)
-        i00, i01, i11 = c * det, -bb * det, a * det
-        x = {}
-        for q in (2, 3):
-            x[0, q] = i00 * s[q, 0] + i01 * s[q, 1]
-            x[1, q] = i01 * s[q, 0] + i11 * s[q, 1]
-        g22 = s[2, 2] - (s[2, 0] * x[0, 2] + s[2, 1] * x[1, 2])
-        g32 = s[3, 2] - (s[3, 0] * x[0, 2] + s[3, 1] * x[1, 2])
-        g33 = s[3, 3] - (s[3, 0] * x[0, 3] + s[3, 1] * x[1, 3])
-        det2 = recip(g22 * g33 - g32 * g32)
-        h00, h01, h11 = g33 * det2, -g32 * det2, g22 * det2
-        low2 = rows[2] - (x[0, 2] * rows[0] + x[1, 2] * rows[1])
-        low3 = rows[3] - (x[0, 3] * rows[0] + x[1, 3] * rows[1])
-        y2 = h00 * low2 + h01 * low3
-        y3 = h01 * low2 + h11 * low3
-        y0 = i00 * rows[0] + i01 * rows[1] - (x[0, 2] * y2 + x[0, 3] * y3)
-        y1 = i01 * rows[0] + i11 * rows[1] - (x[1, 2] * y2 + x[1, 3] * y3)
-        inside = (lanes >= k) & (lanes < k + 4)
-        for i in range(b, n // 8):
-            c4 = cols[i - b]
-            if i == b and r == 0:
-                c4 = [jnp.where(subs >= 4, v, 0.0) for v in c4]
-            elif i == b:
-                continue
-            change = (c4[0] * y0 + c4[1] * y1) + (c4[2] * y2 + c4[3] * y3)
+    for k in range(0, n, 8):
+        b = k // 8
+        wide = [jnp.broadcast_to(work[b][:, k + p : k + p + 1], (8, n)) for p in range(8)]
+        s = {(q, p): jnp.broadcast_to(wide[p][q : q + 1, :], (8, n)) for p in range(8) for q in range(p, 8)}
+        inside = (lanes >= k) & (lanes < k + 8)
+        rows = [
+            jnp.where(lanes == k + p, 1.0, jnp.where(inside, 0.0, jnp.broadcast_to(work[b][p : p + 1, :], (8, n))))
+            for p in range(8)
+        ]
+        solved, x = [None] * 8, {}
+        for p in range(0, 8, 2):
+            a, bb, c = s[p, p], s[p + 1, p], s[p + 1, p + 1]
+            det = recip(a * c - bb * bb)
+            i00, i01, i11 = c * det, -bb * det, a * det
+            for q in range(p + 2, 8):
+                x[p, q] = i00 * s[q, p] + i01 * s[q, p + 1]
+                x[p + 1, q] = i01 * s[q, p] + i11 * s[q, p + 1]
+            for q in range(p + 2, 8):
+                for w in range(p + 2, q + 1):
+                    s[q, w] = s[q, w] - (s[q, p] * x[p, w] + s[q, p + 1] * x[p + 1, w])
+                rows[q] = rows[q] - (x[p, q] * rows[p] + x[p + 1, q] * rows[p + 1])
+            solved[p] = i00 * rows[p] + i01 * rows[p + 1]
+            solved[p + 1] = i01 * rows[p] + i11 * rows[p + 1]
+            ratio = bb * recip(a)
+            out = [rows[p] * lax.rsqrt(a), (rows[p + 1] - ratio * rows[p]) * lax.rsqrt(c - bb * ratio)]
+            for i in range(2):
+                kept = jnp.where(lanes <= k + p + i, out[i], 0.0) * across
+                inverse[k + p + i : k + p + i + 1, :] = kept[0:1]
+        for p in (4, 2, 0):
+            for q in range(p + 2, 8):
+                solved[p] = solved[p] - x[p, q] * solved[q]
+                solved[p + 1] = solved[p + 1] - x[p + 1, q] * solved[q]
+        for i in range(b + 1, n // 8):
+            column = [jnp.broadcast_to(work[i][:, k + p : k + p + 1], (8, n)) * solved[p] for p in range(8)]
+            change = ((column[0] + column[1]) + (column[2] + column[3])) + ((column[4] + column[5]) + (column[6] + column[7]))
             work[i] = jnp.where(inside, 0.0, work[i]) - change
-        ra = recip(a)
-        l10 = bb * ra
-        d1 = c - bb * l10
-        rg = recip(g22)
-        l32 = g32 * rg
-        d3 = g33 - g32 * l32
-        out = [rows[0] * lax.rsqrt(a), (rows[1] - l10 * rows[0]) * lax.rsqrt(d1), low2 * lax.rsqrt(g22), (low3 - l32 * low2) * lax.rsqrt(d3)]
-        for p in range(4):
-            inverse[k + p : k + p + 1, :] = (jnp.where(lanes <= k + p, out[p], 0.0) * across)[0:1]
 
 def rotate_kernel(margin, ordered, rotated, inverse):
     inverse_factor(margin, inverse)
@@ -489,8 +494,9 @@
 
     core = lax.axis_index("core").astype(jnp.int32).reshape(1)
     proj_own = proj_values.reshape(slab_planes, cols, tile_cells).astype(BF16)
-    ours = [proj_own, block_list, tile_count, potential]
+    ours = [proj_own, block_list, tile_count]
     others = [swapped(array) for array in ours]
+    potential_others = swapped(potential)
     piece = bf16((slab_planes, height, tile_cells))
     mine, theirs = call(
         halves_kernel, (piece, piece), in_specs=[scalar, whole], flops=10**7, nbytes=2 * 2**20
@@ -501,39 +507,41 @@
         message = (2 * height + 4 * share_states + (16 if names else 0), tile_cells)
         return [bf16((2 * share_states, count // 2)), bf16(message), bf16(message)]
 
-    field, proj, shift, names, partial, low, high = call(
+    names, partial, low, high = call(
         lambda *r: first_kernel(sizes, *r),
-        [f32(shape), bf16((planes, cols, tile_cells)), f32((planes, rows_y, cells_x)), f32((1, count))] + sent(True),
-        in_specs=[scalar] + [whole] * 10,
+        [f32((1, count))] + sent(True),
+        in_specs=[scalar] + [whole] * 8,
         flops=10**9, nbytes=8 * 2**20,
     )(core, mine, *ours, got, *others)
 
     inside = len(inner_planes(planes))
-    prev, cur, outer = None, field, None
+    prev = cur = outer = None
     for m in range(4):
         first, last = m == 0, m == 3
         outs = [f32(shape), f32((share_states, count)), f32((share_states, inside * cols))]
         if first:
-            args = [core, cur, shift, partial, proj, names, strength.reshape(-1, 128)]
-            outs += [bf16((count, count)), f32((1, count)), bf16((inside, cols, cols))]
+            args = [core, mine, potential, ours[0], got, potential_others, others[0]]
+            args += [partial, names, strength.reshape(-1, 128)]
+            outs = [f32(shape), f32((planes, rows_y, cells_x)), bf16((planes, cols, tile_cells))] + outs
+            outs += [jax.ShapeDtypeStruct((count, count), F8), f32((1, count)), bf16((inside, cols, cols)), bf16((4, tile_cells, cols))]
             made = call(
                 lambda *r: turn_kernel(sizes, True, *r), outs,
-                in_specs=[scalar] + [whole] * 6, flops=1e9, nbytes=8 * 2**20,
+                in_specs=[scalar] + [whole] * 9, flops=1e9, nbytes=8 * 2**20,
             )(*args)
             low, high, *made = lax.optimization_barrier((low, high, *made))
         below = passed_along(high, "ring", 1)
         above = passed_along(low, "ring", -1)
         if first:
-            base, share, inner, own_table, weight, square = call(
+            cur, shift, proj, base, share, inner, own_table, weight, square, turned = call(
                 lambda *r: turn_kernel(sizes, False, *r), outs,
-                in_specs=[scalar] + [whole] * 12, flops=1e9, nbytes=8 * 2**20,
+                in_specs=[scalar] + [whole] * 19, flops=1e9, nbytes=8 * 2**20,
             )(*args, *made)
         else:
             after, base, share, inner = call(
                 lambda *r: local_kernel(sizes, False, *r), [f32(shape)] + outs, flops=1e9, nbytes=8 * 2**20
             )(outer, chosen, base, own_table, prev, shift, partial, proj)
             prev, cur = cur, after
-        args = [base, share, below, above, weight, names, proj, inner, square] + ([] if first else [table])
+        args = [base, share, below, above, weight, names, proj, inner, square, turned] + ([] if first else [table])
         outs = [jax.ShapeDtypeStruct((planes, (planes + 1) * cols, cols), F8)] if first else []
         if last:
             outs += [bf16((CORES * groups, planes * height // (CORES * groups), tile_cells))]

time: 154 us -> 152 us (0.987)
  Pallas kernels: 45 us -> 40.2 us
    pallas_call x1, Pallas kernels: 7.37 us -> 5.73 us  [per_device(): call(rotate_kernel, bf16((groups, slab_planes * rows_y // groups, local_s...]
  transfers between devices with their start and end apart: 13 -> 13, of which waited for: 4 -> 5; matrix products, arithmetic and copies ran while one was open for 0% -> 0% of each run, Pallas kernels for 16% -> 15%
where the time goes in v6:
time: 152 us
  blocking collectives  77.5 us (51%)
  Pallas kernels  40.2 us (26%)
  starting transfers between devices  18.1 us (12%)
  waiting for transfers between devices  11.9 us (8%)
  local copies, waits for them, and re-layouts  1.99 us (1%)
  other arithmetic  1.99 us (1%)
    all_to_all x1, blocking collectives, per_device(): cells = lax.all_to_all(filtered, ('st', 'core'), 0, 0, tiled=True)  28.5 us
    all_to_all x1, blocking collectives, per_device(): rotated = lax.all_to_all(rotated, 'st', 0, 0, tiled=True)  20.7 us
    ppermute x8, starting transfers between devices, passed_along(): lax.ppermute(array, axis, [(i, (i + by) % devices) for i in range(devices)])  16.8 us
    pallas_call x3, Pallas kernels, per_device(): call(lambda *r: local_kernel(sizes, False, *r), [f32(shape)] + outs, flop...  15.2 us
    all_to_all x1, blocking collectives, per_device(): lax.all_to_all(part.reshape(devices, per, nstates), everywhere, 0, 0, til...  14.5 us
    all_to_all x1, blocking collectives, per_device(): lax.all_to_all(jnp.broadcast_to(total, (devices, per, nstates)), everywhe...  13.8 us
    pallas_call x4, Pallas kernels, per_device(): call(lambda *r, first=first, last=last: step_kernel(sizes, first, last, *...  10.6 us
    ppermute x8, waiting for transfers between devices, passed_along(): lax.ppermute(array, axis, [(i, (i + by) % devices) for i in range(devices)])  10.4 us
  transfers between devices with their start and end apart: 13, of which 5 were waited for; matrix products, arithmetic and copies ran while one was open for 0% of the time, Pallas kernels for 15%

profile of v6, /device:TPU:0, one launch (start us, length us, event | category | flops | bytes accessed | tf_op | source)
XLA Modules:
  0.0 151.9 jit_solution(7997692722560536965)
XLA Ops:
  0.0 1.8 %convert_element_type.5 = bf16[4,16,16,512]{3,2,1,0:T(8,128)(2,1)S(1)} convert(f32[4,16,16,512]{3,2,1,0:T(8,128)} %param.8) | non-fusion elementwise | flops 524288 | bytes 3145728 | tf_op jit(solution)/shard_map/convert_element_type | solution.py:496
  6.6 1.7 %collective-permute-start.5 = (bf16[304,512]{1,0:T(8,128)(2,1)S(1)}, bf16[304,512]{1,0:T(8,128)(2,1)S(1)}, u32[]{:S(2)}, u32[]{:S(2)}) collective-permute-start(bf16[304,512]{1,0:T(8,128)(2,1)S(1)} %get-tuple-element.100), channel_id=1, source_target_pairs={{0,16},{16,32},{32,48},{48,64},{64,80},{80,96},{96,112},{112,0},{1... | collective-permute-start | bytes 933896 | tf_op jit(solution)/shard_map/ppermute | solution.py:22
  8.3 2.6 %collective-permute-start.6 = (bf16[304,512]{1,0:T(8,128)(2,1)S(1)}, bf16[304,512]{1,0:T(8,128)(2,1)S(1)}, u32[]{:S(2)}, u32[]{:S(2)}) collective-permute-start(bf16[304,512]{1,0:T(8,128)(2,1)S(1)} %get-tuple-element.101), channel_id=1, source_target_pairs={{0,112},{16,0},{32,16},{48,32},{64,48},{80,64},{96,80},{112,96},{1... | collective-permute-start | bytes 933896 | tf_op jit(solution)/shard_map/ppermute | solution.py:22
  10.8 7.1 %shard_map.67 = (f32[8,128,512]{2,1,0:T(8,128)S(1)}, f32[8,64,128]{2,1,0:T(8,128)S(1)}, bf16[8,256,512]{2,1,0:T(8,128)(2,1)S(1)}, f32[8,128,512]{2,1,0:T(8,128)S...) custom-call(s32[1]{0:T(128)} %bitcast.core.r_0_, ...), custom_call_target="tpu_custom_call" | custom-call | flops 1000000000 | bytes 8388608 | tf_op jit(solution)/shard_map/pallas_call | solution.py:535
  18.5 3.1 %shard_map.68 = (f8e4m3fn[8,2304,256]{2,1,0:T(32,128)(4,1)S(1)}, f32[4,128,512]{2,1,0:T(8,128)S(1)}, bf16[288,512]{1,0:T(8,128)(2,1)S(1)}, bf16[288,512]{1,0:T(8...) custom-call(f32[8,128,512]{2,1,0:T(8,128)S(1)} %get-tuple-element.98.r_0_.r_2_, ...), custom_call_target="tpu_custom_call" | custom-call | flops 1000000000 | bytes 8388608 | tf_op jit(solution)/shard_map/pallas_call | solution.py:551
  21.6 1.5 %collective-permute-start.7 = (bf16[288,512]{1,0:T(8,128)(2,1)S(1)}, bf16[288,512]{1,0:T(8,128)(2,1)S(1)}, u32[]{:S(2)}, u32[]{:S(2)}) collective-permute-start(bf16[288,512]{1,0:T(8,128)(2,1)S(1)} %get-tuple-element.115), channel_id=1, source_target_pairs={{0,16},{16,32},{32,48},{48,64},{64,80},{80,96},{96,112},{112,0},{1... | collective-permute-start | bytes 884744 | tf_op jit(solution)/shard_map/ppermute | solution.py:22
  23.2 2.7 %collective-permute-start.8 = (bf16[288,512]{1,0:T(8,128)(2,1)S(1)}, bf16[288,512]{1,0:T(8,128)(2,1)S(1)}, u32[]{:S(2)}, u32[]{:S(2)}) collective-permute-start(bf16[288,512]{1,0:T(8,128)(2,1)S(1)} %get-tuple-element.116), channel_id=1, source_target_pairs={{0,112},{16,0},{32,16},{48,32},{64,48},{80,64},{96,80},{112,96},{1... | collective-permute-start | bytes 884744 | tf_op jit(solution)/shard_map/ppermute | solution.py:22
  25.8 4.8 %shard_map.69 = (f32[8,128,512]{2,1,0:T(8,128)S(1)}, f32[8,128,512]{2,1,0:T(8,128)S(1)}, f32[8,2048]{1,0:T(8,128)S(1)}, f32[8,1024]{1,0:T(8,128)S(1)}) custom-call(f32[4,128,512]{2,1,0:T(8,128)S(1)} %get-tuple-element.107.r_0_, f32[8,2048]{1,0:T(8,128)S(1)} %get-tuple-element.108.r_1_, f32[8,128,512]{2,1,0:T(8,128)S(1)} %get-tuple-element.98.r_0_.r_2_, ...), custom_call_target="tpu_custom_call" | custom-call | flops 1000000000 | bytes 8388608 | tf_op jit(solution)/shard_map/pallas_call | solution.py:540
  30.6 3.2 %collective-permute-done.8.r_3_ = bf16[288,512]{1,0:T(8,128)(2,1)S(1)} collective-permute-done((bf16[288,512]{1,0:T(8,128)(2,1)S(1)}, bf16[288,512]{1,0:T(8,128)(2,1)S(1)}, u32[]{:S(2)}, u32[]{:S(2)}) %collective-permute-start.8) | collective-permute-done | bytes 294944 | tf_op jit(solution)/shard_map/ppermute | solution.py:22
  33.8 2.5 %shard_map.70 = (f32[4,128,512]{2,1,0:T(8,128)S(1)}, bf16[288,512]{1,0:T(8,128)(2,1)S(1)}, bf16[288,512]{1,0:T(8,128)(2,1)S(1)}, bf16[16,1024]{1,0:T(8,128)(2,1)S(1)}, f32[8,2048]{1,0:T(8,128)S(1)}) custom-call(f32[8,128,512]{2,1,0:T(8,128)S(1)} %get-tuple-element.113.r_0_.r_2_, f32[8,2048]{1,0:T(8,128)S(1)} %get-tuple-element.114.r_1_, ...), custom_call_target="tpu_custom_call" | custom-call | flops 1000000000 | bytes 8388608 | tf_op jit(solution)/shard_map/pallas_call | solution.py:551
  36.3 1.5 %collective-permute-start.9 = (bf16[288,512]{1,0:T(8,128)(2,1)S(1)}, bf16[288,512]{1,0:T(8,128)(2,1)S(1)}, u32[]{:S(2)}, u32[]{:S(2)}) collective-permute-start(bf16[288,512]{1,0:T(8,128)(2,1)S(1)} %get-tuple-element.125), channel_id=1, source_target_pairs={{0,16},{16,32},{32,48},{48,64},{64,80},{80,96},{96,112},{112,0},{1... | collective-permute-start | bytes 884744 | tf_op jit(solution)/shard_map/ppermute | solution.py:22
  37.9 2.7 %collective-permute-start.10 = (bf16[288,512]{1,0:T(8,128)(2,1)S(1)}, bf16[288,512]{1,0:T(8,128)(2,1)S(1)}, u32[]{:S(2)}, u32[]{:S(2)}) collective-permute-start(bf16[288,512]{1,0:T(8,128)(2,1)S(1)} %get-tuple-element.126), channel_id=1, source_target_pairs={{0,112},{16,0},{32,16},{48,32},{64,48},{80,64},{96,80},{112,96},{1... | collective-permute-start | bytes 884744 | tf_op jit(solution)/shard_map/ppermute | solution.py:22
  40.5 4.8 %shard_map.71 = (f32[8,128,512]{2,1,0:T(8,128)S(1)}, f32[8,128,512]{2,1,0:T(8,128)S(1)}, f32[8,2048]{1,0:T(8,128)S(1)}, f32[8,1024]{1,0:T(8,128)S(1)}) custom-call(f32[4,128,512]{2,1,0:T(8,128)S(1)} %get-tuple-element.119.r_0_, f32[8,2048]{1,0:T(8,128)S(1)} %get-tuple-element.120.r_1_, f32[8,128,512]{2,1,0:T(8,128)S(1)} %get-tuple-element.113.r_0_.r_2_, ...), custom_call_target="tpu_custom_call" | custom-call | flops 1000000000 | bytes 8388608 | tf_op jit(solution)/shard_map/pallas_call | solution.py:540
  45.3 4.0 %collective-permute-done.10.r_3_ = bf16[288,512]{1,0:T(8,128)(2,1)S(1)} collective-permute-done((bf16[288,512]{1,0:T(8,128)(2,1)S(1)}, bf16[288,512]{1,0:T(8,128)(2,1)S(1)}, u32[]{:S(2)}, u32[]{:S(2)}) %collective-permute-start.10) | collective-permute-done | bytes 294944 | tf_op jit(solution)/shard_map/ppermute | solution.py:22
  49.3 2.5 %shard_map.72 = (f32[4,128,512]{2,1,0:T(8,128)S(1)}, bf16[288,512]{1,0:T(8,128)(2,1)S(1)}, bf16[288,512]{1,0:T(8,128)(2,1)S(1)}, bf16[16,1024]{1,0:T(8,128)(2,1)S(1)}, f32[8,2048]{1,0:T(8,128)S(1)}) custom-call(f32[8,128,512]{2,1,0:T(8,128)S(1)} %get-tuple-element.123.r_0_.r_2_, f32[8,2048]{1,0:T(8,128)S(1)} %get-tuple-element.124.r_1_, ...), custom_call_target="tpu_custom_call" | custom-call | flops 1000000000 | bytes 8388608 | tf_op jit(solution)/shard_map/pallas_call | solution.py:551
  53.3 2.7 %collective-permute-start.12 = (bf16[288,512]{1,0:T(8,128)(2,1)S(1)}, bf16[288,512]{1,0:T(8,128)(2,1)S(1)}, u32[]{:S(2)}, u32[]{:S(2)}) collective-permute-start(bf16[288,512]{1,0:T(8,128)(2,1)S(1)} %get-tuple-element.135), channel_id=1, source_target_pairs={{0,112},{16,0},{32,16},{48,32},{64,48},{80,64},{96,80},{112,96},{1... | collective-permute-start | bytes 884744 | tf_op jit(solution)/shard_map/ppermute | solution.py:22
  56.0 5.6 %shard_map.73 = (f32[8,128,512]{2,1,0:T(8,128)}, f32[8,128,512]{2,1,0:T(8,128)S(1)}, f32[8,2048]{1,0:T(8,128)S(1)}, f32[8,1024]{1,0:T(8,128)S(1)}) custom-call(f32[4,128,512]{2,1,0:T(8,128)S(1)} %get-tuple-element.128.r_0_, f32[8,2048]{1,0:T(8,128)S(1)} %get-tuple-element.129.r_1_, f32[8,128,512]{2,1,0:T(8,128)S(1)} %get-tuple-element.123.r_0_.r_2_, ...), custom_call_target="tpu_custom_call" | custom-call | flops 1000000000 | bytes 8388608 | tf_op jit(solution)/shard_map/pallas_call | solution.py:540
  61.6 2.7 %collective-permute-done.12.r_3_ = bf16[288,512]{1,0:T(8,128)(2,1)S(1)} collective-permute-done((bf16[288,512]{1,0:T(8,128)(2,1)S(1)}, bf16[288,512]{1,0:T(8,128)(2,1)S(1)}, u32[]{:S(2)}, u32[]{:S(2)}) %collective-permute-start.12) | collective-permute-done | bytes 294944 | tf_op jit(solution)/shard_map/ppermute | solution.py:22
  64.3 2.5 %shard_map.74 = bf16[16,64,512]{2,1,0:T(8,128)(2,1)S(1)} custom-call(f32[8,128,512]{2,1,0:T(8,128)S(1)} %get-tuple-element.132.r_0_, f32[8,2048]{1,0:T(8,128)S(1)} %get-tuple-element.133.r_1_, bf16[288,512]{1,0:T(8,128)(2,1)S(1)} %collective-permute-done.11.r_2_, bf16[288,512]{1,0:T(8,128)(2,1)S(1)} %collective-permute-done.12.r_3_, ...), custom_call_target="tpu_custom_call" | custom-call | flops 1000000000 | bytes 8388608 | tf_op jit(solution)/shard_map/pallas_call | solution.py:551
  66.8 28.5 %all_to_all.20.r_0_ = bf16[16,64,512]{2,1,0:T(8,128)(2,1)S(1)} all-to-all(bf16[16,64,512]{2,1,0:T(8,128)(2,1)S(1)} %shard_map.74), channel_id=1, replica_groups=mesh['ring'=8,'core'=2,'st'=8] {'st','core'}, dimensions={0} | all-to-all | bytes 2097152 | tf_op jit(solution)/shard_map/all_to_all | solution.py:563
  95.8 14.5 %all_to_all.21 = f32[128,1,128]{2,1,0:T(1,128)S(1)} all-to-all(f32[128,1,128]{2,1,0:T(1,128)S(1)} %bitcast.20), channel_id=1, replica_groups=mesh['ring'=8,'core'=2,'st'=8] {'ring','core','st'}, dimensions={0} | all-to-all | bytes 131072 | tf_op jit(solution)/shard_map/all_to_all | solution.py:574
  110.4 13.8 %all_to_all.22 = f32[128,1,128]{2,1,0:T(1,128)S(1)} all-to-all(f32[128,1,128]{2,1,0:T(1,128)S(1)} %broadcast_in_dim.2), channel_id=1, replica_groups=mesh['ring'=8,'core'=2,'st'=8] {'ring','core','st'}, dimensions={0} | all-to-all | bytes 131072 | tf_op jit(solution)/shard_map/all_to_all | solution.py:576
  124.3 5.7 %shard_map.76 = bf16[8,32,16,128]{3,2,1,0:T(8,128)(2,1)S(1)} custom-call(f32[128,128]{1,0:T(8,128)S(1)} %bitcast.19, bf16[8,128,512]{2,1,0:T(8,128)(2,1)S(1)} %get-tuple-element.138.ordered), custom_call_target="tpu_custom_call" | custom-call | flops 200000000 | bytes 2097152 | tf_op jit(solution)/shard_map/pallas_call | solution.py:577
  130.0 20.7 %all_to_all.23 = bf16[8,32,16,128]{3,2,1,0:T(8,128)(2,1)S(1)} all-to-all(bf16[8,32,16,128]{3,2,1,0:T(8,128)(2,1)S(1)} %shard_map.76), channel_id=1, replica_groups=mesh['ring'=8,'core'=2,'st'=8] {'st'}, dimensions={0} | all-to-all | bytes 2097152 | tf_op jit(solution)/shard_map/all_to_all | solution.py:583
  (35 shorter events, 8.6 us)
Async XLA Ops:
  0.0 2.0 %copy-start.4 = (bf16[16,4,64,128]{3,2,1,0:T(8,128)(2,1)S(1)}, bf16[16,4,64,128]{3,2,1,0:T(8,128)(2,1)}, u32[]{:S(2)}) copy-start(bf16[16,4,64,128]{3,2,1,0:T(8,128)(2,1)} %param.6) | copy-start | bytes 3145732
  1.8 1.6 %copy-start = (f32[4,64,128]{2,1,0:T(8,128)S(1)}, f32[4,64,128]{2,1,0:T(8,128)}, u32[]{:S(2)}) copy-start(f32[4,64,128]{2,1,0:T(8,128)} %r_2_.3) | copy-start | bytes 393220
  1.9 1.7 %copy-start.2 = (s32[4,16,16]{2,1,0:T(8,128)S(1)}, s32[4,16,16]{2,1,0:T(8,128)}, u32[]{:S(2)}) copy-start(s32[4,16,16]{2,1,0:T(8,128)} %r_3_.1) | copy-start | bytes 12292
  1.9 2.1 %copy-start.3 = (s32[4,16]{1,0:T(4,128)S(1)}, s32[4,16]{1,0:T(4,128)}, u32[]{:S(2)}) copy-start(s32[4,16]{1,0:T(4,128)} %r_4_.1) | copy-start | bytes 772
  1.9 3.7 %collective-permute-start.2 = (bf16[4,256,512]{2,1,0:T(8,128)(2,1)S(1)}, bf16[4,256,512]{2,1,0:T(8,128)(2,1)S(1)}, u32[]{:S(2)}, u32[]{:S(2)}) collective-permute-start(bf16[4,256,512]{2,1,0:T(8,128)(2,1)S(1)} %bitcast.14), channel_id=1, source_target_pairs={{0,8},{8,0},{1,9},{9,1},{2,10},{10,2},{3,11},{11,3},{4,12},{12,4},... | collective-permute-start | bytes 3145736 | tf_op jit(solution)/shard_map/ppermute | solution.py:493
  2.9 3.7 %copy-start.1 = (f32[12288]{0:T(1024)S(1)}, f32[12288]{0:T(1024)}, u32[]{:S(2)}) copy-start(f32[12288]{0:T(1024)} %param.11) | copy-start | bytes 147460
  2.9 2.7 %collective-permute-start = (bf16[4,128,512]{2,1,0:T(8,128)(2,1)S(1)}, bf16[4,128,512]{2,1,0:T(8,128)(2,1)S(1)}, u32[]{:S(2)}, u32[]{:S(2)}) collective-permute-start(bf16[4,128,512]{2,1,0:T(8,128)(2,1)S(1)} %get-tuple-element.73), channel_id=1, source_target_pairs={{0,8},{8,0},{1,9},{9,1},{2,10},{10,2},{3,11},{11,3},{4,12},{12,4},... | collective-permute-start | bytes 1572872 | tf_op jit(solution)/shard_map/ppermute | solution.py:493
  3.5 3.1 %collective-permute-start.1 = (f32[4,64,128]{2,1,0:T(8,128)S(1)}, f32[4,64,128]{2,1,0:T(8,128)S(1)}, u32[]{:S(2)}, u32[]{:S(2)}) collective-permute-start(f32[4,64,128]{2,1,0:T(8,128)S(1)} %copy-done), channel_id=1, source_target_pairs={{0,8},{8,0},{1,9},{9,1},{2,10},{10,2},{3,11},{11,3},{4,12},{12,4},... | collective-permute-start | bytes 393224 | tf_op jit(solution)/shard_map/ppermute | solution.py:493
  3.6 2.0 %collective-permute-start.3 = (s32[4,16,16]{2,1,0:T(8,128)S(1)}, s32[4,16,16]{2,1,0:T(8,128)S(1)}, u32[]{:S(2)}, u32[]{:S(2)}) collective-permute-start(s32[4,16,16]{2,1,0:T(8,128)S(1)} %copy-done.2), channel_id=1, source_target_pairs={{0,8},{8,0},{1,9},{9,1},{2,10},{10,2},{3,11},{11,3},{4,12},{12,4},... | collective-permute-start | bytes 12296 | tf_op jit(solution)/shard_map/ppermute | solution.py:493
  4.0 1.6 %collective-permute-start.4 = (s32[4,16]{1,0:T(4,128)S(1)}, s32[4,16]{1,0:T(4,128)S(1)}, u32[]{:S(2)}, u32[]{:S(2)}) collective-permute-start(s32[4,16]{1,0:T(4,128)S(1)} %copy-done.3), channel_id=1, source_target_pairs={{0,8},{8,0},{1,9},{9,1},{2,10},{10,2},{3,11},{11,3},{4,12},{12,4},... | collective-permute-start | bytes 776 | tf_op jit(solution)/shard_map/ppermute | solution.py:493
  6.6 11.3 %collective-permute-start.5 = (bf16[304,512]{1,0:T(8,128)(2,1)S(1)}, bf16[304,512]{1,0:T(8,128)(2,1)S(1)}, u32[]{:S(2)}, u32[]{:S(2)}) collective-permute-start(bf16[304,512]{1,0:T(8,128)(2,1)S(1)} %get-tuple-element.100), channel_id=1, source_target_pairs={{0,16},{16,32},{32,48},{48,64},{64,80},{80,96},{96,112},{112,0},{1... | collective-permute-start | bytes 933896 | tf_op jit(solution)/shard_map/ppermute | solution.py:22
  8.3 10.3 %collective-permute-start.6 = (bf16[304,512]{1,0:T(8,128)(2,1)S(1)}, bf16[304,512]{1,0:T(8,128)(2,1)S(1)}, u32[]{:S(2)}, u32[]{:S(2)}) collective-permute-start(bf16[304,512]{1,0:T(8,128)(2,1)S(1)} %get-tuple-element.101), channel_id=1, source_target_pairs={{0,112},{16,0},{32,16},{48,32},{64,48},{80,64},{96,80},{112,96},{1... | collective-permute-start | bytes 933896 | tf_op jit(solution)/shard_map/ppermute | solution.py:22
  21.6 9.0 %collective-permute-start.7 = (bf16[288,512]{1,0:T(8,128)(2,1)S(1)}, bf16[288,512]{1,0:T(8,128)(2,1)S(1)}, u32[]{:S(2)}, u32[]{:S(2)}) collective-permute-start(bf16[288,512]{1,0:T(8,128)(2,1)S(1)} %get-tuple-element.115), channel_id=1, source_target_pairs={{0,16},{16,32},{32,48},{48,64},{64,80},{80,96},{96,112},{112,0},{1... | collective-permute-start | bytes 884744 | tf_op jit(solution)/shard_map/ppermute | solution.py:22
  23.2 10.7 %collective-permute-start.8 = (bf16[288,512]{1,0:T(8,128)(2,1)S(1)}, bf16[288,512]{1,0:T(8,128)(2,1)S(1)}, u32[]{:S(2)}, u32[]{:S(2)}) collective-permute-start(bf16[288,512]{1,0:T(8,128)(2,1)S(1)} %get-tuple-element.116), channel_id=1, source_target_pairs={{0,112},{16,0},{32,16},{48,32},{64,48},{80,64},{96,80},{112,96},{1... | collective-permute-start | bytes 884744 | tf_op jit(solution)/shard_map/ppermute | solution.py:22
  36.3 9.0 %collective-permute-start.9 = (bf16[288,512]{1,0:T(8,128)(2,1)S(1)}, bf16[288,512]{1,0:T(8,128)(2,1)S(1)}, u32[]{:S(2)}, u32[]{:S(2)}) collective-permute-start(bf16[288,512]{1,0:T(8,128)(2,1)S(1)} %get-tuple-element.125), channel_id=1, source_target_pairs={{0,16},{16,32},{32,48},{48,64},{64,80},{80,96},{96,112},{112,0},{1... | collective-permute-start | bytes 884744 | tf_op jit(solution)/shard_map/ppermute | solution.py:22
  37.9 11.5 %collective-permute-start.10 = (bf16[288,512]{1,0:T(8,128)(2,1)S(1)}, bf16[288,512]{1,0:T(8,128)(2,1)S(1)}, u32[]{:S(2)}, u32[]{:S(2)}) collective-permute-start(bf16[288,512]{1,0:T(8,128)(2,1)S(1)} %get-tuple-element.126), channel_id=1, source_target_pairs={{0,112},{16,0},{32,16},{48,32},{64,48},{80,64},{96,80},{112,96},{1... | collective-permute-start | bytes 884744 | tf_op jit(solution)/shard_map/ppermute | solution.py:22
  51.8 9.8 %collective-permute-start.11 = (bf16[288,512]{1,0:T(8,128)(2,1)S(1)}, bf16[288,512]{1,0:T(8,128)(2,1)S(1)}, u32[]{:S(2)}, u32[]{:S(2)}) collective-permute-start(bf16[288,512]{1,0:T(8,128)(2,1)S(1)} %get-tuple-element.134), channel_id=1, source_target_pairs={{0,16},{16,32},{32,48},{48,64},{64,80},{80,96},{96,112},{112,0},{1... | collective-permute-start | bytes 884744 | tf_op jit(solution)/shard_map/ppermute | solution.py:22
  53.3 11.0 %collective-permute-start.12 = (bf16[288,512]{1,0:T(8,128)(2,1)S(1)}, bf16[288,512]{1,0:T(8,128)(2,1)S(1)}, u32[]{:S(2)}, u32[]{:S(2)}) collective-permute-start(bf16[288,512]{1,0:T(8,128)(2,1)S(1)} %get-tuple-element.135), channel_id=1, source_target_pairs={{0,112},{16,0},{32,16},{48,32},{64,48},{80,64},{96,80},{112,96},{1... | collective-permute-start | bytes 884744 | tf_op jit(solution)/shard_map/ppermute | solution.py:22

commit v7 on v6

--- a/solution.py
+++ b/solution.py
@@ -22,7 +22,7 @@
     return lax.ppermute(array, axis, [(i, (i + by) % devices) for i in range(devices)])
 
 
-def call(kernel, out_shape, scratch=(), vmem=20, flops=0, nbytes=0, **specs):
+def call(kernel, out_shape, scratch=(), vmem=12, flops=0, nbytes=0, **specs):
     return pl.pallas_call(
         kernel,
         out_shape=out_shape,
@@ -150,8 +150,9 @@
         high[at, :] = jnp.where(first, theirs[half - 2 + z], mine[half - 2 + z])
     terms = [jnp.where(first, terms[z], terms[(z + half) % planes]) for z in range(planes)]
     terms = [terms[z] * used[:, z * cols : (z + 1) * cols] for z in range(planes)]
-    block = folded(jnp.concatenate(terms, axis=1))
-    partial[...] = block
+    terms = jnp.concatenate(terms, axis=1)
+    partial[...] = terms
+    block = folded(terms)
     parts = named.shape[1] // width
     lines = [v[:, i * width : (i + 1) * width] for v in (top, bottom) for i in range(parts)]
     lines = jnp.concatenate(lines + [jnp.zeros((16 - 2 * parts, width), F32)], axis=0).astype(BF16)
@@ -226,7 +227,7 @@
         mine = jnp.where(named < NO_NAME, named, -1.0)
 
         def store(q, p, same):
-            table[q : q + 128, p : p + 128] = same.astype(F8)
+            table[q : q + 128, p : p + 128] = same.astype(BF16)
 
         same_names(named, mine, store, lambda q, p: True)
         weight[...] = look_up(strength[...], named)
@@ -236,8 +237,13 @@
     tiles, cols = height // states, proj.shape[1]
     gain = (1.0 if first else 2.0) / half_width
     near, far = -gain * 2.0 / 3.0, gain / 24.0
-    terms, scale = in_pieces(unfolded(own[...]))
-    share[...] = from_pieces(lax.dot_general(terms, table[...], NN, preferred_element_type=F32), scale)
+    rest, pieces = own[...], []
+    for _ in range(3):
+        pieces.append(rest.astype(BF16).astype(F32))
+        rest = rest - pieces[-1]
+    terms = jnp.concatenate(pieces + [jnp.zeros_like(rest)], axis=0).astype(BF16)
+    sums = lax.dot_general(terms, table[...], NN, preferred_element_type=F32)
+    share[...] = sums[:states] + sums[states : 2 * states] + sums[2 * states : 3 * states]
     if first:
         same_tile = block_mask(cols, cols, slots, slots)
         for i, z in enumerate(inner_planes(planes)):
@@ -391,8 +397,9 @@
             plane = (low if i < 2 else high)[i % 2 * height : (i % 2 + 1) * height, :]
             both = lax.dot_general(plane, turned[i], NN, preferred_element_type=F32)
             out[z] = of_tiles(both, states, slots) * used[:, z * cols : (z + 1) * cols]
-        block = folded(jnp.concatenate(out, axis=1))
-        partial[...] = block
+        out = jnp.concatenate(out, axis=1)
+        partial[...] = out
+        block = folded(out)
         write_terms(low, 2 * height, block)
         write_terms(high, 2 * height, block)
 
@@ -505,7 +512,7 @@
 
     def sent(names):
         message = (2 * height + 4 * share_states + (16 if names else 0), tile_cells)
-        return [bf16((2 * share_states, count // 2)), bf16(message), bf16(message)]
+        return [f32((share_states, count)), bf16(message), bf16(message)]
 
     names, partial, low, high = call(
         lambda *r: first_kernel(sizes, *r),
@@ -523,7 +530,7 @@
             args = [core, mine, potential, ours[0], got, potential_others, others[0]]
             args += [partial, names, strength.reshape(-1, 128)]
             outs = [f32(shape), f32((planes, rows_y, cells_x)), bf16((planes, cols, tile_cells))] + outs
-            outs += [jax.ShapeDtypeStruct((count, count), F8), f32((1, count)), bf16((inside, cols, cols)), bf16((4, tile_cells, cols))]
+            outs += [bf16((count, count)), f32((1, count)), bf16((inside, cols, cols)), bf16((4, tile_cells, cols))]
             made = call(
                 lambda *r: turn_kernel(sizes, True, *r), outs,
                 in_specs=[scalar] + [whole] * 9, flops=1e9, nbytes=8 * 2**20,

time: 152 us -> 151 us (level)
  waiting for transfers between devices: 11.9 us -> 7.97 us
  Pallas kernels: 40.2 us -> 44.1 us
    ppermute x8, waiting for transfers between devices: 10.4 us -> 6.44 us  [passed_along(): lax.ppermute(array, axis, [(i, (i + by) % devices) for i in range(devices)])]
    pallas_call x3, Pallas kernels: 15.2 us -> 17.7 us  [per_device(): call(lambda *r: local_kernel(sizes, False, *r), [f32(shape)] + outs, flop...]
  transfers between devices with their start and end apart: 13 -> 13, of which waited for: 5 -> 3; matrix products, arithmetic and copies ran while one was open for 0% -> 0% of each run, Pallas kernels for 15% -> 18%
where the time goes in v7:
time: 151 us
  blocking collectives  76.8 us (51%)
  Pallas kernels  44.1 us (29%)
  starting transfers between devices  18.1 us (12%)
  waiting for transfers between devices  7.97 us (5%)
  local copies, waits for them, and re-layouts  1.99 us (1%)
  other arithmetic  1.99 us (1%)
    all_to_all x1, blocking collectives, per_device(): cells = lax.all_to_all(filtered, ('st', 'core'), 0, 0, tiled=True)  29.1 us
    all_to_all x1, blocking collectives, per_device(): rotated = lax.all_to_all(rotated, 'st', 0, 0, tiled=True)  20.6 us
    pallas_call x3, Pallas kernels, per_device(): call(lambda *r: local_kernel(sizes, False, *r), [f32(shape)] + outs, flop...  17.7 us
    ppermute x8, starting transfers between devices, passed_along(): lax.ppermute(array, axis, [(i, (i + by) % devices) for i in range(devices)])  16.8 us
    all_to_all x1, blocking collectives, per_device(): lax.all_to_all(jnp.broadcast_to(total, (devices, per, nstates)), everywhe...  13.9 us
    all_to_all x1, blocking collectives, per_device(): lax.all_to_all(part.reshape(devices, per, nstates), everywhere, 0, 0, til...  13.1 us
    pallas_call x4, Pallas kernels, per_device(): call(lambda *r, first=first, last=last: step_kernel(sizes, first, last, *...  10.6 us
    pallas_call x1, Pallas kernels, per_device(): call(lambda *r: turn_kernel(sizes, False, *r), outs, in_specs=[scalar] +...  8.54 us
  transfers between devices with their start and end apart: 13, of which 3 were waited for; matrix products, arithmetic and copies ran while one was open for 0% of the time, Pallas kernels for 18%

profile of v7, /device:TPU:0, one launch (start us, length us, event | category | flops | bytes accessed | tf_op | source)
XLA Modules:
  0.0 151.2 jit_solution(4453760052295182888)
XLA Ops:
  0.0 1.8 %convert_element_type.5 = bf16[4,16,16,512]{3,2,1,0:T(8,128)(2,1)S(1)} convert(f32[4,16,16,512]{3,2,1,0:T(8,128)} %param.8) | non-fusion elementwise | flops 524288 | bytes 3145728 | tf_op jit(solution)/shard_map/convert_element_type | solution.py:503
  4.1 1.5 %collective-permute-done.4.r_8_ = s32[4,16]{1,0:T(4,128)S(1)} collective-permute-done((s32[4,16]{1,0:T(4,128)S(1)}, s32[4,16]{1,0:T(4,128)S(1)}, u32[]{:S(2)}, u32[]{:S(2)}) %collective-permute-start.4) | collective-permute-done | bytes 288 | tf_op jit(solution)/shard_map/ppermute | solution.py:500
  6.6 1.6 %collective-permute-start.5 = (bf16[304,512]{1,0:T(8,128)(2,1)S(1)}, bf16[304,512]{1,0:T(8,128)(2,1)S(1)}, u32[]{:S(2)}, u32[]{:S(2)}) collective-permute-start(bf16[304,512]{1,0:T(8,128)(2,1)S(1)} %get-tuple-element.100), channel_id=1, source_target_pairs={{0,16},{16,32},{32,48},{48,64},{64,80},{80,96},{96,112},{112,0},{1... | collective-permute-start | bytes 933896 | tf_op jit(solution)/shard_map/ppermute | solution.py:22
  8.2 2.6 %collective-permute-start.6 = (bf16[304,512]{1,0:T(8,128)(2,1)S(1)}, bf16[304,512]{1,0:T(8,128)(2,1)S(1)}, u32[]{:S(2)}, u32[]{:S(2)}) collective-permute-start(bf16[304,512]{1,0:T(8,128)(2,1)S(1)} %get-tuple-element.101), channel_id=1, source_target_pairs={{0,112},{16,0},{32,16},{48,32},{64,48},{80,64},{96,80},{112,96},{1... | collective-permute-start | bytes 933896 | tf_op jit(solution)/shard_map/ppermute | solution.py:22
  10.8 8.5 %shard_map.67 = (f32[8,128,512]{2,1,0:T(8,128)S(1)}, f32[8,64,128]{2,1,0:T(8,128)S(1)}, bf16[8,256,512]{2,1,0:T(8,128)(2,1)S(1)}, f32[8,128,512]{2,1,0:T(8,128)S...) custom-call(s32[1]{0:T(128)} %bitcast.core.r_0_, ...), custom_call_target="tpu_custom_call" | custom-call | flops 1000000000 | bytes 8388608 | tf_op jit(solution)/shard_map/pallas_call | solution.py:542
  19.4 3.1 %shard_map.68 = (f8e4m3fn[8,2304,256]{2,1,0:T(32,128)(4,1)S(1)}, f32[4,128,512]{2,1,0:T(8,128)S(1)}, bf16[288,512]{1,0:T(8,128)(2,1)S(1)}, bf16[288,512]{1,0:T(8...) custom-call(f32[8,128,512]{2,1,0:T(8,128)S(1)} %get-tuple-element.98.r_0_.r_2_, ...), custom_call_target="tpu_custom_call" | custom-call | flops 1000000000 | bytes 8388608 | tf_op jit(solution)/shard_map/pallas_call | solution.py:558
  22.7 4.0 %collective-permute-start.8 = (bf16[288,512]{1,0:T(8,128)(2,1)S(1)}, bf16[288,512]{1,0:T(8,128)(2,1)S(1)}, u32[]{:S(2)}, u32[]{:S(2)}) collective-permute-start(bf16[288,512]{1,0:T(8,128)(2,1)S(1)} %get-tuple-element.116), channel_id=1, source_target_pairs={{0,112},{16,0},{32,16},{48,32},{64,48},{80,64},{96,80},{112,96},{1... | collective-permute-start | bytes 884744 | tf_op jit(solution)/shard_map/ppermute | solution.py:22
  26.7 5.6 %shard_map.69 = (f32[8,128,512]{2,1,0:T(8,128)S(1)}, f32[8,128,512]{2,1,0:T(8,128)S(1)}, f32[8,2048]{1,0:T(8,128)S(1)}, f32[8,1024]{1,0:T(8,128)S(1)}) custom-call(f32[4,128,512]{2,1,0:T(8,128)S(1)} %get-tuple-element.107.r_0_, f32[8,2048]{1,0:T(8,128)S(1)} %get-tuple-element.108.r_1_, f32[8,128,512]{2,1,0:T(8,128)S(1)} %get-tuple-element.98.r_0_.r_2_, ...), custom_call_target="tpu_custom_call" | custom-call | flops 1000000000 | bytes 8388608 | tf_op jit(solution)/shard_map/pallas_call | solution.py:547
  32.4 2.5 %shard_map.70 = (f32[4,128,512]{2,1,0:T(8,128)S(1)}, bf16[288,512]{1,0:T(8,128)(2,1)S(1)}, bf16[288,512]{1,0:T(8,128)(2,1)S(1)}, f32[8,2048]{1,0:T(8,128)S(1)}, f32[8,2048]{1,0:T(8,128)S(1)}) custom-call(f32[8,128,512]{2,1,0:T(8,128)S(1)} %get-tuple-element.113.r_0_.r_2_, f32[8,2048]{1,0:T(8,128)S(1)} %get-tuple-element.114.r_1_, ...), custom_call_target="tpu_custom_call" | custom-call | flops 1000000000 | bytes 8388608 | tf_op jit(solution)/shard_map/pallas_call | solution.py:558
  34.8 1.3 collective-permute-start.9
  36.1 2.9 %collective-permute-start.10 = (bf16[288,512]{1,0:T(8,128)(2,1)S(1)}, bf16[288,512]{1,0:T(8,128)(2,1)S(1)}, u32[]{:S(2)}, u32[]{:S(2)}) collective-permute-start(bf16[288,512]{1,0:T(8,128)(2,1)S(1)} %get-tuple-element.126), channel_id=1, source_target_pairs={{0,112},{16,0},{32,16},{48,32},{64,48},{80,64},{96,80},{112,96},{1... | collective-permute-start | bytes 884744 | tf_op jit(solution)/shard_map/ppermute | solution.py:22
  39.0 5.6 %shard_map.71 = (f32[8,128,512]{2,1,0:T(8,128)S(1)}, f32[8,128,512]{2,1,0:T(8,128)S(1)}, f32[8,2048]{1,0:T(8,128)S(1)}, f32[8,1024]{1,0:T(8,128)S(1)}) custom-call(f32[4,128,512]{2,1,0:T(8,128)S(1)} %get-tuple-element.119.r_0_, f32[8,2048]{1,0:T(8,128)S(1)} %get-tuple-element.120.r_1_, f32[8,128,512]{2,1,0:T(8,128)S(1)} %get-tuple-element.113.r_0_.r_2_, ...), custom_call_target="tpu_custom_call" | custom-call | flops 1000000000 | bytes 8388608 | tf_op jit(solution)/shard_map/pallas_call | solution.py:547
  44.7 2.7 %collective-permute-done.10.r_3_ = bf16[288,512]{1,0:T(8,128)(2,1)S(1)} collective-permute-done((bf16[288,512]{1,0:T(8,128)(2,1)S(1)}, bf16[288,512]{1,0:T(8,128)(2,1)S(1)}, u32[]{:S(2)}, u32[]{:S(2)}) %collective-permute-start.10) | collective-permute-done | bytes 294944 | tf_op jit(solution)/shard_map/ppermute | solution.py:22
  47.4 2.5 %shard_map.72 = (f32[4,128,512]{2,1,0:T(8,128)S(1)}, bf16[288,512]{1,0:T(8,128)(2,1)S(1)}, bf16[288,512]{1,0:T(8,128)(2,1)S(1)}, f32[8,2048]{1,0:T(8,128)S(1)}, f32[8,2048]{1,0:T(8,128)S(1)}) custom-call(f32[8,128,512]{2,1,0:T(8,128)S(1)} %get-tuple-element.123.r_0_.r_2_, f32[8,2048]{1,0:T(8,128)S(1)} %get-tuple-element.124.r_1_, ...), custom_call_target="tpu_custom_call" | custom-call | flops 1000000000 | bytes 8388608 | tf_op jit(solution)/shard_map/pallas_call | solution.py:558
  50.1 4.0 %collective-permute-start.12 = (bf16[288,512]{1,0:T(8,128)(2,1)S(1)}, bf16[288,512]{1,0:T(8,128)(2,1)S(1)}, u32[]{:S(2)}, u32[]{:S(2)}) collective-permute-start(bf16[288,512]{1,0:T(8,128)(2,1)S(1)} %get-tuple-element.135), channel_id=1, source_target_pairs={{0,112},{16,0},{32,16},{48,32},{64,48},{80,64},{96,80},{112,96},{1... | collective-permute-start | bytes 884744 | tf_op jit(solution)/shard_map/ppermute | solution.py:22
  54.1 6.4 %shard_map.73 = (f32[8,128,512]{2,1,0:T(8,128)}, f32[8,128,512]{2,1,0:T(8,128)S(1)}, f32[8,2048]{1,0:T(8,128)S(1)}, f32[8,1024]{1,0:T(8,128)S(1)}) custom-call(f32[4,128,512]{2,1,0:T(8,128)S(1)} %get-tuple-element.128.r_0_, f32[8,2048]{1,0:T(8,128)S(1)} %get-tuple-element.129.r_1_, f32[8,128,512]{2,1,0:T(8,128)S(1)} %get-tuple-element.123.r_0_.r_2_, ...), custom_call_target="tpu_custom_call" | custom-call | flops 1000000000 | bytes 8388608 | tf_op jit(solution)/shard_map/pallas_call | solution.py:547
  60.5 3.8 %collective-permute-done.12.r_3_ = bf16[288,512]{1,0:T(8,128)(2,1)S(1)} collective-permute-done((bf16[288,512]{1,0:T(8,128)(2,1)S(1)}, bf16[288,512]{1,0:T(8,128)(2,1)S(1)}, u32[]{:S(2)}, u32[]{:S(2)}) %collective-permute-start.12) | collective-permute-done | bytes 294944 | tf_op jit(solution)/shard_map/ppermute | solution.py:22
  64.2 2.5 %shard_map.74 = bf16[16,64,512]{2,1,0:T(8,128)(2,1)S(1)} custom-call(f32[8,128,512]{2,1,0:T(8,128)S(1)} %get-tuple-element.132.r_0_, f32[8,2048]{1,0:T(8,128)S(1)} %get-tuple-element.133.r_1_, bf16[288,512]{1,0:T(8,128)(2,1)S(1)} %collective-permute-done.11.r_2_, bf16[288,512]{1,0:T(8,128)(2,1)S(1)} %collective-permute-done.12.r_3_, ...), custom_call_target="tpu_custom_call" | custom-call | flops 1000000000 | bytes 8388608 | tf_op jit(solution)/shard_map/pallas_call | solution.py:558
  66.8 29.1 %all_to_all.20.r_0_ = bf16[16,64,512]{2,1,0:T(8,128)(2,1)S(1)} all-to-all(bf16[16,64,512]{2,1,0:T(8,128)(2,1)S(1)} %shard_map.74), channel_id=1, replica_groups=mesh['ring'=8,'core'=2,'st'=8] {'st','core'}, dimensions={0} | all-to-all | bytes 2097152 | tf_op jit(solution)/shard_map/all_to_all | solution.py:570
  96.3 13.1 %all_to_all.21 = f32[128,1,128]{2,1,0:T(1,128)S(1)} all-to-all(f32[128,1,128]{2,1,0:T(1,128)S(1)} %bitcast.20), channel_id=1, replica_groups=mesh['ring'=8,'core'=2,'st'=8] {'ring','core','st'}, dimensions={0} | all-to-all | bytes 131072 | tf_op jit(solution)/shard_map/all_to_all | solution.py:581
  109.7 13.9 %all_to_all.22 = f32[128,1,128]{2,1,0:T(1,128)S(1)} all-to-all(f32[128,1,128]{2,1,0:T(1,128)S(1)} %broadcast_in_dim.2), channel_id=1, replica_groups=mesh['ring'=8,'core'=2,'st'=8] {'ring','core','st'}, dimensions={0} | all-to-all | bytes 131072 | tf_op jit(solution)/shard_map/all_to_all | solution.py:583
  123.5 5.7 %shard_map.76 = bf16[8,32,16,128]{3,2,1,0:T(8,128)(2,1)S(1)} custom-call(f32[128,128]{1,0:T(8,128)S(1)} %bitcast.19, bf16[8,128,512]{2,1,0:T(8,128)(2,1)S(1)} %get-tuple-element.138.ordered), custom_call_target="tpu_custom_call" | custom-call | flops 200000000 | bytes 2097152 | tf_op jit(solution)/shard_map/pallas_call | solution.py:584
  129.3 20.6 %all_to_all.23 = bf16[8,32,16,128]{3,2,1,0:T(8,128)(2,1)S(1)} all-to-all(bf16[8,32,16,128]{3,2,1,0:T(8,128)(2,1)S(1)} %shard_map.76), channel_id=1, replica_groups=mesh['ring'=8,'core'=2,'st'=8] {'st'}, dimensions={0} | all-to-all | bytes 2097152 | tf_op jit(solution)/shard_map/all_to_all | solution.py:590
  149.9 1.2 copy.14
  (35 shorter events, 4.2 us)
Async XLA Ops:
  0.0 2.0 %copy-start.4 = (bf16[16,4,64,128]{3,2,1,0:T(8,128)(2,1)S(1)}, bf16[16,4,64,128]{3,2,1,0:T(8,128)(2,1)}, u32[]{:S(2)}) copy-start(bf16[16,4,64,128]{3,2,1,0:T(8,128)(2,1)} %param.6) | copy-start | bytes 3145732
  1.8 1.6 %copy-start = (f32[4,64,128]{2,1,0:T(8,128)S(1)}, f32[4,64,128]{2,1,0:T(8,128)}, u32[]{:S(2)}) copy-start(f32[4,64,128]{2,1,0:T(8,128)} %r_2_.3) | copy-start | bytes 393220
  1.9 1.7 %copy-start.2 = (s32[4,16,16]{2,1,0:T(8,128)S(1)}, s32[4,16,16]{2,1,0:T(8,128)}, u32[]{:S(2)}) copy-start(s32[4,16,16]{2,1,0:T(8,128)} %r_3_.1) | copy-start | bytes 12292
  1.9 2.1 %copy-start.3 = (s32[4,16]{1,0:T(4,128)S(1)}, s32[4,16]{1,0:T(4,128)}, u32[]{:S(2)}) copy-start(s32[4,16]{1,0:T(4,128)} %r_4_.1) | copy-start | bytes 772
  1.9 3.7 %collective-permute-start.2 = (bf16[4,256,512]{2,1,0:T(8,128)(2,1)S(1)}, bf16[4,256,512]{2,1,0:T(8,128)(2,1)S(1)}, u32[]{:S(2)}, u32[]{:S(2)}) collective-permute-start(bf16[4,256,512]{2,1,0:T(8,128)(2,1)S(1)} %bitcast.14), channel_id=1, source_target_pairs={{0,8},{8,0},{1,9},{9,1},{2,10},{10,2},{3,11},{11,3},{4,12},{12,4},... | collective-permute-start | bytes 3145736 | tf_op jit(solution)/shard_map/ppermute | solution.py:500
  2.9 3.7 %copy-start.1 = (f32[12288]{0:T(1024)S(1)}, f32[12288]{0:T(1024)}, u32[]{:S(2)}) copy-start(f32[12288]{0:T(1024)} %param.11) | copy-start | bytes 147460
  2.9 2.7 %collective-permute-start = (bf16[4,128,512]{2,1,0:T(8,128)(2,1)S(1)}, bf16[4,128,512]{2,1,0:T(8,128)(2,1)S(1)}, u32[]{:S(2)}, u32[]{:S(2)}) collective-permute-start(bf16[4,128,512]{2,1,0:T(8,128)(2,1)S(1)} %get-tuple-element.73), channel_id=1, source_target_pairs={{0,8},{8,0},{1,9},{9,1},{2,10},{10,2},{3,11},{11,3},{4,12},{12,4},... | collective-permute-start | bytes 1572872 | tf_op jit(solution)/shard_map/ppermute | solution.py:500
  3.5 3.1 %collective-permute-start.1 = (f32[4,64,128]{2,1,0:T(8,128)S(1)}, f32[4,64,128]{2,1,0:T(8,128)S(1)}, u32[]{:S(2)}, u32[]{:S(2)}) collective-permute-start(f32[4,64,128]{2,1,0:T(8,128)S(1)} %copy-done), channel_id=1, source_target_pairs={{0,8},{8,0},{1,9},{9,1},{2,10},{10,2},{3,11},{11,3},{4,12},{12,4},... | collective-permute-start | bytes 393224 | tf_op jit(solution)/shard_map/ppermute | solution.py:500
  3.6 2.0 %collective-permute-start.3 = (s32[4,16,16]{2,1,0:T(8,128)S(1)}, s32[4,16,16]{2,1,0:T(8,128)S(1)}, u32[]{:S(2)}, u32[]{:S(2)}) collective-permute-start(s32[4,16,16]{2,1,0:T(8,128)S(1)} %copy-done.2), channel_id=1, source_target_pairs={{0,8},{8,0},{1,9},{9,1},{2,10},{10,2},{3,11},{11,3},{4,12},{12,4},... | collective-permute-start | bytes 12296 | tf_op jit(solution)/shard_map/ppermute | solution.py:500
  4.0 1.6 %collective-permute-start.4 = (s32[4,16]{1,0:T(4,128)S(1)}, s32[4,16]{1,0:T(4,128)S(1)}, u32[]{:S(2)}, u32[]{:S(2)}) collective-permute-start(s32[4,16]{1,0:T(4,128)S(1)} %copy-done.3), channel_id=1, source_target_pairs={{0,8},{8,0},{1,9},{9,1},{2,10},{10,2},{3,11},{11,3},{4,12},{12,4},... | collective-permute-start | bytes 776 | tf_op jit(solution)/shard_map/ppermute | solution.py:500
  6.6 12.8 %collective-permute-start.5 = (bf16[304,512]{1,0:T(8,128)(2,1)S(1)}, bf16[304,512]{1,0:T(8,128)(2,1)S(1)}, u32[]{:S(2)}, u32[]{:S(2)}) collective-permute-start(bf16[304,512]{1,0:T(8,128)(2,1)S(1)} %get-tuple-element.100), channel_id=1, source_target_pairs={{0,16},{16,32},{32,48},{48,64},{64,80},{80,96},{96,112},{112,0},{1... | collective-permute-start | bytes 933896 | tf_op jit(solution)/shard_map/ppermute | solution.py:22
  8.2 11.1 %collective-permute-start.6 = (bf16[304,512]{1,0:T(8,128)(2,1)S(1)}, bf16[304,512]{1,0:T(8,128)(2,1)S(1)}, u32[]{:S(2)}, u32[]{:S(2)}) collective-permute-start(bf16[304,512]{1,0:T(8,128)(2,1)S(1)} %get-tuple-element.101), channel_id=1, source_target_pairs={{0,112},{16,0},{32,16},{48,32},{64,48},{80,64},{96,80},{112,96},{1... | collective-permute-start | bytes 933896 | tf_op jit(solution)/shard_map/ppermute | solution.py:22
  22.5 9.8 %collective-permute-start.7 = (bf16[288,512]{1,0:T(8,128)(2,1)S(1)}, bf16[288,512]{1,0:T(8,128)(2,1)S(1)}, u32[]{:S(2)}, u32[]{:S(2)}) collective-permute-start(bf16[288,512]{1,0:T(8,128)(2,1)S(1)} %get-tuple-element.115), channel_id=1, source_target_pairs={{0,16},{16,32},{32,48},{48,64},{64,80},{80,96},{96,112},{112,0},{1... | collective-permute-start | bytes 884744 | tf_op jit(solution)/shard_map/ppermute | solution.py:22
  22.7 9.7 %collective-permute-start.8 = (bf16[288,512]{1,0:T(8,128)(2,1)S(1)}, bf16[288,512]{1,0:T(8,128)(2,1)S(1)}, u32[]{:S(2)}, u32[]{:S(2)}) collective-permute-start(bf16[288,512]{1,0:T(8,128)(2,1)S(1)} %get-tuple-element.116), channel_id=1, source_target_pairs={{0,112},{16,0},{32,16},{48,32},{64,48},{80,64},{96,80},{112,96},{1... | collective-permute-start | bytes 884744 | tf_op jit(solution)/shard_map/ppermute | solution.py:22
  34.8 9.9 %collective-permute-start.9 = (bf16[288,512]{1,0:T(8,128)(2,1)S(1)}, bf16[288,512]{1,0:T(8,128)(2,1)S(1)}, u32[]{:S(2)}, u32[]{:S(2)}) collective-permute-start(bf16[288,512]{1,0:T(8,128)(2,1)S(1)} %get-tuple-element.125), channel_id=1, source_target_pairs={{0,16},{16,32},{32,48},{48,64},{64,80},{80,96},{96,112},{112,0},{1... | collective-permute-start | bytes 884744 | tf_op jit(solution)/shard_map/ppermute | solution.py:22
  36.1 11.3 %collective-permute-start.10 = (bf16[288,512]{1,0:T(8,128)(2,1)S(1)}, bf16[288,512]{1,0:T(8,128)(2,1)S(1)}, u32[]{:S(2)}, u32[]{:S(2)}) collective-permute-start(bf16[288,512]{1,0:T(8,128)(2,1)S(1)} %get-tuple-element.126), channel_id=1, source_target_pairs={{0,112},{16,0},{32,16},{48,32},{64,48},{80,64},{96,80},{112,96},{1... | collective-permute-start | bytes 884744 | tf_op jit(solution)/shard_map/ppermute | solution.py:22
  49.9 10.6 %collective-permute-start.11 = (bf16[288,512]{1,0:T(8,128)(2,1)S(1)}, bf16[288,512]{1,0:T(8,128)(2,1)S(1)}, u32[]{:S(2)}, u32[]{:S(2)}) collective-permute-start(bf16[288,512]{1,0:T(8,128)(2,1)S(1)} %get-tuple-element.134), channel_id=1, source_target_pairs={{0,16},{16,32},{32,48},{48,64},{64,80},{80,96},{96,112},{112,0},{1... | collective-permute-start | bytes 884744 | tf_op jit(solution)/shard_map/ppermute | solution.py:22
  50.1 14.1 %collective-permute-start.12 = (bf16[288,512]{1,0:T(8,128)(2,1)S(1)}, bf16[288,512]{1,0:T(8,128)(2,1)S(1)}, u32[]{:S(2)}, u32[]{:S(2)}) collective-permute-start(bf16[288,512]{1,0:T(8,128)(2,1)S(1)} %get-tuple-element.135), channel_id=1, source_target_pairs={{0,112},{16,0},{32,16},{48,32},{64,48},{80,64},{96,80},{112,96},{1... | collective-permute-start | bytes 884744 | tf_op jit(solution)/shard_map/ppermute | solution.py:22

commit v8 on v7

--- a/solution.py
+++ b/solution.py
@@ -348,7 +348,8 @@
     mask = block_mask(height, cols, states, slots)
     used = jnp.where(named < NO_NAME, 1.0, 0.0)
     out = [None] * planes
-    for z in range(planes):
+
+    def couple(z):
         at = slice(z * cols, (z + 1) * cols)
         chosen = lax.dot_general(terms[:, z * cols : z * cols + reach], table[z], NN, preferred_element_type=F32)
         chosen = from_pieces(chosen, scale)
@@ -361,6 +362,10 @@
             i = z - inner_planes(planes)[0]
             of_chosen = lax.dot_general(doubled(chosen), square[i], NN, preferred_element_type=F32)
             out[z] = (inner[:, i * cols : (i + 1) * cols] + of_chosen[:states]) * used[:, at]
+
+    for z in range(planes):
+        if last or z not in inner_planes(planes):
+            couple(z)
 
     def pair_step(pair, carry):
         here = rows_at(pair, 2 * states)
@@ -388,8 +393,10 @@
                     message[rows_at(pair, 2 * states, i % 2 * height), lane(y)] = new.astype(BF16)
         return carry
 
-    lax.fori_loop(0, tiles // 2, pair_step, 0)
+    lax.fori_loop(0, tiles // 2, pair_step, 0, unroll=not last)
     if not last:
+        for z in inner_planes(planes):
+            couple(z)
         for z in range(planes):
             if z in inner_planes(planes):
                 continue

time: 151 us -> 150 us (level)
  no operation moved by 1% of the time
where the time goes in v8:
time: 150 us
  blocking collectives  76.9 us (51%)
  Pallas kernels  43.3 us (29%)
  starting transfers between devices  18.3 us (12%)
  waiting for transfers between devices  7.6 us (5%)
  local copies, waits for them, and re-layouts  1.99 us (1%)
  other arithmetic  1.99 us (1%)
    all_to_all x1, blocking collectives, per_device(): cells = lax.all_to_all(filtered, ('st', 'core'), 0, 0, tiled=True)  29.2 us
    all_to_all x1, blocking collectives, per_device(): rotated = lax.all_to_all(rotated, 'st', 0, 0, tiled=True)  20.6 us
    pallas_call x3, Pallas kernels, per_device(): call(lambda *r: local_kernel(sizes, False, *r), [f32(shape)] + outs, flop...  17.7 us
    ppermute x8, starting transfers between devices, passed_along(): lax.ppermute(array, axis, [(i, (i + by) % devices) for i in range(devices)])  17 us
    all_to_all x1, blocking collectives, per_device(): lax.all_to_all(jnp.broadcast_to(total, (devices, per, nstates)), everywhe...  13.9 us
    all_to_all x1, blocking collectives, per_device(): lax.all_to_all(part.reshape(devices, per, nstates), everywhere, 0, 0, til...  13.1 us
    pallas_call x4, Pallas kernels, per_device(): call(lambda *r, first=first, last=last: step_kernel(sizes, first, last, *...  9.72 us
    pallas_call x1, Pallas kernels, per_device(): call(lambda *r: turn_kernel(sizes, False, *r), outs, in_specs=[scalar] +...  8.54 us
  transfers between devices with their start and end apart: 13, of which 3 were waited for; matrix products, arithmetic and copies ran while one was open for 0% of the time, Pallas kernels for 18%

profile of v8, /device:TPU:0, one launch (start us, length us, event | category | flops | bytes accessed | tf_op | source)
XLA Modules:
  0.0 150.3 jit_solution(5241654569728743442)
XLA Ops:
  0.0 1.8 %convert_element_type.5 = bf16[4,16,16,512]{3,2,1,0:T(8,128)(2,1)S(1)} convert(f32[4,16,16,512]{3,2,1,0:T(8,128)} %param.8) | non-fusion elementwise | flops 524288 | bytes 3145728 | tf_op jit(solution)/shard_map/convert_element_type | solution.py:510
  4.1 1.5 %collective-permute-done.4.r_8_ = s32[4,16]{1,0:T(4,128)S(1)} collective-permute-done((s32[4,16]{1,0:T(4,128)S(1)}, s32[4,16]{1,0:T(4,128)S(1)}, u32[]{:S(2)}, u32[]{:S(2)}) %collective-permute-start.4) | collective-permute-done | bytes 288 | tf_op jit(solution)/shard_map/ppermute | solution.py:507
  6.6 1.6 %collective-permute-start.5 = (bf16[304,512]{1,0:T(8,128)(2,1)S(1)}, bf16[304,512]{1,0:T(8,128)(2,1)S(1)}, u32[]{:S(2)}, u32[]{:S(2)}) collective-permute-start(bf16[304,512]{1,0:T(8,128)(2,1)S(1)} %get-tuple-element.100), channel_id=1, source_target_pairs={{0,16},{16,32},{32,48},{48,64},{64,80},{80,96},{96,112},{112,0},{1... | collective-permute-start | bytes 933896 | tf_op jit(solution)/shard_map/ppermute | solution.py:22
  8.2 2.6 %collective-permute-start.6 = (bf16[304,512]{1,0:T(8,128)(2,1)S(1)}, bf16[304,512]{1,0:T(8,128)(2,1)S(1)}, u32[]{:S(2)}, u32[]{:S(2)}) collective-permute-start(bf16[304,512]{1,0:T(8,128)(2,1)S(1)} %get-tuple-element.101), channel_id=1, source_target_pairs={{0,112},{16,0},{32,16},{48,32},{64,48},{80,64},{96,80},{112,96},{1... | collective-permute-start | bytes 933896 | tf_op jit(solution)/shard_map/ppermute | solution.py:22
  10.8 8.5 %shard_map.67 = (f32[8,128,512]{2,1,0:T(8,128)S(1)}, f32[8,64,128]{2,1,0:T(8,128)S(1)}, bf16[8,256,512]{2,1,0:T(8,128)(2,1)S(1)}, f32[8,128,512]{2,1,0:T(8,128)S...) custom-call(s32[1]{0:T(128)} %bitcast.core.r_0_, ...), custom_call_target="tpu_custom_call" | custom-call | flops 1000000000 | bytes 8388608 | tf_op jit(solution)/shard_map/pallas_call | solution.py:549
  19.4 3.0 %shard_map.68 = (f8e4m3fn[8,2304,256]{2,1,0:T(32,128)(4,1)S(1)}, f32[4,128,512]{2,1,0:T(8,128)S(1)}, bf16[288,512]{1,0:T(8,128)(2,1)S(1)}, bf16[288,512]{1,0:T(8...) custom-call(f32[8,128,512]{2,1,0:T(8,128)S(1)} %get-tuple-element.98.r_0_.r_2_, ...), custom_call_target="tpu_custom_call" | custom-call | flops 1000000000 | bytes 8388608 | tf_op jit(solution)/shard_map/pallas_call | solution.py:565
  22.6 4.0 %collective-permute-start.8 = (bf16[288,512]{1,0:T(8,128)(2,1)S(1)}, bf16[288,512]{1,0:T(8,128)(2,1)S(1)}, u32[]{:S(2)}, u32[]{:S(2)}) collective-permute-start(bf16[288,512]{1,0:T(8,128)(2,1)S(1)} %get-tuple-element.116), channel_id=1, source_target_pairs={{0,112},{16,0},{32,16},{48,32},{64,48},{80,64},{96,80},{112,96},{1... | collective-permute-start | bytes 884744 | tf_op jit(solution)/shard_map/ppermute | solution.py:22
  26.6 5.6 %shard_map.69 = (f32[8,128,512]{2,1,0:T(8,128)S(1)}, f32[8,128,512]{2,1,0:T(8,128)S(1)}, f32[8,2048]{1,0:T(8,128)S(1)}, f32[8,1024]{1,0:T(8,128)S(1)}) custom-call(f32[4,128,512]{2,1,0:T(8,128)S(1)} %get-tuple-element.107.r_0_, f32[8,2048]{1,0:T(8,128)S(1)} %get-tuple-element.108.r_1_, f32[8,128,512]{2,1,0:T(8,128)S(1)} %get-tuple-element.98.r_0_.r_2_, ...), custom_call_target="tpu_custom_call" | custom-call | flops 1000000000 | bytes 8388608 | tf_op jit(solution)/shard_map/pallas_call | solution.py:554
  32.2 2.1 %shard_map.70 = (f32[4,128,512]{2,1,0:T(8,128)S(1)}, bf16[288,512]{1,0:T(8,128)(2,1)S(1)}, bf16[288,512]{1,0:T(8,128)(2,1)S(1)}, f32[8,2048]{1,0:T(8,128)S(1)}, f32[8,2048]{1,0:T(8,128)S(1)}) custom-call(f32[8,128,512]{2,1,0:T(8,128)S(1)} %get-tuple-element.113.r_0_.r_2_, f32[8,2048]{1,0:T(8,128)S(1)} %get-tuple-element.114.r_1_, ...), custom_call_target="tpu_custom_call" | custom-call | flops 1000000000 | bytes 8388608 | tf_op jit(solution)/shard_map/pallas_call | solution.py:565
  34.4 1.6 %collective-permute-start.9 = (bf16[288,512]{1,0:T(8,128)(2,1)S(1)}, bf16[288,512]{1,0:T(8,128)(2,1)S(1)}, u32[]{:S(2)}, u32[]{:S(2)}) collective-permute-start(bf16[288,512]{1,0:T(8,128)(2,1)S(1)} %get-tuple-element.125), channel_id=1, source_target_pairs={{0,16},{16,32},{32,48},{48,64},{64,80},{80,96},{96,112},{112,0},{1... | collective-permute-start | bytes 884744 | tf_op jit(solution)/shard_map/ppermute | solution.py:22
  35.9 2.8 %collective-permute-start.10 = (bf16[288,512]{1,0:T(8,128)(2,1)S(1)}, bf16[288,512]{1,0:T(8,128)(2,1)S(1)}, u32[]{:S(2)}, u32[]{:S(2)}) collective-permute-start(bf16[288,512]{1,0:T(8,128)(2,1)S(1)} %get-tuple-element.126), channel_id=1, source_target_pairs={{0,112},{16,0},{32,16},{48,32},{64,48},{80,64},{96,80},{112,96},{1... | collective-permute-start | bytes 884744 | tf_op jit(solution)/shard_map/ppermute | solution.py:22
  38.8 5.7 %shard_map.71 = (f32[8,128,512]{2,1,0:T(8,128)S(1)}, f32[8,128,512]{2,1,0:T(8,128)S(1)}, f32[8,2048]{1,0:T(8,128)S(1)}, f32[8,1024]{1,0:T(8,128)S(1)}) custom-call(f32[4,128,512]{2,1,0:T(8,128)S(1)} %get-tuple-element.119.r_0_, f32[8,2048]{1,0:T(8,128)S(1)} %get-tuple-element.120.r_1_, f32[8,128,512]{2,1,0:T(8,128)S(1)} %get-tuple-element.113.r_0_.r_2_, ...), custom_call_target="tpu_custom_call" | custom-call | flops 1000000000 | bytes 8388608 | tf_op jit(solution)/shard_map/pallas_call | solution.py:554
  44.5 2.6 %collective-permute-done.10.r_3_ = bf16[288,512]{1,0:T(8,128)(2,1)S(1)} collective-permute-done((bf16[288,512]{1,0:T(8,128)(2,1)S(1)}, bf16[288,512]{1,0:T(8,128)(2,1)S(1)}, u32[]{:S(2)}, u32[]{:S(2)}) %collective-permute-start.10) | collective-permute-done | bytes 294944 | tf_op jit(solution)/shard_map/ppermute | solution.py:22
  47.1 2.1 %shard_map.72 = (f32[4,128,512]{2,1,0:T(8,128)S(1)}, bf16[288,512]{1,0:T(8,128)(2,1)S(1)}, bf16[288,512]{1,0:T(8,128)(2,1)S(1)}, f32[8,2048]{1,0:T(8,128)S(1)}, f32[8,2048]{1,0:T(8,128)S(1)}) custom-call(f32[8,128,512]{2,1,0:T(8,128)S(1)} %get-tuple-element.123.r_0_.r_2_, f32[8,2048]{1,0:T(8,128)S(1)} %get-tuple-element.124.r_1_, ...), custom_call_target="tpu_custom_call" | custom-call | flops 1000000000 | bytes 8388608 | tf_op jit(solution)/shard_map/pallas_call | solution.py:565
  49.6 3.8 %collective-permute-start.12 = (bf16[288,512]{1,0:T(8,128)(2,1)S(1)}, bf16[288,512]{1,0:T(8,128)(2,1)S(1)}, u32[]{:S(2)}, u32[]{:S(2)}) collective-permute-start(bf16[288,512]{1,0:T(8,128)(2,1)S(1)} %get-tuple-element.135), channel_id=1, source_target_pairs={{0,112},{16,0},{32,16},{48,32},{64,48},{80,64},{96,80},{112,96},{1... | collective-permute-start | bytes 884744 | tf_op jit(solution)/shard_map/ppermute | solution.py:22
  53.4 6.4 %shard_map.73 = (f32[8,128,512]{2,1,0:T(8,128)}, f32[8,128,512]{2,1,0:T(8,128)S(1)}, f32[8,2048]{1,0:T(8,128)S(1)}, f32[8,1024]{1,0:T(8,128)S(1)}) custom-call(f32[4,128,512]{2,1,0:T(8,128)S(1)} %get-tuple-element.128.r_0_, f32[8,2048]{1,0:T(8,128)S(1)} %get-tuple-element.129.r_1_, f32[8,128,512]{2,1,0:T(8,128)S(1)} %get-tuple-element.123.r_0_.r_2_, ...), custom_call_target="tpu_custom_call" | custom-call | flops 1000000000 | bytes 8388608 | tf_op jit(solution)/shard_map/pallas_call | solution.py:554
  59.8 3.4 %collective-permute-done.12.r_3_ = bf16[288,512]{1,0:T(8,128)(2,1)S(1)} collective-permute-done((bf16[288,512]{1,0:T(8,128)(2,1)S(1)}, bf16[288,512]{1,0:T(8,128)(2,1)S(1)}, u32[]{:S(2)}, u32[]{:S(2)}) %collective-permute-start.12) | collective-permute-done | bytes 294944 | tf_op jit(solution)/shard_map/ppermute | solution.py:22
  63.2 2.5 %shard_map.74 = bf16[16,64,512]{2,1,0:T(8,128)(2,1)S(1)} custom-call(f32[8,128,512]{2,1,0:T(8,128)S(1)} %get-tuple-element.132.r_0_, f32[8,2048]{1,0:T(8,128)S(1)} %get-tuple-element.133.r_1_, bf16[288,512]{1,0:T(8,128)(2,1)S(1)} %collective-permute-done.11.r_2_, bf16[288,512]{1,0:T(8,128)(2,1)S(1)} %collective-permute-done.12.r_3_, ...), custom_call_target="tpu_custom_call" | custom-call | flops 1000000000 | bytes 8388608 | tf_op jit(solution)/shard_map/pallas_call | solution.py:565
  65.8 29.2 %all_to_all.20.r_0_ = bf16[16,64,512]{2,1,0:T(8,128)(2,1)S(1)} all-to-all(bf16[16,64,512]{2,1,0:T(8,128)(2,1)S(1)} %shard_map.74), channel_id=1, replica_groups=mesh['ring'=8,'core'=2,'st'=8] {'st','core'}, dimensions={0} | all-to-all | bytes 2097152 | tf_op jit(solution)/shard_map/all_to_all | solution.py:577
  95.5 13.1 %all_to_all.21 = f32[128,1,128]{2,1,0:T(1,128)S(1)} all-to-all(f32[128,1,128]{2,1,0:T(1,128)S(1)} %bitcast.20), channel_id=1, replica_groups=mesh['ring'=8,'core'=2,'st'=8] {'ring','core','st'}, dimensions={0} | all-to-all | bytes 131072 | tf_op jit(solution)/shard_map/all_to_all | solution.py:588
  108.8 13.9 %all_to_all.22 = f32[128,1,128]{2,1,0:T(1,128)S(1)} all-to-all(f32[128,1,128]{2,1,0:T(1,128)S(1)} %broadcast_in_dim.2), channel_id=1, replica_groups=mesh['ring'=8,'core'=2,'st'=8] {'ring','core','st'}, dimensions={0} | all-to-all | bytes 131072 | tf_op jit(solution)/shard_map/all_to_all | solution.py:590
  122.7 5.7 %shard_map.76 = bf16[8,32,16,128]{3,2,1,0:T(8,128)(2,1)S(1)} custom-call(f32[128,128]{1,0:T(8,128)S(1)} %bitcast.19, bf16[8,128,512]{2,1,0:T(8,128)(2,1)S(1)} %get-tuple-element.138.ordered), custom_call_target="tpu_custom_call" | custom-call | flops 200000000 | bytes 2097152 | tf_op jit(solution)/shard_map/pallas_call | solution.py:591
  128.4 20.6 %all_to_all.23 = bf16[8,32,16,128]{3,2,1,0:T(8,128)(2,1)S(1)} all-to-all(bf16[8,32,16,128]{3,2,1,0:T(8,128)(2,1)S(1)} %shard_map.76), channel_id=1, replica_groups=mesh['ring'=8,'core'=2,'st'=8] {'st'}, dimensions={0} | all-to-all | bytes 2097152 | tf_op jit(solution)/shard_map/all_to_all | solution.py:597
  149.0 1.2 copy.14
  (35 shorter events, 4.3 us)
Async XLA Ops:
  0.0 2.0 %copy-start.4 = (bf16[16,4,64,128]{3,2,1,0:T(8,128)(2,1)S(1)}, bf16[16,4,64,128]{3,2,1,0:T(8,128)(2,1)}, u32[]{:S(2)}) copy-start(bf16[16,4,64,128]{3,2,1,0:T(8,128)(2,1)} %param.6) | copy-start | bytes 3145732
  1.8 1.6 %copy-start = (f32[4,64,128]{2,1,0:T(8,128)S(1)}, f32[4,64,128]{2,1,0:T(8,128)}, u32[]{:S(2)}) copy-start(f32[4,64,128]{2,1,0:T(8,128)} %r_2_.3) | copy-start | bytes 393220
  1.9 1.7 %copy-start.2 = (s32[4,16,16]{2,1,0:T(8,128)S(1)}, s32[4,16,16]{2,1,0:T(8,128)}, u32[]{:S(2)}) copy-start(s32[4,16,16]{2,1,0:T(8,128)} %r_3_.1) | copy-start | bytes 12292
  1.9 2.1 %copy-start.3 = (s32[4,16]{1,0:T(4,128)S(1)}, s32[4,16]{1,0:T(4,128)}, u32[]{:S(2)}) copy-start(s32[4,16]{1,0:T(4,128)} %r_4_.1) | copy-start | bytes 772
  1.9 3.7 %collective-permute-start.2 = (bf16[4,256,512]{2,1,0:T(8,128)(2,1)S(1)}, bf16[4,256,512]{2,1,0:T(8,128)(2,1)S(1)}, u32[]{:S(2)}, u32[]{:S(2)}) collective-permute-start(bf16[4,256,512]{2,1,0:T(8,128)(2,1)S(1)} %bitcast.14), channel_id=1, source_target_pairs={{0,8},{8,0},{1,9},{9,1},{2,10},{10,2},{3,11},{11,3},{4,12},{12,4},... | collective-permute-start | bytes 3145736 | tf_op jit(solution)/shard_map/ppermute | solution.py:507
  2.9 3.7 %copy-start.1 = (f32[12288]{0:T(1024)S(1)}, f32[12288]{0:T(1024)}, u32[]{:S(2)}) copy-start(f32[12288]{0:T(1024)} %param.11) | copy-start | bytes 147460
  2.9 2.7 %collective-permute-start = (bf16[4,128,512]{2,1,0:T(8,128)(2,1)S(1)}, bf16[4,128,512]{2,1,0:T(8,128)(2,1)S(1)}, u32[]{:S(2)}, u32[]{:S(2)}) collective-permute-start(bf16[4,128,512]{2,1,0:T(8,128)(2,1)S(1)} %get-tuple-element.73), channel_id=1, source_target_pairs={{0,8},{8,0},{1,9},{9,1},{2,10},{10,2},{3,11},{11,3},{4,12},{12,4},... | collective-permute-start | bytes 1572872 | tf_op jit(solution)/shard_map/ppermute | solution.py:507
  3.5 3.1 %collective-permute-start.1 = (f32[4,64,128]{2,1,0:T(8,128)S(1)}, f32[4,64,128]{2,1,0:T(8,128)S(1)}, u32[]{:S(2)}, u32[]{:S(2)}) collective-permute-start(f32[4,64,128]{2,1,0:T(8,128)S(1)} %copy-done), channel_id=1, source_target_pairs={{0,8},{8,0},{1,9},{9,1},{2,10},{10,2},{3,11},{11,3},{4,12},{12,4},... | collective-permute-start | bytes 393224 | tf_op jit(solution)/shard_map/ppermute | solution.py:507
  3.6 2.0 %collective-permute-start.3 = (s32[4,16,16]{2,1,0:T(8,128)S(1)}, s32[4,16,16]{2,1,0:T(8,128)S(1)}, u32[]{:S(2)}, u32[]{:S(2)}) collective-permute-start(s32[4,16,16]{2,1,0:T(8,128)S(1)} %copy-done.2), channel_id=1, source_target_pairs={{0,8},{8,0},{1,9},{9,1},{2,10},{10,2},{3,11},{11,3},{4,12},{12,4},... | collective-permute-start | bytes 12296 | tf_op jit(solution)/shard_map/ppermute | solution.py:507
  4.0 1.6 %collective-permute-start.4 = (s32[4,16]{1,0:T(4,128)S(1)}, s32[4,16]{1,0:T(4,128)S(1)}, u32[]{:S(2)}, u32[]{:S(2)}) collective-permute-start(s32[4,16]{1,0:T(4,128)S(1)} %copy-done.3), channel_id=1, source_target_pairs={{0,8},{8,0},{1,9},{9,1},{2,10},{10,2},{3,11},{11,3},{4,12},{12,4},... | collective-permute-start | bytes 776 | tf_op jit(solution)/shard_map/ppermute | solution.py:507
  6.6 12.8 %collective-permute-start.5 = (bf16[304,512]{1,0:T(8,128)(2,1)S(1)}, bf16[304,512]{1,0:T(8,128)(2,1)S(1)}, u32[]{:S(2)}, u32[]{:S(2)}) collective-permute-start(bf16[304,512]{1,0:T(8,128)(2,1)S(1)} %get-tuple-element.100), channel_id=1, source_target_pairs={{0,16},{16,32},{32,48},{48,64},{64,80},{80,96},{96,112},{112,0},{1... | collective-permute-start | bytes 933896 | tf_op jit(solution)/shard_map/ppermute | solution.py:22
  8.2 11.1 %collective-permute-start.6 = (bf16[304,512]{1,0:T(8,128)(2,1)S(1)}, bf16[304,512]{1,0:T(8,128)(2,1)S(1)}, u32[]{:S(2)}, u32[]{:S(2)}) collective-permute-start(bf16[304,512]{1,0:T(8,128)(2,1)S(1)} %get-tuple-element.101), channel_id=1, source_target_pairs={{0,112},{16,0},{32,16},{48,32},{64,48},{80,64},{96,80},{112,96},{1... | collective-permute-start | bytes 933896 | tf_op jit(solution)/shard_map/ppermute | solution.py:22
  22.4 9.8 %collective-permute-start.7 = (bf16[288,512]{1,0:T(8,128)(2,1)S(1)}, bf16[288,512]{1,0:T(8,128)(2,1)S(1)}, u32[]{:S(2)}, u32[]{:S(2)}) collective-permute-start(bf16[288,512]{1,0:T(8,128)(2,1)S(1)} %get-tuple-element.115), channel_id=1, source_target_pairs={{0,16},{16,32},{32,48},{48,64},{64,80},{80,96},{96,112},{112,0},{1... | collective-permute-start | bytes 884744 | tf_op jit(solution)/shard_map/ppermute | solution.py:22
  22.6 9.7 %collective-permute-start.8 = (bf16[288,512]{1,0:T(8,128)(2,1)S(1)}, bf16[288,512]{1,0:T(8,128)(2,1)S(1)}, u32[]{:S(2)}, u32[]{:S(2)}) collective-permute-start(bf16[288,512]{1,0:T(8,128)(2,1)S(1)} %get-tuple-element.116), channel_id=1, source_target_pairs={{0,112},{16,0},{32,16},{48,32},{64,48},{80,64},{96,80},{112,96},{1... | collective-permute-start | bytes 884744 | tf_op jit(solution)/shard_map/ppermute | solution.py:22
  34.4 10.1 %collective-permute-start.9 = (bf16[288,512]{1,0:T(8,128)(2,1)S(1)}, bf16[288,512]{1,0:T(8,128)(2,1)S(1)}, u32[]{:S(2)}, u32[]{:S(2)}) collective-permute-start(bf16[288,512]{1,0:T(8,128)(2,1)S(1)} %get-tuple-element.125), channel_id=1, source_target_pairs={{0,16},{16,32},{32,48},{48,64},{64,80},{80,96},{96,112},{112,0},{1... | collective-permute-start | bytes 884744 | tf_op jit(solution)/shard_map/ppermute | solution.py:22
  35.9 11.2 %collective-permute-start.10 = (bf16[288,512]{1,0:T(8,128)(2,1)S(1)}, bf16[288,512]{1,0:T(8,128)(2,1)S(1)}, u32[]{:S(2)}, u32[]{:S(2)}) collective-permute-start(bf16[288,512]{1,0:T(8,128)(2,1)S(1)} %get-tuple-element.126), channel_id=1, source_target_pairs={{0,112},{16,0},{32,16},{48,32},{64,48},{80,64},{96,80},{112,96},{1... | collective-permute-start | bytes 884744 | tf_op jit(solution)/shard_map/ppermute | solution.py:22
  49.2 10.6 %collective-permute-start.11 = (bf16[288,512]{1,0:T(8,128)(2,1)S(1)}, bf16[288,512]{1,0:T(8,128)(2,1)S(1)}, u32[]{:S(2)}, u32[]{:S(2)}) collective-permute-start(bf16[288,512]{1,0:T(8,128)(2,1)S(1)} %get-tuple-element.134), channel_id=1, source_target_pairs={{0,16},{16,32},{32,48},{48,64},{64,80},{80,96},{96,112},{112,0},{1... | collective-permute-start | bytes 884744 | tf_op jit(solution)/shard_map/ppermute | solution.py:22
  49.6 13.7 %collective-permute-start.12 = (bf16[288,512]{1,0:T(8,128)(2,1)S(1)}, bf16[288,512]{1,0:T(8,128)(2,1)S(1)}, u32[]{:S(2)}, u32[]{:S(2)}) collective-permute-start(bf16[288,512]{1,0:T(8,128)(2,1)S(1)} %get-tuple-element.135), channel_id=1, source_target_pairs={{0,112},{16,0},{32,16},{48,32},{64,48},{80,64},{96,80},{112,96},{1... | collective-permute-start | bytes 884744 | tf_op jit(solution)/shard_map/ppermute | solution.py:22

commit v9 on v8

--- a/solution.py
+++ b/solution.py
@@ -393,7 +393,7 @@
                     message[rows_at(pair, 2 * states, i % 2 * height), lane(y)] = new.astype(BF16)
         return carry
 
-    lax.fori_loop(0, tiles // 2, pair_step, 0, unroll=not last)
+    lax.fori_loop(0, tiles // 2, pair_step, 0, unroll=True)
     if not last:
         for z in inner_planes(planes):
             couple(z)

time: 150 us -> 150 us (level)
  no operation moved by 1% of the time
where the time goes in v9:
time: 150 us
  blocking collectives  76.9 us (51%)
  Pallas kernels  42.9 us (29%)
  starting transfers between devices  18.3 us (12%)
  waiting for transfers between devices  7.6 us (5%)
  local copies, waits for them, and re-layouts  1.99 us (1%)
  other arithmetic  1.99 us (1%)
    all_to_all x1, blocking collectives, per_device(): cells = lax.all_to_all(filtered, ('st', 'core'), 0, 0, tiled=True)  29.2 us
    all_to_all x1, blocking collectives, per_device(): rotated = lax.all_to_all(rotated, 'st', 0, 0, tiled=True)  20.7 us
    pallas_call x3, Pallas kernels, per_device(): call(lambda *r: local_kernel(sizes, False, *r), [f32(shape)] + outs, flop...  17.7 us
    ppermute x8, starting transfers between devices, passed_along(): lax.ppermute(array, axis, [(i, (i + by) % devices) for i in range(devices)])  17 us
    all_to_all x1, blocking collectives, per_device(): lax.all_to_all(jnp.broadcast_to(total, (devices, per, nstates)), everywhe...  13.9 us
    all_to_all x1, blocking collectives, per_device(): lax.all_to_all(part.reshape(devices, per, nstates), everywhere, 0, 0, til...  13.1 us
    pallas_call x4, Pallas kernels, per_device(): call(lambda *r, first=first, last=last: step_kernel(sizes, first, last, *...  9.31 us
    pallas_call x1, Pallas kernels, per_device(): call(lambda *r: turn_kernel(sizes, False, *r), outs, in_specs=[scalar] +...  8.54 us
  transfers between devices with their start and end apart: 13, of which 3 were waited for; matrix products, arithmetic and copies ran while one was open for 0% of the time, Pallas kernels for 18%

profile of v9, /device:TPU:0, one launch (start us, length us, event | category | flops | bytes accessed | tf_op | source)
XLA Modules:
  0.0 149.9 jit_solution(1037184991941005674)
XLA Ops:
  0.0 1.8 %convert_element_type.5 = bf16[4,16,16,512]{3,2,1,0:T(8,128)(2,1)S(1)} convert(f32[4,16,16,512]{3,2,1,0:T(8,128)} %param.8) | non-fusion elementwise | flops 524288 | bytes 3145728 | tf_op jit(solution)/shard_map/convert_element_type | solution.py:510
  4.1 1.5 %collective-permute-done.4.r_8_ = s32[4,16]{1,0:T(4,128)S(1)} collective-permute-done((s32[4,16]{1,0:T(4,128)S(1)}, s32[4,16]{1,0:T(4,128)S(1)}, u32[]{:S(2)}, u32[]{:S(2)}) %collective-permute-start.4) | collective-permute-done | bytes 288 | tf_op jit(solution)/shard_map/ppermute | solution.py:507
  6.6 1.6 %collective-permute-start.5 = (bf16[304,512]{1,0:T(8,128)(2,1)S(1)}, bf16[304,512]{1,0:T(8,128)(2,1)S(1)}, u32[]{:S(2)}, u32[]{:S(2)}) collective-permute-start(bf16[304,512]{1,0:T(8,128)(2,1)S(1)} %get-tuple-element.100), channel_id=1, source_target_pairs={{0,16},{16,32},{32,48},{48,64},{64,80},{80,96},{96,112},{112,0},{1... | collective-permute-start | bytes 933896 | tf_op jit(solution)/shard_map/ppermute | solution.py:22
  8.2 2.6 %collective-permute-start.6 = (bf16[304,512]{1,0:T(8,128)(2,1)S(1)}, bf16[304,512]{1,0:T(8,128)(2,1)S(1)}, u32[]{:S(2)}, u32[]{:S(2)}) collective-permute-start(bf16[304,512]{1,0:T(8,128)(2,1)S(1)} %get-tuple-element.101), channel_id=1, source_target_pairs={{0,112},{16,0},{32,16},{48,32},{64,48},{80,64},{96,80},{112,96},{1... | collective-permute-start | bytes 933896 | tf_op jit(solution)/shard_map/ppermute | solution.py:22
  10.8 8.5 %shard_map.67 = (f32[8,128,512]{2,1,0:T(8,128)S(1)}, f32[8,64,128]{2,1,0:T(8,128)S(1)}, bf16[8,256,512]{2,1,0:T(8,128)(2,1)S(1)}, f32[8,128,512]{2,1,0:T(8,128)S...) custom-call(s32[1]{0:T(128)} %bitcast.core.r_0_, ...), custom_call_target="tpu_custom_call" | custom-call | flops 1000000000 | bytes 8388608 | tf_op jit(solution)/shard_map/pallas_call | solution.py:549
  19.4 3.0 %shard_map.68 = (f8e4m3fn[8,2304,256]{2,1,0:T(32,128)(4,1)S(1)}, f32[4,128,512]{2,1,0:T(8,128)S(1)}, bf16[288,512]{1,0:T(8,128)(2,1)S(1)}, bf16[288,512]{1,0:T(8...) custom-call(f32[8,128,512]{2,1,0:T(8,128)S(1)} %get-tuple-element.98.r_0_.r_2_, ...), custom_call_target="tpu_custom_call" | custom-call | flops 1000000000 | bytes 8388608 | tf_op jit(solution)/shard_map/pallas_call | solution.py:565
  22.6 4.0 %collective-permute-start.8 = (bf16[288,512]{1,0:T(8,128)(2,1)S(1)}, bf16[288,512]{1,0:T(8,128)(2,1)S(1)}, u32[]{:S(2)}, u32[]{:S(2)}) collective-permute-start(bf16[288,512]{1,0:T(8,128)(2,1)S(1)} %get-tuple-element.116), channel_id=1, source_target_pairs={{0,112},{16,0},{32,16},{48,32},{64,48},{80,64},{96,80},{112,96},{1... | collective-permute-start | bytes 884744 | tf_op jit(solution)/shard_map/ppermute | solution.py:22
  26.6 5.6 %shard_map.69 = (f32[8,128,512]{2,1,0:T(8,128)S(1)}, f32[8,128,512]{2,1,0:T(8,128)S(1)}, f32[8,2048]{1,0:T(8,128)S(1)}, f32[8,1024]{1,0:T(8,128)S(1)}) custom-call(f32[4,128,512]{2,1,0:T(8,128)S(1)} %get-tuple-element.107.r_0_, f32[8,2048]{1,0:T(8,128)S(1)} %get-tuple-element.108.r_1_, f32[8,128,512]{2,1,0:T(8,128)S(1)} %get-tuple-element.98.r_0_.r_2_, ...), custom_call_target="tpu_custom_call" | custom-call | flops 1000000000 | bytes 8388608 | tf_op jit(solution)/shard_map/pallas_call | solution.py:554
  32.2 2.1 %shard_map.70 = (f32[4,128,512]{2,1,0:T(8,128)S(1)}, bf16[288,512]{1,0:T(8,128)(2,1)S(1)}, bf16[288,512]{1,0:T(8,128)(2,1)S(1)}, f32[8,2048]{1,0:T(8,128)S(1)}, f32[8,2048]{1,0:T(8,128)S(1)}) custom-call(f32[8,128,512]{2,1,0:T(8,128)S(1)} %get-tuple-element.113.r_0_.r_2_, f32[8,2048]{1,0:T(8,128)S(1)} %get-tuple-element.114.r_1_, ...), custom_call_target="tpu_custom_call" | custom-call | flops 1000000000 | bytes 8388608 | tf_op jit(solution)/shard_map/pallas_call | solution.py:565
  34.4 1.6 %collective-permute-start.9 = (bf16[288,512]{1,0:T(8,128)(2,1)S(1)}, bf16[288,512]{1,0:T(8,128)(2,1)S(1)}, u32[]{:S(2)}, u32[]{:S(2)}) collective-permute-start(bf16[288,512]{1,0:T(8,128)(2,1)S(1)} %get-tuple-element.125), channel_id=1, source_target_pairs={{0,16},{16,32},{32,48},{48,64},{64,80},{80,96},{96,112},{112,0},{1... | collective-permute-start | bytes 884744 | tf_op jit(solution)/shard_map/ppermute | solution.py:22
  35.9 2.8 %collective-permute-start.10 = (bf16[288,512]{1,0:T(8,128)(2,1)S(1)}, bf16[288,512]{1,0:T(8,128)(2,1)S(1)}, u32[]{:S(2)}, u32[]{:S(2)}) collective-permute-start(bf16[288,512]{1,0:T(8,128)(2,1)S(1)} %get-tuple-element.126), channel_id=1, source_target_pairs={{0,112},{16,0},{32,16},{48,32},{64,48},{80,64},{96,80},{112,96},{1... | collective-permute-start | bytes 884744 | tf_op jit(solution)/shard_map/ppermute | solution.py:22
  38.8 5.7 %shard_map.71 = (f32[8,128,512]{2,1,0:T(8,128)S(1)}, f32[8,128,512]{2,1,0:T(8,128)S(1)}, f32[8,2048]{1,0:T(8,128)S(1)}, f32[8,1024]{1,0:T(8,128)S(1)}) custom-call(f32[4,128,512]{2,1,0:T(8,128)S(1)} %get-tuple-element.119.r_0_, f32[8,2048]{1,0:T(8,128)S(1)} %get-tuple-element.120.r_1_, f32[8,128,512]{2,1,0:T(8,128)S(1)} %get-tuple-element.113.r_0_.r_2_, ...), custom_call_target="tpu_custom_call" | custom-call | flops 1000000000 | bytes 8388608 | tf_op jit(solution)/shard_map/pallas_call | solution.py:554
  44.5 2.6 %collective-permute-done.10.r_3_ = bf16[288,512]{1,0:T(8,128)(2,1)S(1)} collective-permute-done((bf16[288,512]{1,0:T(8,128)(2,1)S(1)}, bf16[288,512]{1,0:T(8,128)(2,1)S(1)}, u32[]{:S(2)}, u32[]{:S(2)}) %collective-permute-start.10) | collective-permute-done | bytes 294944 | tf_op jit(solution)/shard_map/ppermute | solution.py:22
  47.1 2.1 %shard_map.72 = (f32[4,128,512]{2,1,0:T(8,128)S(1)}, bf16[288,512]{1,0:T(8,128)(2,1)S(1)}, bf16[288,512]{1,0:T(8,128)(2,1)S(1)}, f32[8,2048]{1,0:T(8,128)S(1)}, f32[8,2048]{1,0:T(8,128)S(1)}) custom-call(f32[8,128,512]{2,1,0:T(8,128)S(1)} %get-tuple-element.123.r_0_.r_2_, f32[8,2048]{1,0:T(8,128)S(1)} %get-tuple-element.124.r_1_, ...), custom_call_target="tpu_custom_call" | custom-call | flops 1000000000 | bytes 8388608 | tf_op jit(solution)/shard_map/pallas_call | solution.py:565
  49.6 3.8 %collective-permute-start.12 = (bf16[288,512]{1,0:T(8,128)(2,1)S(1)}, bf16[288,512]{1,0:T(8,128)(2,1)S(1)}, u32[]{:S(2)}, u32[]{:S(2)}) collective-permute-start(bf16[288,512]{1,0:T(8,128)(2,1)S(1)} %get-tuple-element.135), channel_id=1, source_target_pairs={{0,112},{16,0},{32,16},{48,32},{64,48},{80,64},{96,80},{112,96},{1... | collective-permute-start | bytes 884744 | tf_op jit(solution)/shard_map/ppermute | solution.py:22
  53.4 6.4 %shard_map.73 = (f32[8,128,512]{2,1,0:T(8,128)}, f32[8,128,512]{2,1,0:T(8,128)S(1)}, f32[8,2048]{1,0:T(8,128)S(1)}, f32[8,1024]{1,0:T(8,128)S(1)}) custom-call(f32[4,128,512]{2,1,0:T(8,128)S(1)} %get-tuple-element.128.r_0_, f32[8,2048]{1,0:T(8,128)S(1)} %get-tuple-element.129.r_1_, f32[8,128,512]{2,1,0:T(8,128)S(1)} %get-tuple-element.123.r_0_.r_2_, ...), custom_call_target="tpu_custom_call" | custom-call | flops 1000000000 | bytes 8388608 | tf_op jit(solution)/shard_map/pallas_call | solution.py:554
  59.8 3.4 %collective-permute-done.12.r_3_ = bf16[288,512]{1,0:T(8,128)(2,1)S(1)} collective-permute-done((bf16[288,512]{1,0:T(8,128)(2,1)S(1)}, bf16[288,512]{1,0:T(8,128)(2,1)S(1)}, u32[]{:S(2)}, u32[]{:S(2)}) %collective-permute-start.12) | collective-permute-done | bytes 294944 | tf_op jit(solution)/shard_map/ppermute | solution.py:22
  63.2 2.1 %shard_map.74 = bf16[16,64,512]{2,1,0:T(8,128)(2,1)S(1)} custom-call(f32[8,128,512]{2,1,0:T(8,128)S(1)} %get-tuple-element.132.r_0_, f32[8,2048]{1,0:T(8,128)S(1)} %get-tuple-element.133.r_1_, bf16[288,512]{1,0:T(8,128)(2,1)S(1)} %collective-permute-done.11.r_2_, bf16[288,512]{1,0:T(8,128)(2,1)S(1)} %collective-permute-done.12.r_3_, ...), custom_call_target="tpu_custom_call" | custom-call | flops 1000000000 | bytes 8388608 | tf_op jit(solution)/shard_map/pallas_call | solution.py:565
  65.4 29.2 %all_to_all.20.r_0_ = bf16[16,64,512]{2,1,0:T(8,128)(2,1)S(1)} all-to-all(bf16[16,64,512]{2,1,0:T(8,128)(2,1)S(1)} %shard_map.74), channel_id=1, replica_groups=mesh['ring'=8,'core'=2,'st'=8] {'st','core'}, dimensions={0} | all-to-all | bytes 2097152 | tf_op jit(solution)/shard_map/all_to_all | solution.py:577
  95.1 13.1 %all_to_all.21 = f32[128,1,128]{2,1,0:T(1,128)S(1)} all-to-all(f32[128,1,128]{2,1,0:T(1,128)S(1)} %bitcast.20), channel_id=1, replica_groups=mesh['ring'=8,'core'=2,'st'=8] {'ring','core','st'}, dimensions={0} | all-to-all | bytes 131072 | tf_op jit(solution)/shard_map/all_to_all | solution.py:588
  108.4 13.9 %all_to_all.22 = f32[128,1,128]{2,1,0:T(1,128)S(1)} all-to-all(f32[128,1,128]{2,1,0:T(1,128)S(1)} %broadcast_in_dim.2), channel_id=1, replica_groups=mesh['ring'=8,'core'=2,'st'=8] {'ring','core','st'}, dimensions={0} | all-to-all | bytes 131072 | tf_op jit(solution)/shard_map/all_to_all | solution.py:590
  122.3 5.7 %shard_map.76 = bf16[8,32,16,128]{3,2,1,0:T(8,128)(2,1)S(1)} custom-call(f32[128,128]{1,0:T(8,128)S(1)} %bitcast.19, bf16[8,128,512]{2,1,0:T(8,128)(2,1)S(1)} %get-tuple-element.138.ordered), custom_call_target="tpu_custom_call" | custom-call | flops 200000000 | bytes 2097152 | tf_op jit(solution)/shard_map/pallas_call | solution.py:591
  128.0 20.7 %all_to_all.23 = bf16[8,32,16,128]{3,2,1,0:T(8,128)(2,1)S(1)} all-to-all(bf16[8,32,16,128]{3,2,1,0:T(8,128)(2,1)S(1)} %shard_map.76), channel_id=1, replica_groups=mesh['ring'=8,'core'=2,'st'=8] {'st'}, dimensions={0} | all-to-all | bytes 2097152 | tf_op jit(solution)/shard_map/all_to_all | solution.py:597
  148.6 1.2 copy.14
  (35 shorter events, 4.3 us)
Async XLA Ops:
  0.0 2.0 %copy-start.4 = (bf16[16,4,64,128]{3,2,1,0:T(8,128)(2,1)S(1)}, bf16[16,4,64,128]{3,2,1,0:T(8,128)(2,1)}, u32[]{:S(2)}) copy-start(bf16[16,4,64,128]{3,2,1,0:T(8,128)(2,1)} %param.6) | copy-start | bytes 3145732
  1.8 1.6 %copy-start = (f32[4,64,128]{2,1,0:T(8,128)S(1)}, f32[4,64,128]{2,1,0:T(8,128)}, u32[]{:S(2)}) copy-start(f32[4,64,128]{2,1,0:T(8,128)} %r_2_.3) | copy-start | bytes 393220
  1.9 1.7 %copy-start.2 = (s32[4,16,16]{2,1,0:T(8,128)S(1)}, s32[4,16,16]{2,1,0:T(8,128)}, u32[]{:S(2)}) copy-start(s32[4,16,16]{2,1,0:T(8,128)} %r_3_.1) | copy-start | bytes 12292
  1.9 2.1 %copy-start.3 = (s32[4,16]{1,0:T(4,128)S(1)}, s32[4,16]{1,0:T(4,128)}, u32[]{:S(2)}) copy-start(s32[4,16]{1,0:T(4,128)} %r_4_.1) | copy-start | bytes 772
  1.9 3.7 %collective-permute-start.2 = (bf16[4,256,512]{2,1,0:T(8,128)(2,1)S(1)}, bf16[4,256,512]{2,1,0:T(8,128)(2,1)S(1)}, u32[]{:S(2)}, u32[]{:S(2)}) collective-permute-start(bf16[4,256,512]{2,1,0:T(8,128)(2,1)S(1)} %bitcast.14), channel_id=1, source_target_pairs={{0,8},{8,0},{1,9},{9,1},{2,10},{10,2},{3,11},{11,3},{4,12},{12,4},... | collective-permute-start | bytes 3145736 | tf_op jit(solution)/shard_map/ppermute | solution.py:507
  2.9 3.7 %copy-start.1 = (f32[12288]{0:T(1024)S(1)}, f32[12288]{0:T(1024)}, u32[]{:S(2)}) copy-start(f32[12288]{0:T(1024)} %param.11) | copy-start | bytes 147460
  2.9 2.7 %collective-permute-start = (bf16[4,128,512]{2,1,0:T(8,128)(2,1)S(1)}, bf16[4,128,512]{2,1,0:T(8,128)(2,1)S(1)}, u32[]{:S(2)}, u32[]{:S(2)}) collective-permute-start(bf16[4,128,512]{2,1,0:T(8,128)(2,1)S(1)} %get-tuple-element.73), channel_id=1, source_target_pairs={{0,8},{8,0},{1,9},{9,1},{2,10},{10,2},{3,11},{11,3},{4,12},{12,4},... | collective-permute-start | bytes 1572872 | tf_op jit(solution)/shard_map/ppermute | solution.py:507
  3.5 3.1 %collective-permute-start.1 = (f32[4,64,128]{2,1,0:T(8,128)S(1)}, f32[4,64,128]{2,1,0:T(8,128)S(1)}, u32[]{:S(2)}, u32[]{:S(2)}) collective-permute-start(f32[4,64,128]{2,1,0:T(8,128)S(1)} %copy-done), channel_id=1, source_target_pairs={{0,8},{8,0},{1,9},{9,1},{2,10},{10,2},{3,11},{11,3},{4,12},{12,4},... | collective-permute-start | bytes 393224 | tf_op jit(solution)/shard_map/ppermute | solution.py:507
  3.6 2.0 %collective-permute-start.3 = (s32[4,16,16]{2,1,0:T(8,128)S(1)}, s32[4,16,16]{2,1,0:T(8,128)S(1)}, u32[]{:S(2)}, u32[]{:S(2)}) collective-permute-start(s32[4,16,16]{2,1,0:T(8,128)S(1)} %copy-done.2), channel_id=1, source_target_pairs={{0,8},{8,0},{1,9},{9,1},{2,10},{10,2},{3,11},{11,3},{4,12},{12,4},... | collective-permute-start | bytes 12296 | tf_op jit(solution)/shard_map/ppermute | solution.py:507
  4.0 1.6 %collective-permute-start.4 = (s32[4,16]{1,0:T(4,128)S(1)}, s32[4,16]{1,0:T(4,128)S(1)}, u32[]{:S(2)}, u32[]{:S(2)}) collective-permute-start(s32[4,16]{1,0:T(4,128)S(1)} %copy-done.3), channel_id=1, source_target_pairs={{0,8},{8,0},{1,9},{9,1},{2,10},{10,2},{3,11},{11,3},{4,12},{12,4},... | collective-permute-start | bytes 776 | tf_op jit(solution)/shard_map/ppermute | solution.py:507
  6.6 12.8 %collective-permute-start.5 = (bf16[304,512]{1,0:T(8,128)(2,1)S(1)}, bf16[304,512]{1,0:T(8,128)(2,1)S(1)}, u32[]{:S(2)}, u32[]{:S(2)}) collective-permute-start(bf16[304,512]{1,0:T(8,128)(2,1)S(1)} %get-tuple-element.100), channel_id=1, source_target_pairs={{0,16},{16,32},{32,48},{48,64},{64,80},{80,96},{96,112},{112,0},{1... | collective-permute-start | bytes 933896 | tf_op jit(solution)/shard_map/ppermute | solution.py:22
  8.2 11.1 %collective-permute-start.6 = (bf16[304,512]{1,0:T(8,128)(2,1)S(1)}, bf16[304,512]{1,0:T(8,128)(2,1)S(1)}, u32[]{:S(2)}, u32[]{:S(2)}) collective-permute-start(bf16[304,512]{1,0:T(8,128)(2,1)S(1)} %get-tuple-element.101), channel_id=1, source_target_pairs={{0,112},{16,0},{32,16},{48,32},{64,48},{80,64},{96,80},{112,96},{1... | collective-permute-start | bytes 933896 | tf_op jit(solution)/shard_map/ppermute | solution.py:22
  22.4 9.8 %collective-permute-start.7 = (bf16[288,512]{1,0:T(8,128)(2,1)S(1)}, bf16[288,512]{1,0:T(8,128)(2,1)S(1)}, u32[]{:S(2)}, u32[]{:S(2)}) collective-permute-start(bf16[288,512]{1,0:T(8,128)(2,1)S(1)} %get-tuple-element.115), channel_id=1, source_target_pairs={{0,16},{16,32},{32,48},{48,64},{64,80},{80,96},{96,112},{112,0},{1... | collective-permute-start | bytes 884744 | tf_op jit(solution)/shard_map/ppermute | solution.py:22
  22.6 9.7 %collective-permute-start.8 = (bf16[288,512]{1,0:T(8,128)(2,1)S(1)}, bf16[288,512]{1,0:T(8,128)(2,1)S(1)}, u32[]{:S(2)}, u32[]{:S(2)}) collective-permute-start(bf16[288,512]{1,0:T(8,128)(2,1)S(1)} %get-tuple-element.116), channel_id=1, source_target_pairs={{0,112},{16,0},{32,16},{48,32},{64,48},{80,64},{96,80},{112,96},{1... | collective-permute-start | bytes 884744 | tf_op jit(solution)/shard_map/ppermute | solution.py:22
  34.4 10.1 %collective-permute-start.9 = (bf16[288,512]{1,0:T(8,128)(2,1)S(1)}, bf16[288,512]{1,0:T(8,128)(2,1)S(1)}, u32[]{:S(2)}, u32[]{:S(2)}) collective-permute-start(bf16[288,512]{1,0:T(8,128)(2,1)S(1)} %get-tuple-element.125), channel_id=1, source_target_pairs={{0,16},{16,32},{32,48},{48,64},{64,80},{80,96},{96,112},{112,0},{1... | collective-permute-start | bytes 884744 | tf_op jit(solution)/shard_map/ppermute | solution.py:22
  35.9 11.2 %collective-permute-start.10 = (bf16[288,512]{1,0:T(8,128)(2,1)S(1)}, bf16[288,512]{1,0:T(8,128)(2,1)S(1)}, u32[]{:S(2)}, u32[]{:S(2)}) collective-permute-start(bf16[288,512]{1,0:T(8,128)(2,1)S(1)} %get-tuple-element.126), channel_id=1, source_target_pairs={{0,112},{16,0},{32,16},{48,32},{64,48},{80,64},{96,80},{112,96},{1... | collective-permute-start | bytes 884744 | tf_op jit(solution)/shard_map/ppermute | solution.py:22
  49.2 10.6 %collective-permute-start.11 = (bf16[288,512]{1,0:T(8,128)(2,1)S(1)}, bf16[288,512]{1,0:T(8,128)(2,1)S(1)}, u32[]{:S(2)}, u32[]{:S(2)}) collective-permute-start(bf16[288,512]{1,0:T(8,128)(2,1)S(1)} %get-tuple-element.134), channel_id=1, source_target_pairs={{0,16},{16,32},{32,48},{48,64},{64,80},{80,96},{96,112},{112,0},{1... | collective-permute-start | bytes 884744 | tf_op jit(solution)/shard_map/ppermute | solution.py:22
  49.6 13.7 %collective-permute-start.12 = (bf16[288,512]{1,0:T(8,128)(2,1)S(1)}, bf16[288,512]{1,0:T(8,128)(2,1)S(1)}, u32[]{:S(2)}, u32[]{:S(2)}) collective-permute-start(bf16[288,512]{1,0:T(8,128)(2,1)S(1)} %get-tuple-element.135), channel_id=1, source_target_pairs={{0,112},{16,0},{32,16},{48,32},{64,48},{80,64},{96,80},{112,96},{1... | collective-permute-start | bytes 884744 | tf_op jit(solution)/shard_map/ppermute | solution.py:22
